TPU v7x, 256 devices: a whole 4x4x8 slice. The times are simulated.
256 devices in a mesh: tile: 32 (over z, x), round: 8 (over y, core).
Axes of the slice: x: 4, y: 4, z: 8, core: 2. Of those that a mesh axis runs over, the one named last changes fastest.
Arguments:
- images: bfloat16 [48, 2, 256, 8192], P('round', None, 'tile'), may hold values from 0.5 to 8
- labels: int32 [2, 256, 8192], P(None, 'round', 'tile'), may hold values from 0 to 256
- counts: int32 [32], replicated, may hold values from 64 to 256, as said below
- owners: int32 [8192, 1], P('tile'), may hold values from 0 to 31; in each aligned block of 256 rows (0 to 255, 256 to 511, ...) at most 16 rows name the same one
- codebook: bfloat16 [48, 550], replicated
Outputs:
- cell_genes: float32 [32, 32, 16, 550], P('tile')
Inputs may be any that keep to these rules, and one draw needn't show every extreme that they name: `counts`: some tile has 256 live slots, and at least a quarter of them in every tile. `owners`: at most 16 slots of one tile have the same owner, and this is reached.
All inputs are finite; a program needn't handle non-finite values.
Results may differ from a plain program's by a relative error of at most 0.0027.
The roundings to bfloat16 on the way count: a program that leaves them out, or rounds other values in their place, can miss the bound.
Values may be sent and summed in bfloat16 or wider, within the bound.
No kernel may reach another device: no remote copies, remote signals or barrier semaphores. Data moves between devices by JAX's collectives and lax.ppermute only.
A program may use at most 128 MiB of HBM per device.

v0:
```python
import math

import jax
import jax.numpy as jnp
from jax import lax
from jax.sharding import PartitionSpec as P

SOFTMAX_HEAT = 0.6
SHARPEN = 0.15
NOISE_LEVEL = 1.0


def with_halo(cells, sides, width):
    for axis, dim in sides:
        count = lax.axis_size(axis)
        ends = count - 1
        head = lax.slice_in_dim(cells, 0, width, axis=dim)
        tail = lax.slice_in_dim(cells, cells.shape[dim] - width, cells.shape[dim], axis=dim)
        cells = jnp.concatenate(
            [
                lax.ppermute(tail, axis, [(i, (i + 1) % count) for i in range(ends)]),
                cells,
                lax.ppermute(head, axis, [((i + 1) % count, i) for i in range(ends)]),
            ],
            axis=dim,
        )
    return cells


def stencil(padded_stack):
    zpadded = jnp.pad(padded_stack, ((0, 0), (1, 1), (0, 0), (0, 0)))
    center = padded_stack[:, :, 1:-1, 1:-1]
    beside = padded_stack[:, :, 2:, 1:-1] + padded_stack[:, :, :-2, 1:-1]
    beside = beside + padded_stack[:, :, 1:-1, 2:] + padded_stack[:, :, 1:-1, :-2]
    beside = beside + zpadded[:, 2:, 1:-1, 1:-1] + zpadded[:, :-2, 1:-1, 1:-1]
    return (center, beside)


def posterior_sums(unit_flat, label_flat, live, codebook, cells):
    voxels = unit_flat.shape[1]
    block = math.gcd(voxels, 2048)
    slots = jnp.arange(cells, dtype=jnp.int32)

    def step(total, block_index):
        start = block_index * block
        unit_block = lax.dynamic_slice_in_dim(unit_flat, start, block, 1)
        label_block = lax.dynamic_slice_in_dim(label_flat, start, block, 0)
        gene_logits = SOFTMAX_HEAT * lax.dot_general(
            unit_block, codebook, (((0,), (0,)), ((), ())), preferred_element_type=jnp.float32
        )
        posterior = jax.nn.softmax(gene_logits, axis=1).astype(jnp.bfloat16)
        label_block = jnp.where(label_block < live, label_block, -1)
        onehot = (slots[:, None] == label_block[None, :]).astype(jnp.bfloat16)
        return (total + jnp.dot(onehot, posterior, preferred_element_type=jnp.float32), None)

    start_total = jnp.zeros((cells, codebook.shape[1]), jnp.float32)
    total, _ = lax.scan(step, start_total, jnp.arange(voxels // block, dtype=jnp.int32))
    return total


def local(images, labels, counts, owners, codebook):
    gathered = lax.all_to_all(
        lax.all_to_all(images, "tile", split_axis=3, concat_axis=2, tiled=True),
        "round",
        split_axis=2,
        concat_axis=0,
        tiled=True,
    )
    tiles = lax.axis_size("tile")
    raw_padded = with_halo(gathered, (("tile", 3), ("round", 2)), 1)
    center, beside = stencil(raw_padded.astype(jnp.float32))
    highpass = center - (center + beside) / 7.0
    high_padded = with_halo(highpass, (("tile", 3), ("round", 2)), 1)
    center, beside = stencil(high_padded)
    sharp = center + SHARPEN * (6.0 * center - beside)
    mean_square = jnp.mean(sharp * sharp, axis=0)
    unit = (sharp / jnp.sqrt(mean_square + NOISE_LEVEL)).astype(jnp.bfloat16)
    channels = unit.shape[0]
    unit_flat = unit.reshape(channels, -1)
    label_flat = labels.reshape(-1)
    local_tile = lax.axis_index("tile")
    live = jnp.sum(jnp.where(jnp.arange(tiles) == local_tile, counts, 0))
    cells = owners.shape[0]
    capacity = max(2, 2 * cells // tiles)
    partial_value = posterior_sums(unit_flat, label_flat, live, codebook, cells)
    owner_of = owners[:, 0]
    chosen = (owner_of[:, None] == jnp.arange(tiles)[None, :]).astype(jnp.int32)
    before = jnp.cumsum(chosen, axis=0) - chosen
    slot = jnp.sum(before * chosen, axis=1)
    target = jnp.arange(tiles, dtype=jnp.int32)[:, None, None]
    place = jnp.arange(capacity, dtype=jnp.int32)[None, :, None]
    selector = ((owner_of[None, None, :] == target) & (slot[None, None, :] == place)).astype(
        jnp.float32
    )
    selector = selector.reshape(tiles * capacity, cells)
    genes = codebook.shape[1]
    summed = lax.psum(partial_value, "round")
    packed = jnp.dot(
        selector, summed, precision=lax.Precision.HIGHEST, preferred_element_type=jnp.float32
    )
    received = lax.all_to_all(
        packed.reshape(tiles, capacity, genes), "tile", split_axis=0, concat_axis=0, tiled=True
    )
    return received[None]


def solution(mesh):
    in_specs = (P("round", None, "tile", None), P(None, "round", "tile"), P(), P("tile", None), P())
    out_specs = P("tile", None, None, None)
    return jax.shard_map(local, mesh=mesh, in_specs=in_specs, out_specs=out_specs, check_vma=False)
```

profile of v0, /device:TPU:1, one launch (start us, length us, event | category | flops | bytes accessed | tf_op | source)
XLA Modules:
  0.0 475.6 jit_solution(6741341460430317833)
XLA Ops:
  6.5 26.0 %copy.25 = bf16[6,2,8,8192]{2,0,1,3:T(8,128)(2,1)} copy(bf16[6,2,8,8192]{3,2,1,0:T(8,128)(2,1)} %param.7) | data formatting | bytes 3145728 | tf_op args[0]
  32.5 34.5 %reshape.92 = bf16[32,2,12288]{2,1,0:T(2,128)(2,1)S(1)} reshape(bf16[8192,2,6,8]{3,2,1,0:T(8,128)(2,1)} %bitcast.47) | data formatting | bytes 3145728
  67.0 50.2 %all_to_all.41 = bf16[32,2,12288]{2,1,0:T(2,128)(2,1)S(1)} all-to-all(bf16[32,2,12288]{2,1,0:T(2,128)(2,1)S(1)} %reshape.92), channel_id=1, replica_groups=mesh['tile'=32,'round'=8] {'tile'}, dimensions={0} | all-to-all | bytes 3145728 | tf_op jit(solution)/shard_map/all_to_all | solution.py:63
  117.2 32.0 %reshape.93 = bf16[8192,2,6,8]{3,2,1,0:T(8,128)(2,1)} reshape(bf16[32,2,12288]{2,1,0:T(2,128)(2,1)S(1)} %all_to_all.41) | data formatting | bytes 3145728
  149.2 34.0 %copy.26 = bf16[6,2,32,8,256]{4,1,0,3,2:T(2,128)(2,1)S(1)} copy(bf16[6,2,32,8,256]{3,0,1,4,2:T(8,128)(2,1)} %bitcast.46) | data formatting | bytes 3145728 | tf_op jit(solution)/shard_map/all_to_all | solution.py:63
  183.1 27.8 %all_to_all.42 = bf16[6,2,256,256]{3,1,0,2:T(2,128)(2,1)S(1)} all-to-all(bf16[6,2,256,256]{3,1,0,2:T(2,128)(2,1)S(1)} %bitcast.51), channel_id=1, replica_groups=mesh['tile'=32,'round'=8] {'round'}, dimensions={2} | all-to-all | bytes 3145728 | tf_op jit(solution)/shard_map/all_to_all | solution.py:62
  212.7 2.4 collective-permute-start
  222.8 4.5 collective-permute-start.2
  229.7 4.2 collective-permute-done.3
  233.9 4.1 maximum_convert_fusion
  238.0 4.7 fusion.15
  242.7 2.2 fusion.33
  244.9 2.2 copy.33
  247.2 3.1 collective-permute-start.4
  250.3 2.2 copy.34
  253.9 2.4 copy.35
  257.1 2.4 copy.36
  259.5 2.4 pad_maximum_fusion.8
  263.8 3.9 collective-permute-start.7
  269.6 5.9 %select_maximum_fusion = f32[48,4,34,258]{3,2,1,0:T(8,128)} fusion(f32[48,2,1,258]{3,2,1,0:T(1,128)S(1)} %collective-permute-done.6, f32[48,2,1,258]{3,2,1,0:T(1,128)S(1)} %collective-permute-done.7, f32[48,2,32,1]{3,2,1,0:T(8,128)S(1)} %copy-done.2, f32[48,2,32,256]{3,2,1,0:T(8,128)S(1)} %fusion.15, f32[48,2,32,1]{3,2,1,0:T(8,128)S(1)} %copy-done.1), kind=kLoop, calls=%fused_computation.18 | loop fusion | flops 20210688 | bytes 10105344 | tf_op jit(solution)/shard_map/concatenate | solution.py:19
  275.5 8.7 %multiply_reduce_fusion.1 = (f32[2,32,256]{2,1,0:T(8,128)S(1)}, f32[48,2,32,256]{3,2,1,0:T(8,128)S(1)}) fusion(f32[48,2,32,256]{3,2,1,0:T(8,128)S(1)} %fusion.15, f32[48,4,34,258]{3,2,1,0:T(8,128)} %select_maximum_fusion, f32[48,2,32,1]{3,2,1,0:T(8,128)S(1)} %copy-done.1, f32[48,2,32,1]{3,2,1,0:T(8,128)S(1)} %copy-done.2, ...), kind=kLoop, calls=%fused_computation.48 | loop fusion | flops 14925824 | bytes 12871168 | tf_op jit(solution)/shard_map/reduce_sum | solution.py:76
  285.7 73.1 %while.11 = (s32[]{:T(128)}, f32[256,550]{0,1:T(8,128)S(1)}, s32[8]{0:T(128)S(1)}, s32[16384]{0:T(1024)S(1)}, s32[]{:T(128)}, /*index=5*/bf16[48,16384]{1,0:T(8,...) while((s32[]{:T(128)}, f32[256,550]{0,1:T(8,128)S(1)}, ...), condition=%wide.region_8.9_spmd.clone, body=%wide.region_5.8_spmd.clone.sunk | while | flops 695794688 | bytes 32989400 | solution.py:57
  291.2 3.6 fusion.41
  300.3 3.6 fusion.41
  309.5 3.6 fusion.41
  318.6 3.6 fusion.41
  327.7 3.6 fusion.41
  336.9 3.6 fusion.41
  346.0 3.6 fusion.41
  355.2 3.6 fusion.41
  359.7 66.1 %all-reduce.4.cloned.1.call-done = f32[256,550]{0,1:T(8,128)} async-done(((f32[256,550]{0,1:T(8,128)}), f32[256,550]{0,1:T(8,128)}) %all-reduce.4.cloned.1.call-update) | async-done | bytes 563216 | tf_op jit(solution)/shard_map/psum | solution.py:97
  427.7 40.0 %all_to_all.43 = f32[32,16,550]{2,1,0:T(8,128)S(1)} all-to-all(f32[32,16,550]{2,1,0:T(8,128)S(1)} %fusion.22), channel_id=1, replica_groups=mesh['tile'=32,'round'=8] {'tile'}, dimensions={0} | all-to-all | bytes 2252800 | tf_op jit(solution)/shard_map/all_to_all | solution.py:101
  (105 shorter events, 61.5 us)
Async XLA Ops:
  6.5 419.2 %all-reduce.4.cloned.1.call-start = ((), (), s32[]{:S(2)}) async-start(), calls=%async_computation.3 | async-start | bytes 1130496 | tf_op jit(solution)/shard_map/psum | solution.py:97
  211.3 6.1 %copy-start.7 = (s32[256,1]{0,1:T(1,128)S(1)}, s32[256,1]{0,1:T(1,128)}, u32[]{:S(2)}) copy-start(s32[256,1]{0,1:T(1,128)} %param.10) | copy-start | bytes 3076
  212.7 5.3 %collective-permute-start = (bf16[48,2,32,1]{0,2,3,1:T(8,128)(2,1)S(1)}, bf16[48,2,32,1]{0,2,3,1:T(8,128)(2,1)S(1)}, u32[]{:S(2)}, u32[]{:S(2)}) collective-permute-start(bf16[48,2,32,1]{0,2,3,1:T(8,128)(2,1)S(1)} %copy.29), channel_id=1, source_target_pairs={{0,8},{8,16},{16,24},{24,32},{32,40},{40,48},{48,56},{56,64},{64,7... | collective-permute-start | bytes 18440 | tf_op jit(solution)/shard_map/ppermute | solution.py:21
  216.1 4.5 collective-permute-start.1
  222.8 6.9 %collective-permute-start.2 = (bf16[48,2,1,258]{3,2,1,0:T(2,128)(2,1)S(1)}, bf16[48,2,1,258]{3,2,1,0:T(2,128)(2,1)}, u32[]{:S(2)}, u32[]{:S(2)}) collective-permute-start(bf16[48,2,1,258]{3,2,1,0:T(2,128)(2,1)S(1)} %get-tuple-element.96), channel_id=1, source_target_pairs={{0,1},{1,2},{2,3},{3,4},{4,5},{5,6},{6,7},{8,9},{9,10},{10,11},{11... | collective-permute-start | bytes 148616 | tf_op jit(solution)/shard_map/ppermute | solution.py:21
  227.4 6.6 %collective-permute-start.3 = (bf16[48,2,1,258]{3,2,1,0:T(2,128)(2,1)S(1)}, bf16[48,2,1,258]{3,2,1,0:T(2,128)(2,1)}, u32[]{:S(2)}, u32[]{:S(2)}) collective-permute-start(bf16[48,2,1,258]{3,2,1,0:T(2,128)(2,1)S(1)} %get-tuple-element.97), channel_id=1, source_target_pairs={{1,0},{2,1},{3,2},{4,3},{5,4},{6,5},{7,6},{9,8},{10,9},{11,10},{12... | collective-permute-start | bytes 148616 | tf_op jit(solution)/shard_map/ppermute | solution.py:23
  229.7 8.3 %copy-start.8 = (s32[32,3]{0,1:T(4,128)}, s32[32,3]{0,1:T(4,128)S(1)}, u32[]{:S(2)}) copy-start(s32[32,3]{0,1:T(4,128)S(1)} %reduce-window.9) | copy-start | bytes 1156
  244.9 8.8 %slice-start = ((s32[32,3]{0,1:T(4,128)}), s32[32,2]{0,1:T(2,128)S(1)}, s32[]{:S(2)}) async-start(s32[32,3]{0,1:T(4,128)} %copy-done.8), calls=%async_computation.4 | async-start | bytes 2048 | tf_op jit(solution)/shard_map/slice.1
  244.9 8.9 %copy-start.6 = (s32[2,32,256]{2,1,0:T(8,128)S(1)}, s32[2,32,256]{2,1,0:T(8,128)}, u32[]{:S(2)}) copy-start(s32[2,32,256]{2,1,0:T(8,128)} %param.8) | copy-start | bytes 196612
  247.2 6.7 %collective-permute-start.4 = (f32[48,2,32,1]{0,2,3,1:T(8,128)S(1)}, f32[48,2,32,1]{0,2,3,1:T(8,128)S(1)}, u32[]{:S(2)}, u32[]{:S(2)}) collective-permute-start(f32[48,2,32,1]{0,2,3,1:T(8,128)S(1)} %copy.33), channel_id=1, source_target_pairs={{0,8},{8,16},{16,24},{24,32},{32,40},{40,48},{48,56},{56,64},{64,7... | collective-permute-start | bytes 36872 | tf_op jit(solution)/shard_map/ppermute | solution.py:21
  252.5 4.6 collective-permute-start.5
  259.5 8.2 %copy-start.9 = (s32[32]{0:T(128)S(1)}, s32[32]{0:T(128)}, u32[]{:S(2)}) copy-start(s32[32]{0:T(128)} %param.9) | copy-start | bytes 388
  259.5 10.1 %copy-start.1 = (f32[48,2,32,1]{3,2,1,0:T(8,128)S(1)}, f32[48,2,32,1]{3,2,1,0:T(8,128)}, u32[]{:S(2)}) copy-start(f32[48,2,32,1]{3,2,1,0:T(8,128)} %copy.35) | copy-start | bytes 36868
  259.5 10.1 %copy-start.2 = (f32[48,2,32,1]{3,2,1,0:T(8,128)S(1)}, f32[48,2,32,1]{3,2,1,0:T(8,128)}, u32[]{:S(2)}) copy-start(f32[48,2,32,1]{3,2,1,0:T(8,128)} %copy.36) | copy-start | bytes 36868
  261.9 6.5 %collective-permute-start.6 = (f32[48,2,1,258]{3,2,1,0:T(1,128)S(1)}, f32[48,2,1,258]{3,2,1,0:T(1,128)S(1)}, u32[]{:S(2)}, u32[]{:S(2)}) collective-permute-start(f32[48,2,1,258]{3,2,1,0:T(1,128)S(1)} %get-tuple-element.93), channel_id=1, source_target_pairs={{1,0},{2,1},{3,2},{4,3},{5,4},{6,5},{7,6},{9,8},{10,9},{11,10},{12... | collective-permute-start | bytes 297224 | tf_op jit(solution)/shard_map/ppermute | solution.py:23
  263.8 5.7 %collective-permute-start.7 = (f32[48,2,1,258]{3,2,1,0:T(1,128)S(1)}, f32[48,2,1,258]{3,2,1,0:T(1,128)S(1)}, u32[]{:S(2)}, u32[]{:S(2)}) collective-permute-start(f32[48,2,1,258]{3,2,1,0:T(1,128)S(1)} %get-tuple-element.92), channel_id=1, source_target_pairs={{0,1},{1,2},{2,3},{3,4},{4,5},{5,6},{6,7},{8,9},{9,10},{10,11},{11... | collective-permute-start | bytes 297224 | tf_op jit(solution)/shard_map/ppermute | solution.py:21
  284.2 1.4 copy-start.3
  284.2 1.4 copy-start.4
  287.7 2.0 copy-start
  296.9 2.0 copy-start
  306.0 2.0 copy-start
  315.2 2.0 copy-start
  324.3 2.0 copy-start
  333.4 2.0 copy-start
  342.6 2.0 copy-start
  351.7 2.0 copy-start
  358.8 0.8 copy-start.5
Sparse Core Ops, SparseCore 0:
  359.8 65.9 all-reduce.3
where the time goes:
time: 483 us; the launch traced here: 476 us
  local copies, waits for them, and re-layouts  167 us (35%)
  blocking collectives  118 us (24%)
  waiting for transfers between devices  73.5 us (15%)
  other arithmetic  39.7 us (8%)
  matrix products  37.3 us (8%)
  starting transfers between devices  20.5 us (4%)
  between operations  13.7 us (3%)
  loops' own time  5.67 us (1%)
    unnamed x24, local copies, waits for them, and re-layouts  95.3 us
    psum x1, waiting for transfers between devices, local(): summed = lax.psum(partial_value, 'round')  66.1 us
    all_to_all x1, blocking collectives, local(): lax.all_to_all(images, 'tile', split_axis=3, concat_axis=2, tiled=True)  50.2 us
    all_to_all x1, blocking collectives, local(): lax.all_to_all(packed.reshape(tiles, capacity, genes), 'tile', split_axis...  40 us
    all_to_all x1, local copies, waits for them, and re-layouts, local(): lax.all_to_all(images, 'tile', split_axis=3, concat_axis=2, tiled=True)  34 us
    dot_general x8, matrix products, step(): jnp.dot(onehot, posterior, preferred_element_type=jnp.float32)  29 us
    all_to_all x1, blocking collectives, local(): lax.all_to_all(lax.all_to_all(images, 'tile', split_axis=3, concat_axis=2...  27.8 us
    while x16, local copies, waits for them, and re-layouts  16.2 us
  transfers between devices with their start and end apart: 9, of which 5 were waited for; matrix products, arithmetic and copies ran while one was open for 2% of the time, Pallas kernels for 0%

commit v1 on v0

v1 whole, which is shorter than its diff:
```python
import jax
import jax.numpy as jnp
from jax import lax
from jax.experimental import pallas as pl
from jax.experimental.pallas import tpu as pltpu
from jax.sharding import Mesh, PartitionSpec as P

SOFTMAX_HEAT = 0.6
SHARPEN = 0.15
NOISE_LEVEL = 1.0
LOG2E = 1.4426950408889634

CH, GENES, ZP, PT, CELLS, TILES, CAP = 48, 550, 2, 256, 256, 32, 16
NZ, NXD, NR = 8, 4, 8
GP = 552
COLOUR = CH // NR
PAIRS = COLOUR * ZP
PIECE = 2 * PAIRS + 1
ROWS = 32
SCALE = 0.25
F32, BF16 = jnp.float32, jnp.bfloat16


def pack_kernel(img, before, after, out):
    r = pl.program_id(0)
    lane = lax.broadcasted_iota(jnp.int32, (8, 128), 1)
    has_before, has_after = (r > 0).astype(F32), (r < NR - 1).astype(F32)
    for x in range(NXD):
        border = jnp.zeros((8, 128), F32)
        for i in range(PAIRS):
            c, p = i // ZP, i % ZP
            out[x, 0, 2 * i] = img[c, p, :, 256 * x : 256 * x + 128]
            out[x, 0, 2 * i + 1] = img[c, p, :, 256 * x + 128 : 256 * x + 256]
            if x < NXD - 1:
                right = img[c, p, :, 256 * x + 256 : 256 * x + 384].astype(F32)
            else:
                right = after[c, p].astype(F32) * has_after
            if x > 0:
                left = img[c, p, :, 256 * x - 128 : 256 * x].astype(F32)
            else:
                left = before[c, p].astype(F32) * has_before
            both = jnp.where(lane < 64, right, left)
            if i > 0:
                both = pltpu.roll(both, 4 * i, 1)
            border = jnp.where(((lane - 4 * i + 2) & 127) < 4, both, border)
        out[x, 0, 2 * PAIRS] = border.astype(BF16)


def pack(images):
    return pl.pallas_call(
        pack_kernel,
        grid=(NR,),
        in_specs=[
            pl.BlockSpec((COLOUR, ZP, 8, 1024), lambda r: (0, 0, 0, r)),
            pl.BlockSpec((COLOUR, ZP, 8, 128), lambda r: (0, 0, 0, jnp.maximum(8 * r - 1, 0))),
            pl.BlockSpec((COLOUR, ZP, 8, 128), lambda r: (0, 0, 0, jnp.minimum(8 * r + 8, 63))),
        ],
        out_specs=pl.BlockSpec((NXD, 1, PIECE, 8, 128), lambda r: (0, r, 0, 0, 0)),
        out_shape=jax.ShapeDtypeStruct((NXD, NR, PIECE, 8, 128), BF16),
        name="pack_pieces",
    )(images, images, images)


def neighbours(tiles, lane):
    n = len(tiles)
    up = [pltpu.roll(t, 1, 1) for t in tiles]
    down = [pltpu.roll(t, 127, 1) for t in tiles]
    first, last = lane == 0, lane == 127
    left = [jnp.where(first, up[k - 1], up[k]) for k in range(n)]
    right = [jnp.where(last, down[(k + 1) % n], down[k]) for k in range(n)]
    return left, right


def decode_kernel(g, gu, gd, labels, owners, counts, codebook, out, s, hp, unit, cbt, acc):
    z, x, r = lax.axis_index("z"), lax.axis_index("x"), lax.axis_index("r")
    tile = NXD * r + x
    lane = lax.broadcasted_iota(jnp.int32, (CH, 128), 1)

    def unpack(src, at, rr):
        border = src[2 * PAIRS].astype(F32)
        for i in range(PAIRS):
            c, p = i // ZP, i % ZP
            rows = pl.ds(pl.multiple_of((COLOUR * rr + c) * 8, 8), 8)
            s[0, at * ZP + p, rows, :] = src[2 * i].astype(F32)
            s[1, at * ZP + p, rows, :] = src[2 * i + 1].astype(F32)
            s[2, at * ZP + p, rows, :] = pltpu.roll(border, 128 - 4 * i, 1) if i else border

    def unpack_step(k, _):
        unpack(g.at[k], k // NR + 1, k % NR)
        return 0

    lax.fori_loop(0, NXD * NR, unpack_step, 0)

    def unpack_border(k, _):
        unpack(gu.at[k], 0, k)
        unpack(gd.at[k], NXD + 1, k)
        return 0

    lax.fori_loop(0, NR, unpack_border, 0)

    def raw(row, p):
        at, inner = (row + 8) // 8, (row + 8) % 8
        return [s[k, at * ZP + p, pl.ds(inner, CH, stride=8), :] for k in range(3)]

    left_ok = jnp.where(tile > 0, 1.0, 0.0)
    right_ok = jnp.where(tile < TILES - 1, 1.0, 0.0)
    edge = jnp.where(lane < 64, right_ok, left_ok)

    def highpass(k, _):
        row = k - 1
        inside = jnp.where(((row >= 0) | (z > 0)) & ((row < ROWS) | (z < NZ - 1)), 1.0, 0.0)
        mid = [raw(row, p) for p in range(ZP)]
        for p in range(ZP):
            above, below = raw(row - 1, p), raw(row + 1, p)
            left, right = neighbours(mid[p], lane)
            for t in range(3):
                beside = (below[t] + above[t]) + (right[t] + left[t]) + mid[1 - p][t]
                high = mid[p][t] - (mid[p][t] + beside) * (1.0 / 7.0)
                high = high * (edge * inside if t == 2 else inside)
                hp[k, p, t] = high
        return 0

    lax.fori_loop(0, ROWS + 2, highpass, 0)

    def sharpen(k, _):
        mid = [[hp[k + 1, p, t] for t in range(3)] for p in range(ZP)]
        for p in range(ZP):
            left, right = neighbours(mid[p], lane)
            for t in range(2):
                beside = (hp[k + 2, p, t] + hp[k, p, t]) + (right[t] + left[t]) + mid[1 - p][t]
                sharp = mid[p][t] + SHARPEN * (6.0 * mid[p][t] - beside)
                mean = jnp.sum(sharp * sharp, axis=0, keepdims=True) * (1.0 / CH)
                scaled = sharp * lax.rsqrt(mean + NOISE_LEVEL)
                unit[k, :, p * 256 + t * 128 : p * 256 + (t + 1) * 128] = scaled.astype(BF16)
        return 0

    lax.fori_loop(0, ROWS, sharpen, 0)

    wide = codebook[...].astype(F32) * (SOFTMAX_HEAT * LOG2E)
    flat = jnp.concatenate([wide, jnp.zeros((CH, GP - GENES), F32)], axis=1).T
    hi = flat.astype(BF16)
    mid = (flat - hi.astype(F32)).astype(BF16)
    lo = (flat - hi.astype(F32) - mid.astype(F32)).astype(BF16)
    gene = lax.broadcasted_iota(jnp.int32, (GP, 16), 0)
    which = lax.broadcasted_iota(jnp.int32, (GP, 16), 1)
    shut = jnp.where((gene >= GENES) & (which == 0), -3.0e38, 0.0).astype(BF16)
    cbt[...] = jnp.concatenate([hi, mid, lo, shut], axis=1)
    acc[...] = jnp.zeros_like(acc)
    slots = lax.broadcasted_iota(jnp.int32, (CELLS, ZP * PT), 0)

    def posterior(k, _):
        u = unit[k]
        stacked = jnp.concatenate([u, u, u, jnp.ones((16, ZP * PT), BF16)], axis=0)
        logits = jnp.dot(cbt[...], stacked, preferred_element_type=F32)
        top = jnp.max(logits, axis=0, keepdims=True)
        e = jnp.exp2(logits - top)
        total = jnp.sum(e, axis=0, keepdims=True)
        post = (e * (1.0 / total)).astype(BF16)
        row = jnp.concatenate([labels[p, pl.ds(k, 1), :] for p in range(ZP)], axis=1)
        onehot = jnp.where(slots == row, 1.0, 0.0).astype(BF16)
        acc[...] += lax.dot_general(post, onehot, (((1,), (1,)), ((), ())), preferred_element_type=F32)
        return 0

    lax.fori_loop(0, ROWS, posterior, 0)

    owner = owners[...]
    own = lax.broadcasted_iota(jnp.int32, (TILES, CELLS), 0) == owner
    own_f = jnp.where(own, 1.0, 0.0)
    earlier = lax.broadcasted_iota(jnp.int32, (CELLS, CELLS), 0) < lax.broadcasted_iota(jnp.int32, (CELLS, CELLS), 1)
    before = jnp.dot(own_f.astype(BF16), jnp.where(earlier, 1.0, 0.0).astype(BF16), preferred_element_type=F32)
    place = jnp.sum(own_f * before, axis=0, keepdims=True).astype(jnp.int32)
    cell = lax.broadcasted_iota(jnp.int32, (1, CELLS), 1)
    goes = jnp.where(cell < counts[tile], owner * CAP + place, -1)
    select = jnp.where(lax.broadcasted_iota(jnp.int32, (TILES * CAP, CELLS), 0) == goes, SCALE, 0.0).astype(BF16)
    sums = acc[...]
    high = sums.astype(BF16)
    low = (sums - high.astype(F32)).astype(BF16)
    nt = (((1,), (1,)), ((), ()))
    packed = lax.dot_general(select, high, nt, preferred_element_type=F32)
    packed = packed + lax.dot_general(select, low, nt, preferred_element_type=F32)
    out[...] = packed[:, :GENES]


def decode(g, gu, gd, labels, owners, counts, codebook):
    vmem, smem = pl.BlockSpec(memory_space=pltpu.VMEM), pl.BlockSpec(memory_space=pltpu.SMEM)
    return pl.pallas_call(
        decode_kernel,
        in_specs=[vmem, vmem, vmem, vmem, vmem, smem, vmem],
        out_specs=vmem,
        out_shape=jax.ShapeDtypeStruct((TILES * CAP, GENES), F32),
        scratch_shapes=[
            pltpu.VMEM((3, (NXD + 2) * ZP, CH * 8, 128), F32),
            pltpu.VMEM((ROWS + 2, ZP, 3, CH, 128), F32),
            pltpu.VMEM((ROWS, CH, ZP * PT), BF16),
            pltpu.VMEM((GP, 3 * CH + 16), BF16),
            pltpu.VMEM((GP, CELLS), F32),
        ],
        compiler_params=pltpu.CompilerParams(vmem_limit_bytes=48 * 1024 * 1024),
        name="decode_band",
    )(g, gu, gd, labels, owners, counts, codebook)


def local(images, labels, counts, owners, codebook):
    swap = [
        (z * NXD * NR + x * NR + r, r * NXD * NR + x * NR + z)
        for z in range(NZ)
        for x in range(NXD)
        for r in range(NR)
    ]
    everywhere = ("z", "x", "r")
    labels = lax.ppermute(labels, everywhere, swap)
    owners = lax.ppermute(owners.reshape(1, CELLS), everywhere, swap)
    pieces = pack(images).reshape(NXD * NR, PIECE, 8, 128)
    g = lax.all_to_all(pieces, ("x", "r"), split_axis=0, concat_axis=0, tiled=True)
    gu = lax.ppermute(g[(NXD - 1) * NR :], "z", [(i, i + 1) for i in range(NZ - 1)])
    gd = lax.ppermute(g[:NR], "z", [(i + 1, i) for i in range(NZ - 1)])
    packed = decode(g, gu, gd, labels, owners, counts, codebook)
    packed = packed.astype(jnp.float16).reshape(NZ, NXD * CAP, GENES)
    parts = lax.all_to_all(packed, "z", split_axis=0, concat_axis=0, tiled=True)
    summed = jnp.sum(parts.astype(F32), axis=0).astype(jnp.float16).reshape(NXD, 1, CAP, GENES)
    spread = jnp.broadcast_to(summed, (NXD, NR, CAP, GENES)).reshape(NXD * NR, CAP, GENES)
    received = lax.all_to_all(spread, ("x", "r"), split_axis=0, concat_axis=0, tiled=True)
    received = received.reshape(NXD, NR, CAP, GENES).transpose(1, 0, 2, 3).reshape(1, TILES, CAP, GENES)
    return received.astype(F32) * (1.0 / SCALE)


def solution(mesh):
    grid = Mesh(mesh.devices.reshape(NZ, NXD, NR), ("z", "x", "r"))
    in_specs = (P("r", None, ("z", "x"), None), P(None, "r", ("z", "x")), P(), P(("z", "x"), None), P())
    out_specs = P(("z", "x"), None, None, None)
    return jax.shard_map(local, mesh=grid, in_specs=in_specs, out_specs=out_specs, check_vma=False)
```

time: 483 us -> 149 us (0.31); the launches traced: 476 us -> 148 us
  local copies, waits for them, and re-layouts: 167 us -> 1.31 us
  waiting for transfers between devices: 73.5 us -> 5.08 us
  Pallas kernels: 0 us -> 48.1 us
  other arithmetic: 39.7 us -> 0.3 us
  matrix products: 37.3 us -> 0 us
  blocking collectives: 118 us -> 82.1 us
  between operations: 13.7 us -> 0.12 us
  starting transfers between devices: 20.5 us -> 11.2 us
  loops' own time: 5.67 us -> 0 us
    unnamed x24 -> x8, local copies, waits for them, and re-layouts: 95.3 us -> 0.01 us
    psum x1 -> x0, waiting for transfers between devices: 66.1 us -> none  [local(): summed = lax.psum(partial_value, 'round')]
    pallas_call x0 -> x2, Pallas kernels: none -> 48.1 us  [the longest x1 42.2 us: decode(): pl.pallas_call(decode_kernel, in_specs=[vmem, vmem, vmem, vmem, vmem, sme...]
    dot_general x17 -> x0, matrix products: 37.3 us -> none  [the longest x8 29 us: step(): jnp.dot(onehot, posterior, preferred_element_type=jnp.float32)]
    all_to_all x3, blocking collectives: 118 us -> 82.1 us  [the longest x1 32.1 us: local(): lax.all_to_all(pieces, ('x', 'r'), split_axis=0, concat_axis=0, tiled=True)]
    all_to_all x3 -> x0, local copies, waits for them, and re-layouts: 34.3 us -> none  [the longest x1 34 us: local(): lax.all_to_all(images, 'tile', split_axis=3, concat_axis=2, tiled=True)]
    while x16 -> x0, local copies, waits for them, and re-layouts: 16.2 us -> none
    reduce_sum x11 -> x1, other arithmetic: 15.7 us -> 0.09 us  [local(): jnp.sum(parts.astype(F32), axis=0).astype(jnp.float16)]
  transfers between devices with their start and end apart: 9 -> 4, of which waited for: 5 -> 1; matrix products, arithmetic and copies ran while one was open for 2% -> 0% of each run, Pallas kernels for 0% -> 0%
where the time goes in v1:
time: 149 us; the launch traced here: 148 us
  blocking collectives  82.1 us (55%)
  Pallas kernels  48.1 us (32%)
  starting transfers between devices  11.2 us (8%)
  waiting for transfers between devices  5.08 us (3%)
    pallas_call x1, Pallas kernels, decode(): pl.pallas_call(decode_kernel, in_specs=[vmem, vmem, vmem, vmem, vmem, sme...  42.2 us
    all_to_all x1, blocking collectives, local(): lax.all_to_all(pieces, ('x', 'r'), split_axis=0, concat_axis=0, tiled=True)  32.1 us
    all_to_all x1, blocking collectives, local(): parts = lax.all_to_all(packed, 'z', split_axis=0, concat_axis=0, tiled=True)  28.7 us
    all_to_all x1, blocking collectives, local(): lax.all_to_all(spread, ('x', 'r'), split_axis=0, concat_axis=0, tiled=True)  21.3 us
    pallas_call x1, Pallas kernels, pack(): pl.pallas_call(pack_kernel, grid=(NR,), in_specs=[pl.BlockSpec((COLOUR, Z...  5.92 us
    ppermute x1, waiting for transfers between devices, local(): owners = lax.ppermute(owners.reshape(1, CELLS), everywhere, swap)  5.08 us
    ppermute x1, starting transfers between devices, local(): lax.ppermute(g[(NXD - 1) * NR:], 'z', [(i, i + 1) for i in range(NZ - 1)])  4.2 us
    ppermute x1, starting transfers between devices, local(): labels = lax.ppermute(labels, everywhere, swap)  3.56 us
  transfers between devices with their start and end apart: 4, of which 1 were waited for; matrix products, arithmetic and copies ran while one was open for 0% of the time, Pallas kernels for 0%

profile of v1, /device:TPU:1, one launch (start us, length us, event | category | flops | bytes accessed | tf_op | source)
XLA Modules:
  0.0 148.2 jit_solution(763350739963306615)
XLA Ops:
  0.0 5.9 %pack_pieces.1 = bf16[4,8,25,8,128]{4,3,2,1,0:T(8,128)(2,1)} custom-call(bf16[6,2,8,8192]{3,2,1,0:T(8,128)(2,1)} %after.1, bf16[6,2,8,8192]{3,2,1,0:T(8,128)(2,1)} %after.1, bf16[6,2,8,8192]{3,2,1,0:T(8,128)(2,1)} %after.1), custom_call_target="tpu_custom_call" | custom-call | tf_op jit(solution)/shard_map/pack_pieces/pallas_call | solution.py:50
  5.9 32.1 %all_to_all.15.g = bf16[32,25,8,128]{3,2,1,0:T(8,128)(2,1)S(1)} all-to-all(bf16[32,25,8,128]{3,2,1,0:T(8,128)(2,1)} %bitcast.9), channel_id=1, replica_groups=mesh['z'=8,'x'=4,'r'=8] {'x','r'}, dimensions={0} | all-to-all | bytes 3276800 | tf_op jit(solution)/shard_map/all_to_all | solution.py:214
  38.0 0.0 copy-start.2
  38.0 0.0 copy-start.3
  38.0 0.0 copy-start
  38.0 0.0 copy-start.1
  38.0 0.1 fusion
  38.1 1.4 collective-permute-start.1
  39.5 4.2 %collective-permute-start = (bf16[8,25,8,128]{3,2,1,0:T(8,128)(2,1)S(1)}, bf16[8,25,8,128]{3,2,1,0:T(8,128)(2,1)S(1)}, u32[]{:S(2)}, u32[]{:S(2)}) collective-permute-start(bf16[8,25,8,128]{3,2,1,0:T(8,128)(2,1)S(1)} %get-tuple-element.6), channel_id=1, source_target_pairs={{0,32},{32,64},{64,96},{96,128},{128,160},{160,192},{192,224},{1,3... | collective-permute-start | bytes 1228808 | tf_op jit(solution)/shard_map/ppermute | solution.py:215
  43.7 0.0 copy-done.2
  43.7 3.6 %collective-permute-start.2 = (s32[2,32,256]{2,1,0:T(8,128)S(1)}, s32[2,32,256]{2,1,0:T(8,128)S(1)}, u32[]{:S(2)}, u32[]{:S(2)}) collective-permute-start(s32[2,32,256]{2,1,0:T(8,128)S(1)} %copy-done.2), channel_id=1, source_target_pairs={{0,0},{1,32},{2,64},{3,96},{4,128},{5,160},{6,192},{7,224},{8,8},{... | collective-permute-start | bytes 196616 | tf_op jit(solution)/shard_map/ppermute | solution.py:211
  47.3 0.0 copy-done.3
  47.3 2.0 %collective-permute-start.3 = (s32[1,256]{1,0:T(1,128)S(1)}, s32[1,256]{1,0:T(1,128)S(1)}, u32[]{:S(2)}, u32[]{:S(2)}) collective-permute-start(s32[1,256]{1,0:T(1,128)S(1)} %bitcast.14), channel_id=1, source_target_pairs={{0,0},{1,32},{2,64},{3,96},{4,128},{5,160},{6,192},{7,224},{8,8},{... | collective-permute-start | bytes 3080 | tf_op jit(solution)/shard_map/ppermute | solution.py:212
  49.3 5.1 %collective-permute-done.3.owners = s32[1,256]{1,0:T(1,128)S(1)} collective-permute-done((s32[1,256]{1,0:T(1,128)S(1)}, s32[1,256]{1,0:T(1,128)S(1)}, u32[]{:S(2)}, u32[]{:S(2)}) %collective-permute-start.3) | collective-permute-done | bytes 1056 | tf_op jit(solution)/shard_map/ppermute | solution.py:212
  54.4 0.0 collective-permute-done.2.labels
  54.4 0.0 collective-permute-done.1.gd
  54.4 0.0 collective-permute-done.gu
  54.4 0.0 copy-done
  54.4 0.0 copy-done.1
  54.4 42.2 %decode_band.1 = f32[512,550]{1,0:T(8,128)S(1)} custom-call(bf16[32,25,8,128]{3,2,1,0:T(8,128)(2,1)S(1)} %all_to_all.15.g, bf16[8,25,8,128]{3,2,1,0:T(8,128)(2,1)S(1)} %collective-permute-done.gu, bf16[8,25,8,128]{3,2,1,0:T(8,128)(2,1)S(1)} %collective-permute-done.1.gd, s32[2,32,256]{2,1,0:T(8,128)S(1)} %collective-permute-done.2.labels, ...), custom_call_target="tpu_custom_call" | custom-call | tf_op jit(solution)/shard_map/decode_band/pallas_call | solution.py:186
  96.6 0.1 convert_element_type.30
  96.7 28.7 %all_to_all.16 = f16[8,64,550]{2,1,0:T(8,128)(2,1)S(1)} all-to-all(f16[8,64,550]{2,1,0:T(8,128)(2,1)S(1)} %bitcast.12), channel_id=1, replica_groups=mesh['z'=8,'x'=4,'r'=8] {'z'}, dimensions={0} | all-to-all | bytes 1126400 | tf_op jit(solution)/shard_map/all_to_all | solution.py:219
  125.4 0.1 convert_reduce_fusion
  125.5 0.1 broadcast_in_dim.2
  125.6 21.3 %all_to_all.17 = f16[32,16,550]{2,1,0:T(8,128)(2,1)S(1)} all-to-all(f16[32,16,550]{2,1,0:T(8,128)(2,1)S(1)} %bitcast.11), channel_id=1, replica_groups=mesh['z'=8,'x'=4,'r'=8] {'x','r'}, dimensions={0} | all-to-all | bytes 1126400 | tf_op jit(solution)/shard_map/all_to_all | solution.py:222
  146.9 0.1 convert_multiply_fusion
  147.0 1.2 copy.6
  (1 shorter events, 0.0 us)
Async XLA Ops:
  38.0 5.7 %copy-start.2 = (s32[2,32,256]{2,1,0:T(8,128)S(1)}, s32[2,32,256]{2,1,0:T(8,128)}, u32[]{:S(2)}) copy-start(s32[2,32,256]{2,1,0:T(8,128)} %param.6) | copy-start | bytes 196612
  38.0 9.3 %copy-start.3 = (s32[256,1]{0,1:T(1,128)S(1)}, s32[256,1]{0,1:T(1,128)}, u32[]{:S(2)}) copy-start(s32[256,1]{0,1:T(1,128)} %param.8) | copy-start | bytes 3076
  38.0 16.4 %copy-start = (bf16[48,550]{1,0:T(8,128)(2,1)S(1)}, bf16[48,550]{1,0:T(8,128)(2,1)}, u32[]{:S(2)}) copy-start(bf16[48,550]{1,0:T(8,128)(2,1)} %codebook.1) | copy-start | bytes 158404
  38.0 16.4 %copy-start.1 = (s32[32]{0:T(128)S(1)}, s32[32]{0:T(128)}, u32[]{:S(2)}) copy-start(s32[32]{0:T(128)} %counts.1) | copy-start | bytes 388
  38.1 16.3 %collective-permute-start.1 = (bf16[8,25,8,128]{3,2,1,0:T(8,128)(2,1)S(1)}, bf16[8,25,8,128]{3,2,1,0:T(8,128)(2,1)S(1)}, u32[]{:S(2)}, u32[]{:S(2)}) collective-permute-start(bf16[8,25,8,128]{3,2,1,0:T(8,128)(2,1)S(1)} %get-tuple-element.5), channel_id=1, source_target_pairs={{32,0},{64,32},{96,64},{128,96},{160,128},{192,160},{224,192},{33,... | collective-permute-start | bytes 1228808 | tf_op jit(solution)/shard_map/ppermute | solution.py:216
  39.5 14.9 %collective-permute-start = (bf16[8,25,8,128]{3,2,1,0:T(8,128)(2,1)S(1)}, bf16[8,25,8,128]{3,2,1,0:T(8,128)(2,1)S(1)}, u32[]{:S(2)}, u32[]{:S(2)}) collective-permute-start(bf16[8,25,8,128]{3,2,1,0:T(8,128)(2,1)S(1)} %get-tuple-element.6), channel_id=1, source_target_pairs={{0,32},{32,64},{64,96},{96,128},{128,160},{160,192},{192,224},{1,3... | collective-permute-start | bytes 1228808 | tf_op jit(solution)/shard_map/ppermute | solution.py:215
  43.7 10.7 %collective-permute-start.2 = (s32[2,32,256]{2,1,0:T(8,128)S(1)}, s32[2,32,256]{2,1,0:T(8,128)S(1)}, u32[]{:S(2)}, u32[]{:S(2)}) collective-permute-start(s32[2,32,256]{2,1,0:T(8,128)S(1)} %copy-done.2), channel_id=1, source_target_pairs={{0,0},{1,32},{2,64},{3,96},{4,128},{5,160},{6,192},{7,224},{8,8},{... | collective-permute-start | bytes 196616 | tf_op jit(solution)/shard_map/ppermute | solution.py:211
  47.3 7.1 %collective-permute-start.3 = (s32[1,256]{1,0:T(1,128)S(1)}, s32[1,256]{1,0:T(1,128)S(1)}, u32[]{:S(2)}, u32[]{:S(2)}) collective-permute-start(s32[1,256]{1,0:T(1,128)S(1)} %bitcast.14), channel_id=1, source_target_pairs={{0,0},{1,32},{2,64},{3,96},{4,128},{5,160},{6,192},{7,224},{8,8},{... | collective-permute-start | bytes 3080 | tf_op jit(solution)/shard_map/ppermute | solution.py:212

commit v2 on v1

v2 whole, which is shorter than its diff:
```python
import jax
import jax.numpy as jnp
from jax import lax
from jax.experimental import pallas as pl
from jax.experimental.pallas import tpu as pltpu
from jax.sharding import Mesh, PartitionSpec as P

SOFTMAX_HEAT = 0.6
SHARPEN = 0.15
NOISE_LEVEL = 1.0
LOG2E = 1.4426950408889634

CH, GENES, ZP, PT, CELLS, TILES, CAP = 48, 550, 2, 256, 256, 32, 16
NZ, NXD, NR = 8, 4, 8
GP = 552
COLOUR = CH // NR
PAIRS = COLOUR * ZP
PIECE = 2 * PAIRS + 1
ROWS = 32
WIDE = PT + 128
VOX = ZP * PT
SCALE = 0.25
SAFE = 100.0
F32, BF16 = jnp.float32, jnp.bfloat16
NT = (((1,), (1,)), ((), ()))


def position():
    return lax.axis_index("z"), lax.axis_index("x"), lax.axis_index("r")


def pack_kernel(img, labels, owners, counts, out, marks):
    z, x_here, _ = position()
    lane = lax.broadcasted_iota(jnp.int32, (8, 128), 1)
    windows = [(lane // 4) == i for i in range(PAIRS)]

    def column(r, _):
        start = pl.multiple_of(r * (NXD * PT), NXD * PT)
        before = pl.multiple_of(jnp.maximum(start - 128, 0), 128)
        after = pl.multiple_of(jnp.minimum(start + NXD * PT, (TILES * PT) - 128), 128)
        has_before, has_after = (r > 0).astype(F32), (r < NR - 1).astype(F32)
        for x in range(NXD):
            border = jnp.zeros((8, 128), F32)
            for i in range(PAIRS):
                c, p = i // ZP, i % ZP
                for t in range(2):
                    out[x * NR + r, 2 * i + t] = img[c, p, :, pl.ds(start + PT * x + 128 * t, 128)]
                if x < NXD - 1:
                    right = img[c, p, :, pl.ds(start + PT * (x + 1), 128)].astype(F32)
                else:
                    right = img[c, p, :, pl.ds(after, 128)].astype(F32) * has_after
                if x > 0:
                    left = img[c, p, :, pl.ds(start + PT * x - 128, 128)].astype(F32)
                else:
                    left = img[c, p, :, pl.ds(before, 128)].astype(F32) * has_before
                both = pltpu.roll(jnp.where(lane < 64, right, left), 4 * i + 2, 1)
                border = jnp.where(windows[i], both, border)
            out[x * NR + r, 2 * PAIRS] = border.astype(BF16)
        return 0

    lax.fori_loop(0, NR, column, 0)

    owner = owners[...]
    own = lax.broadcasted_iota(jnp.int32, (TILES, CELLS), 0) == owner
    own_f = jnp.where(own, 1.0, 0.0)
    earlier = lax.broadcasted_iota(jnp.int32, (CELLS, CELLS), 0) < lax.broadcasted_iota(jnp.int32, (CELLS, CELLS), 1)
    earlier = jnp.where(earlier, 1.0, 0.0).astype(BF16)
    ahead = jnp.dot(own_f.astype(BF16), earlier, preferred_element_type=F32)
    place = jnp.sum(own_f * ahead, axis=0, keepdims=True).astype(jnp.int32)
    cell = lax.broadcasted_iota(jnp.int32, (1, CELLS), 1)
    goes = jnp.where(cell < counts[NXD * z + x_here], owner * CAP + place, -1)
    for p in range(ZP):
        marks[p * ROWS : (p + 1) * ROWS] = labels[p]
    marks[ZP * ROWS :] = jnp.broadcast_to(goes, (8, CELLS))


def pack(images, labels, owners, counts):
    vmem, smem = pl.BlockSpec(memory_space=pltpu.VMEM), pl.BlockSpec(memory_space=pltpu.SMEM)
    return pl.pallas_call(
        pack_kernel,
        in_specs=[vmem, vmem, vmem, smem],
        out_specs=[vmem, vmem],
        out_shape=[
            jax.ShapeDtypeStruct((NXD * NR, PIECE, 8, 128), BF16),
            jax.ShapeDtypeStruct((ZP * ROWS + 8, CELLS), jnp.int32),
        ],
        compiler_params=pltpu.CompilerParams(vmem_limit_bytes=32 * 1024 * 1024),
        name="pack_pieces",
    )(images, labels, owners, counts)


def channels_last(load):
    return [jnp.swapaxes(jnp.stack([load(r, c) for r in range(NR)]).astype(F32), 0, 1) for c in range(COLOUR)]


def border_masks():
    lane = lax.broadcasted_iota(jnp.int32, (CH, 128), 1)
    colour = lax.broadcasted_iota(jnp.int32, (CH, 128), 0) // NR
    return [(lane // 4) == colour * ZP + p for p in range(ZP)]


def transposed_rows(src, rows, store):
    masks = border_masks()
    edge = jnp.swapaxes(jnp.stack([src(r, 2 * PAIRS) for r in range(NR)]).astype(F32), 0, 1)
    for p in range(ZP):
        for t in range(2):
            parts = channels_last(lambda r, c: src(r, 2 * (ZP * c + p) + t))
            for row in rows:
                block = jnp.concatenate([part[row] for part in parts], axis=0)
                store(row, p, t, block.astype(BF16))
        for row in rows:
            block = jnp.concatenate([edge[row]] * COLOUR, axis=0)
            store(row, p, 2, jnp.where(masks[p], block, 0.0).astype(BF16))


def stencil_kernel(g, unit, rim, ends, band, xt, y, a_s, b_s):
    z, x, r = position()
    tile = NXD * r + x
    left_ok = (tile > 0).astype(F32)
    right_ok = (tile < TILES - 1).astype(F32)

    source = lax.broadcasted_iota(jnp.int32, (WIDE, PT), 0)
    target = lax.broadcasted_iota(jnp.int32, (WIDE, PT), 1)
    e = source - PT
    side = e % 4
    beyond = jnp.where(side < 2, side - 2, PT - 2 + side)
    at = jnp.where(source < PT, source, jnp.where(e < 4 * PAIRS, beyond, 4 * WIDE))
    gap = jnp.abs(at - target)
    own = 2.0 - jnp.where(at == 0, 1.0 - left_ok, 0.0) - jnp.where(at == PT - 1, 1.0 - right_ok, 0.0)
    band[:, :PT] = jnp.where(gap == 1, 1.0, 0.0).astype(BF16)
    band[:, PT:] = jnp.where(gap == 2, 1.0, jnp.where(gap == 0, own, 0.0)).astype(BF16)

    step = ZP * CH
    blank = jnp.zeros((step, WIDE), BF16)
    xt[:step] = blank
    xt[(ROWS + 1) * step :] = blank

    def regroup(k, _):
        base = (k * 8 + 1) * step

        def store(row, p, t, block):
            start = pl.multiple_of(base + (row * ZP + p) * CH, 16)
            xt[pl.ds(start, CH), t * 128 : (t + 1) * 128] = block

        transposed_rows(lambda r, i: g[k * NR + r, i], range(8), store)
        rows = xt[pl.ds(pl.multiple_of(base, 16), 8 * step), :]
        y[pl.ds(pl.multiple_of(k * 8 * step, 16), 8 * step), :] = jnp.dot(rows, band[...], preferred_element_type=F32)
        return 0

    lax.fori_loop(0, ROWS // 8, regroup, 0)

    def raw(row, p, t):
        start = pl.multiple_of((row + 1) * step + p * CH, 16)
        return xt[pl.ds(start, CH), t * 128 : (t + 1) * 128].astype(F32)

    def cols(row, p, t, twice):
        start = pl.multiple_of(row * step + p * CH, 16)
        at = twice * PT + t * 128
        return y[pl.ds(start, CH), at : at + 128]

    b_s[0] = jnp.zeros_like(b_s[0])
    b_s[ROWS + 1] = jnp.zeros_like(b_s[0])

    def first(row, _):
        for t in range(2):
            here = [raw(row, p, t) for p in range(ZP)]
            for p in range(ZP):
                mx = 6.0 * here[p] - (raw(row - 1, p, t) + raw(row + 1, p, t)) - here[1 - p]
                cx = cols(row, p, t, 0)
                a = mx - cx
                a_s[row, p, t] = a
                b_s[row + 1, p, t] = a - cx
        return 0

    lax.fori_loop(0, ROWS, first, 0)

    def sharp7(row, t):
        mid = [b_s[row + 1, p, t] for p in range(ZP)]
        outs = []
        for p in range(ZP):
            mb = 6.0 * mid[p] - (b_s[row, p, t] + b_s[row + 2, p, t]) - mid[1 - p]
            outs.append(a_s[row, p, t] + SHARPEN * (mb + cols(row, p, t, 1)))
        return outs

    def second(row, _):
        for t in range(2):
            for p, value in enumerate(sharp7(row, t)):
                unit[row, :, p * PT + t * 128 : p * PT + (t + 1) * 128] = normalise(value)
        return 0

    lax.fori_loop(2, ROWS - 2, second, 0)
    for k, row in enumerate((0, 1, ROWS - 2, ROWS - 1)):
        for t in range(2):
            for p, value in enumerate(sharp7(row, t)):
                rim[k, p, t] = value
    for k, row in enumerate((0, ROWS - 1)):
        for t in range(2):
            for p in range(ZP):
                ends[k, p, t] = raw(row, p, t)


def normalise(value):
    mean = jnp.sum(value * value, axis=0, keepdims=True) * (1.0 / CH)
    return (value * lax.rsqrt(mean + 49.0 * NOISE_LEVEL)).astype(BF16)


def stencil(g):
    vmem = pl.BlockSpec(memory_space=pltpu.VMEM)
    step = ZP * CH
    return pl.pallas_call(
        stencil_kernel,
        in_specs=[vmem],
        out_specs=[vmem] * 4,
        out_shape=[
            jax.ShapeDtypeStruct((ROWS, CH, VOX), BF16),
            jax.ShapeDtypeStruct((4, ZP, 2, CH, 128), F32),
            jax.ShapeDtypeStruct((2, ZP, 2, CH, 128), F32),
            jax.ShapeDtypeStruct((WIDE, 2 * PT), BF16),
        ],
        scratch_shapes=[
            pltpu.VMEM(((ROWS + 2) * step, WIDE), BF16),
            pltpu.VMEM((ROWS * step, 2 * PT), F32),
            pltpu.VMEM((ROWS, ZP, 2, CH, 128), F32),
            pltpu.VMEM((ROWS + 2, ZP, 2, CH, 128), F32),
        ],
        compiler_params=pltpu.CompilerParams(vmem_limit_bytes=40 * 1024 * 1024),
        cost_estimate=pl.CostEstimate(flops=8_000_000_000, bytes_accessed=8_000_000, transcendentals=0),
        name="stencil_band",
    )(g)


def posterior_kernel(unit, rim, ends, band, gu, gd, marks, codebook, out, xh, ue, cbt, acc, e0, e1):
    z = position()[0]
    for side, src in enumerate((gu, gd)):
        near, far = (7, 6) if side == 0 else (0, 1)

        def store(row, p, t, block):
            start = (p + (0 if row == near else ZP)) * CH
            xh[start : start + CH, t * 128 : (t + 1) * 128] = block

        transposed_rows(lambda r, i: src[r, i], (near, far), store)
        cx = jnp.dot(xh[: ZP * CH], band[:, :PT], preferred_element_type=F32)
        inside = jnp.where((z > 0) if side == 0 else (z < NZ - 1), 1.0, 0.0)
        k0, k1 = (0, 1) if side == 0 else (3, 2)
        for t in range(2):
            lanes = slice(t * 128, (t + 1) * 128)
            x1 = [xh[p * CH : (p + 1) * CH, lanes].astype(F32) for p in range(ZP)]
            x2 = [xh[(p + ZP) * CH : (p + ZP + 1) * CH, lanes].astype(F32) for p in range(ZP)]
            for p in range(ZP):
                b1 = 6.0 * x1[p] - (ends[side, p, t] + x2[p]) - x1[1 - p] - 2.0 * cx[p * CH : (p + 1) * CH, lanes]
                b1 = b1 * inside
                at = slice(p * PT + t * 128, p * PT + (t + 1) * 128)
                ue[k0, :, at] = normalise(rim[k0, p, t] - x1[p] + SHARPEN * (x1[1 - p] - 6.0 * x1[p] - b1))
                ue[k1, :, at] = normalise(rim[k1, p, t] + SHARPEN * x1[p])

    out_row = lax.broadcasted_iota(jnp.int32, (CH, CH), 0)
    in_row = lax.broadcasted_iota(jnp.int32, (CH, CH), 1)
    order = jnp.where(in_row == (out_row % NR) * COLOUR + out_row // NR, 1.0, 0.0).astype(BF16)
    wide = jnp.dot(order, codebook[...], preferred_element_type=F32)
    bound = jnp.max(jnp.sum(wide * wide, axis=0, keepdims=True))
    fine = bound * (CH * (1.01 * SOFTMAX_HEAT * LOG2E) ** 2) <= SAFE * SAFE
    wide = wide * (SOFTMAX_HEAT * LOG2E)
    flat = jnp.concatenate([wide, jnp.zeros((CH, GP - GENES), F32)], axis=1).T
    hi = flat.astype(BF16)
    mid = (flat - hi.astype(F32)).astype(BF16)
    lo = (flat - hi.astype(F32) - mid.astype(F32)).astype(BF16)
    gene = lax.broadcasted_iota(jnp.int32, (GP, 16), 0)
    which = lax.broadcasted_iota(jnp.int32, (GP, 16), 1)
    shut = jnp.where((gene >= GENES) & (which == 0), -3.0e38, 0.0).astype(BF16)
    cbt[...] = jnp.concatenate([hi, mid, lo, shut], axis=1)
    acc[...] = jnp.zeros_like(acc)
    slots = lax.broadcasted_iota(jnp.int32, (CELLS, VOX), 0)
    rim_rows = (0, 1, ROWS - 2, ROWS - 1)

    def logits_of(u):
        stacked = jnp.concatenate([u, u, u, jnp.ones((16, VOX), BF16)], axis=0)
        return jnp.dot(cbt[...], stacked, preferred_element_type=F32)

    def add(post, row):
        label = jnp.concatenate([marks[pl.ds(p * ROWS + row, 1), :] for p in range(ZP)], axis=1)
        onehot = jnp.where(slots == label, 1.0, 0.0).astype(BF16)
        acc[...] += lax.dot_general(post, onehot, NT, preferred_element_type=F32)

    def plain(u, e_s):
        e = jnp.exp2(logits_of(u))
        e_s[...] = e
        return 1.0 / jnp.sum(e, axis=0, keepdims=True)

    def finish(inverse, row, e_s):
        add((e_s[...] * inverse).astype(BF16), row)

    @pl.when(fine)
    def _():
        inv = plain(ue[0], e0)
        nxt = plain(ue[1], e1)
        finish(inv, 0, e0)
        inv = plain(ue[2], e0)
        finish(nxt, 1, e1)
        nxt = plain(ue[3], e1)
        finish(inv, ROWS - 2, e0)
        inv = plain(unit[2], e0)
        finish(nxt, ROWS - 1, e1)

        def pair(k, inv):
            row = 2 * k + 2
            nxt = plain(unit[row + 1], e1)
            finish(inv, row, e0)
            inv = plain(unit[jnp.minimum(row + 2, ROWS - 3)], e0)
            finish(nxt, row + 1, e1)
            return inv

        lax.fori_loop(0, (ROWS - 4) // 2, pair, inv)

    @pl.when(jnp.logical_not(fine))
    def _():
        def careful(u, row):
            logits = logits_of(u)
            e = jnp.exp2(logits - jnp.max(logits, axis=0, keepdims=True))
            add((e * (1.0 / jnp.sum(e, axis=0, keepdims=True))).astype(BF16), row)

        def inner(row, _):
            careful(unit[row], row)
            return 0

        def outer(k, _):
            careful(ue[k], jnp.where(k < 2, k, ROWS - 4 + k))
            return 0

        lax.fori_loop(2, ROWS - 2, inner, 0)
        lax.fori_loop(0, 4, outer, 0)

    goes = marks[ZP * ROWS : ZP * ROWS + 1]
    select = jnp.where(lax.broadcasted_iota(jnp.int32, (TILES * CAP, CELLS), 0) == goes, SCALE, 0.0).astype(BF16)
    sums = acc[...]
    high = sums.astype(BF16)
    low = (sums - high.astype(F32)).astype(BF16)
    packed = lax.dot_general(select, high, NT, preferred_element_type=F32)
    packed = packed + lax.dot_general(select, low, NT, preferred_element_type=F32)
    out[...] = packed[:, :GENES]


def posterior(unit, rim, ends, band, gu, gd, marks, codebook):
    vmem = pl.BlockSpec(memory_space=pltpu.VMEM)
    return pl.pallas_call(
        posterior_kernel,
        in_specs=[vmem] * 8,
        out_specs=vmem,
        out_shape=jax.ShapeDtypeStruct((TILES * CAP, GENES), F32),
        scratch_shapes=[
            pltpu.VMEM((2 * ZP * CH, WIDE), BF16),
            pltpu.VMEM((4, CH, VOX), BF16),
            pltpu.VMEM((GP, 3 * CH + 16), BF16),
            pltpu.VMEM((GP, CELLS), F32),
            pltpu.VMEM((GP, VOX), F32),
            pltpu.VMEM((GP, VOX), F32),
        ],
        compiler_params=pltpu.CompilerParams(vmem_limit_bytes=40 * 1024 * 1024),
        name="posterior_sums",
    )(unit, rim, ends, band, gu, gd, marks, codebook)


def local(images, labels, counts, owners, codebook):
    swap = [
        (z * NXD * NR + x * NR + r, r * NXD * NR + x * NR + z)
        for z in range(NZ)
        for x in range(NXD)
        for r in range(NR)
    ]
    pieces, marks = pack(images, labels, owners.reshape(1, CELLS), counts)
    marks = lax.ppermute(marks, ("z", "x", "r"), swap)
    g = lax.all_to_all(pieces, ("x", "r"), split_axis=0, concat_axis=0, tiled=True)
    gu = lax.ppermute(g[(NXD - 1) * NR :], "z", [(i, i + 1) for i in range(NZ - 1)])
    gd = lax.ppermute(g[:NR], "z", [(i + 1, i) for i in range(NZ - 1)])
    unit, rim, ends, band = stencil(g)
    packed = posterior(unit, rim, ends, band, gu, gd, marks, codebook)
    packed = packed.astype(jnp.float16).reshape(NZ, NXD * CAP, GENES)
    parts = lax.all_to_all(packed, "z", split_axis=0, concat_axis=0, tiled=True)
    summed = jnp.sum(parts.astype(F32), axis=0).astype(jnp.float16).reshape(NXD, 1, CAP, GENES)
    spread = jnp.broadcast_to(summed, (NXD, NR, CAP, GENES)).reshape(NXD * NR, CAP, GENES)
    received = lax.all_to_all(spread, ("x", "r"), split_axis=0, concat_axis=0, tiled=True)
    received = received.reshape(NXD, NR, CAP, GENES).transpose(1, 0, 2, 3).reshape(1, TILES, CAP, GENES)
    return received.astype(F32) * (1.0 / SCALE)


def solution(mesh):
    grid = Mesh(mesh.devices.reshape(NZ, NXD, NR), ("z", "x", "r"))
    in_specs = (P("r", None, ("z", "x"), None), P(None, "r", ("z", "x")), P(), P(("z", "x"), None), P())
    out_specs = P(("z", "x"), None, None, None)
    return jax.shard_map(local, mesh=grid, in_specs=in_specs, out_specs=out_specs, check_vma=False)
```

time: 149 us -> 132 us (0.89)
  blocking collectives: 82.1 us -> 50.6 us
  waiting for transfers between devices: 5.08 us -> 21.3 us
  Pallas kernels: 48.1 us -> 36.1 us
  starting transfers between devices: 11.2 us -> 17.9 us
  local copies, waits for them, and re-layouts: 1.31 us -> 4.88 us
    all_to_all x1 -> x0, blocking collectives: 32.1 us -> none  [local(): lax.all_to_all(pieces, ('x', 'r'), split_axis=0, concat_axis=0, tiled=True)]
    all_to_all x0 -> x1, waiting for transfers between devices: none -> 19.7 us  [local(): lax.all_to_all(pieces, ('x', 'r'), split_axis=0, concat_axis=0, tiled=True)]
    pallas_call x2 -> x3, Pallas kernels: 48.1 us -> 36.1 us  [the longest x1 26.9 us: posterior(): pl.pallas_call(posterior_kernel, in_specs=[vmem] * 8, out_specs=vmem, out...]
    all_to_all x0 -> x1, starting transfers between devices: none -> 8.59 us  [local(): lax.all_to_all(pieces, ('x', 'r'), split_axis=0, concat_axis=0, tiled=True)]
    ppermute x2 -> x1, waiting for transfers between devices: 5.08 us -> 0.01 us  [local(): marks = lax.ppermute(marks, ('z', 'x', 'r'), swap)]
    unnamed x8 -> x10, local copies, waits for them, and re-layouts: 0.01 us -> 3.59 us
    ppermute x2 -> x1, starting transfers between devices: 5.56 us -> 3.67 us  [local(): marks = lax.ppermute(marks, ('z', 'x', 'r'), swap)]
  transfers between devices with their start and end apart: 4 -> 4, of which waited for: 1 -> 3; matrix products, arithmetic and copies ran while one was open for 0% -> 0% of each run, Pallas kernels for 0% -> 5%
where the time goes in v2:
time: 132 us; the launch traced here: 131 us
  blocking collectives  50.6 us (38%)
  Pallas kernels  36.1 us (27%)
  waiting for transfers between devices  21.3 us (16%)
  starting transfers between devices  17.9 us (14%)
  local copies, waits for them, and re-layouts  4.88 us (4%)
    all_to_all x1, blocking collectives, local(): parts = lax.all_to_all(packed, 'z', split_axis=0, concat_axis=0, tiled=True)  30 us
    pallas_call x1, Pallas kernels, posterior(): pl.pallas_call(posterior_kernel, in_specs=[vmem] * 8, out_specs=vmem, out...  26.9 us
    all_to_all x1, blocking collectives, local(): lax.all_to_all(spread, ('x', 'r'), split_axis=0, concat_axis=0, tiled=True)  20.6 us
    all_to_all x1, waiting for transfers between devices, local(): lax.all_to_all(pieces, ('x', 'r'), split_axis=0, concat_axis=0, tiled=True)  19.7 us
    all_to_all x1, starting transfers between devices, local(): lax.all_to_all(pieces, ('x', 'r'), split_axis=0, concat_axis=0, tiled=True)  8.59 us
    pallas_call x1, Pallas kernels, stencil(): pl.pallas_call(stencil_kernel, in_specs=[vmem], out_specs=[vmem] * 4, out...  6.17 us
    ppermute x1, starting transfers between devices, local(): lax.ppermute(g[(NXD - 1) * NR:], 'z', [(i, i + 1) for i in range(NZ - 1)])  4.33 us
    ppermute x1, starting transfers between devices, local(): marks = lax.ppermute(marks, ('z', 'x', 'r'), swap)  3.67 us
  transfers between devices with their start and end apart: 4, of which 3 were waited for; matrix products, arithmetic and copies ran while one was open for 0% of the time, Pallas kernels for 5%

profile of v2, /device:TPU:1, one launch (start us, length us, event | category | flops | bytes accessed | tf_op | source)
XLA Modules:
  0.0 131.2 jit_solution(10409642578647866335)
XLA Ops:
  0.0 0.0 copy-start
  0.0 1.4 %copy-done = bf16[6,2,8,8192]{3,2,1,0:T(8,128)(2,1)S(1)} copy-done((bf16[6,2,8,8192]{3,2,1,0:T(8,128)(2,1)S(1)}, bf16[6,2,8,8192]{3,2,1,0:T(8,128)(2,1)}, u32[]{:S(2)}) %copy-start) | copy-done | bytes 1572888
  1.4 0.0 copy-start.1
  1.4 0.8 copy-done.1
  2.2 0.0 copy-start.3
  2.3 0.7 copy-done.3
  2.9 0.0 copy-start.4
  2.9 0.7 copy-done.4
  3.6 3.0 %pack_pieces.1 = (bf16[32,25,8,128]{3,2,1,0:T(8,128)(2,1)}, s32[72,256]{1,0:T(8,128)S(1)}) custom-call(bf16[6,2,8,8192]{3,2,1,0:T(8,128)(2,1)S(1)} %copy-done, s32[2,32,256]{2,1,0:T(8,128)S(1)} %copy-done.1, s32[1,256]{1,0:T(1,128)S(1)} %bitcast.8, s32[32]{0:T(128)S(1)} %copy-done.4), custom_call_target="tpu_custom_call" | custom-call | tf_op jit(solution)/shard_map/pack_pieces/pallas_call | solution.py:79
  6.5 8.6 %all-to-all-start = ((bf16[32,25,8,128]{3,2,1,0:T(8,128)(2,1)}), bf16[32,25,8,128]{3,2,1,0:T(8,128)(2,1)S(1)}, u32[]{:S(2)}, u32[]{:S(2)}) async-start(bf16[32,25,8,128]{3,2,1,0:T(8,128)(2,1)} %get-tuple-element.11), calls=%async_computation | async-start | bytes 3276800 | tf_op jit(solution)/shard_map/all_to_all | solution.py:371
  15.1 3.7 %collective-permute-start.2 = (s32[72,256]{1,0:T(8,128)S(1)}, s32[72,256]{1,0:T(8,128)S(1)}, u32[]{:S(2)}, u32[]{:S(2)}) collective-permute-start(s32[72,256]{1,0:T(8,128)S(1)} %get-tuple-element.16), channel_id=1, source_target_pairs={{0,0},{1,32},{2,64},{3,96},{4,128},{5,160},{6,192},{7,224},{8,8},{... | collective-permute-start | bytes 221192 | tf_op jit(solution)/shard_map/ppermute | solution.py:370
  18.8 19.7 %all-to-all-done.g = bf16[32,25,8,128]{3,2,1,0:T(8,128)(2,1)S(1)} async-done(((bf16[32,25,8,128]{3,2,1,0:T(8,128)(2,1)}), bf16[32,25,8,128]{3,2,1,0:T(8,128)(2,1)S(1)}, u32[]{:S(2)}, u32[]{:S(2)}) %all-to-all-start) | async-done | bytes 1638432 | tf_op jit(solution)/shard_map/all_to_all | solution.py:371
  38.5 0.1 fusion
  38.6 1.3 collective-permute-start.1
  39.9 0.0 copy-start.2
  39.9 4.3 %collective-permute-start = (bf16[8,25,8,128]{3,2,1,0:T(8,128)(2,1)S(1)}, bf16[8,25,8,128]{3,2,1,0:T(8,128)(2,1)S(1)}, u32[]{:S(2)}, u32[]{:S(2)}) collective-permute-start(bf16[8,25,8,128]{3,2,1,0:T(8,128)(2,1)S(1)} %get-tuple-element.18), channel_id=1, source_target_pairs={{0,32},{32,64},{64,96},{96,128},{128,160},{160,192},{192,224},{1,3... | collective-permute-start | bytes 1228808 | tf_op jit(solution)/shard_map/ppermute | solution.py:372
  44.2 6.2 %stencil_band.1 = (bf16[32,48,512]{2,1,0:T(8,128)(2,1)S(1)}, f32[4,2,2,48,128]{4,3,2,1,0:T(8,128)S(1)}, f32[2,2,2,48,128]{4,3,2,1,0:T(8,128)S(1)}, bf16[384,512]{1,0:T(8,128)(2,1)S(1)}) custom-call(bf16[32,25,8,128]{3,2,1,0:T(8,128)(2,1)S(1)} %all-to-all-done.g), custom_call_target="tpu_custom_call" | custom-call | flops 8000000000 | bytes 8000000 | tf_op jit(solution)/shard_map/stencil_band/pallas_call | solution.py:210
  50.4 0.0 collective-permute-done.2.marks
  50.4 0.6 collective-permute-done.1.gd
  51.1 1.0 collective-permute-done.gu
  52.1 0.0 copy-done.2
  52.1 26.9 %posterior_sums.1 = f32[512,550]{1,0:T(8,128)S(1)} custom-call(bf16[32,48,512]{2,1,0:T(8,128)(2,1)S(1)} %get-tuple-element.12.unit, f32[4,2,2,48,128]{4,3,2,1,0:T(8,128)S(1)} %get-tuple-element.13.rim, f32[2,2,2,48,128]{4,3,2,1,0:T(8,128)S(1)} %get-tuple-element.14.ends, bf16[384,512]{1,0:T(8,128)(2,1)S(1)} %get-tuple-element.15.band, ...), custom_call_target="tpu_custom_call" | custom-call | tf_op jit(solution)/shard_map/posterior_sums/pallas_call | solution.py:344
  79.0 0.1 convert_element_type.30
  79.1 30.0 %all_to_all.15 = f16[8,64,550]{2,1,0:T(8,128)(2,1)S(1)} all-to-all(f16[8,64,550]{2,1,0:T(8,128)(2,1)S(1)} %bitcast.11), channel_id=1, replica_groups=mesh['z'=8,'x'=4,'r'=8] {'z'}, dimensions={0} | all-to-all | bytes 1126400 | tf_op jit(solution)/shard_map/all_to_all | solution.py:377
  109.1 0.1 convert_reduce_fusion
  109.2 0.1 broadcast_in_dim.2
  109.3 20.6 %all_to_all.16 = f16[32,16,550]{2,1,0:T(8,128)(2,1)S(1)} all-to-all(f16[32,16,550]{2,1,0:T(8,128)(2,1)S(1)} %bitcast.10), channel_id=1, replica_groups=mesh['z'=8,'x'=4,'r'=8] {'x','r'}, dimensions={0} | all-to-all | bytes 1126400 | tf_op jit(solution)/shard_map/all_to_all | solution.py:380
  129.9 0.1 convert_multiply_fusion
  130.0 1.2 copy.6
  (1 shorter events, 0.0 us)
Async XLA Ops:
  0.0 1.4 %copy-start = (bf16[6,2,8,8192]{3,2,1,0:T(8,128)(2,1)S(1)}, bf16[6,2,8,8192]{3,2,1,0:T(8,128)(2,1)}, u32[]{:S(2)}) copy-start(bf16[6,2,8,8192]{3,2,1,0:T(8,128)(2,1)} %img.1) | copy-start | bytes 4718596
  1.4 0.8 copy-start.1
  2.2 0.7 copy-start.3
  2.9 0.7 copy-start.4
  6.5 32.0 %all-to-all-start = ((bf16[32,25,8,128]{3,2,1,0:T(8,128)(2,1)}), bf16[32,25,8,128]{3,2,1,0:T(8,128)(2,1)S(1)}, u32[]{:S(2)}, u32[]{:S(2)}) async-start(bf16[32,25,8,128]{3,2,1,0:T(8,128)(2,1)} %get-tuple-element.11), calls=%async_computation | async-start | bytes 3276800 | tf_op jit(solution)/shard_map/all_to_all | solution.py:371
  15.1 35.3 %collective-permute-start.2 = (s32[72,256]{1,0:T(8,128)S(1)}, s32[72,256]{1,0:T(8,128)S(1)}, u32[]{:S(2)}, u32[]{:S(2)}) collective-permute-start(s32[72,256]{1,0:T(8,128)S(1)} %get-tuple-element.16), channel_id=1, source_target_pairs={{0,0},{1,32},{2,64},{3,96},{4,128},{5,160},{6,192},{7,224},{8,8},{... | collective-permute-start | bytes 221192 | tf_op jit(solution)/shard_map/ppermute | solution.py:370
  38.6 12.5 %collective-permute-start.1 = (bf16[8,25,8,128]{3,2,1,0:T(8,128)(2,1)S(1)}, bf16[8,25,8,128]{3,2,1,0:T(8,128)(2,1)S(1)}, u32[]{:S(2)}, u32[]{:S(2)}) collective-permute-start(bf16[8,25,8,128]{3,2,1,0:T(8,128)(2,1)S(1)} %get-tuple-element.17), channel_id=1, source_target_pairs={{32,0},{64,32},{96,64},{128,96},{160,128},{192,160},{224,192},{33,... | collective-permute-start | bytes 1228808 | tf_op jit(solution)/shard_map/ppermute | solution.py:373
  39.9 12.2 %copy-start.2 = (bf16[48,550]{1,0:T(8,128)(2,1)S(1)}, bf16[48,550]{1,0:T(8,128)(2,1)}, u32[]{:S(2)}) copy-start(bf16[48,550]{1,0:T(8,128)(2,1)} %codebook.1) | copy-start | bytes 158404
  39.9 12.2 %collective-permute-start = (bf16[8,25,8,128]{3,2,1,0:T(8,128)(2,1)S(1)}, bf16[8,25,8,128]{3,2,1,0:T(8,128)(2,1)S(1)}, u32[]{:S(2)}, u32[]{:S(2)}) collective-permute-start(bf16[8,25,8,128]{3,2,1,0:T(8,128)(2,1)S(1)} %get-tuple-element.18), channel_id=1, source_target_pairs={{0,32},{32,64},{64,96},{96,128},{128,160},{160,192},{192,224},{1,3... | collective-permute-start | bytes 1228808 | tf_op jit(solution)/shard_map/ppermute | solution.py:372

commit v3 on v0

v3 whole, which is shorter than its diff:
```python
import functools

import jax
import jax.numpy as jnp
from jax import lax
from jax.experimental import pallas as pl
from jax.experimental.pallas import tpu as pltpu
from jax.sharding import Mesh, PartitionSpec as P

SOFTMAX_HEAT = 0.6
SHARPEN = 0.15
NOISE_LEVEL = 1.0
LOG2E = 1.4426950408889634

CH, GENES, ZP, PT, CELLS, TILES, CAP = 48, 550, 2, 256, 256, 32, 16
NZ, NXD, NR = 8, 4, 8
GP = 552
COLOUR = CH // NR
PAIRS = COLOUR * ZP
HALF = PT // 2
PIECE = PAIRS + 1
ROWS = 32
STEP = ZP * CH
WIDE = HALF + 128
VOX = 2 * ZP * HALF
MARKS = ZP * ROWS + 8
FULL = GENES // 128
REST = GENES - 128 * FULL
OUT_ROWS = FULL * CAP + CAP // 2
SCALE = 0.25
SAFE = 100.0
F32, BF16 = jnp.float32, jnp.bfloat16
NT = (((1,), (1,)), ((), ()))
VMEM = pl.BlockSpec(memory_space=pltpu.VMEM)
SMEM = pl.BlockSpec(memory_space=pltpu.SMEM)
MIB = 1024 * 1024


def position():
    return lax.axis_index("z"), lax.axis_index("x"), lax.axis_index("r")


def params(mib):
    return pltpu.CompilerParams(vmem_limit_bytes=mib * MIB)


def cost(us):
    return pl.CostEstimate(flops=int(us * 1e9), bytes_accessed=int(us * 3e6), transcendentals=0)


def pack_kernel(half, img, out, buf, sems):
    lane = lax.broadcasted_iota(jnp.int32, (8, 128), 1)
    windows = [(lane // 4) == i for i in range(PAIRS)]

    def fetch(r):
        start = pl.multiple_of(r * (NXD * PT), NXD * PT)
        return pltpu.make_async_copy(img.at[:, :, :, pl.ds(start, NXD * PT)], buf.at[r], sems.at[r])

    for r in range(NR):
        fetch(r).start()
    if half:
        fetch(0).wait()

    def column(r, _):
        if half:

            @pl.when(r < NR - 1)
            def _():
                fetch(jnp.minimum(r + 1, NR - 1)).wait()
        else:
            fetch(r).wait()
        near = jnp.minimum(r + 1, NR - 1) if half else jnp.maximum(r - 1, 0)
        inside = ((r < NR - 1) if half else (r > 0)).astype(F32)
        for x in range(NXD):
            at = PT * x + HALF * half
            border = jnp.zeros((8, 128), F32)
            for i in range(PAIRS):
                c, p = i // ZP, i % ZP
                out[x * NR + r, i] = buf[r, c, p, :, at : at + HALF]
                if at + HALF < NXD * PT:
                    right = buf[r, c, p, :, at + HALF : at + 2 * HALF].astype(F32)
                else:
                    right = buf[near, c, p, :, :128].astype(F32) * inside
                if at > 0:
                    left = buf[r, c, p, :, at - 128 : at].astype(F32)
                else:
                    left = buf[near, c, p, :, NXD * PT - 128 :].astype(F32) * inside
                both = pltpu.roll(jnp.where(lane < 64, right, left), 4 * i + 2, 1)
                border = jnp.where(windows[i], both, border)
            out[x * NR + r, PAIRS] = border.astype(BF16)
        return 0

    lax.fori_loop(0, NR, column, 0)


def pack(images, half):
    return pl.pallas_call(
        functools.partial(pack_kernel, half),
        in_specs=[pl.BlockSpec(memory_space=pltpu.HBM)],
        out_specs=VMEM,
        out_shape=jax.ShapeDtypeStruct((NXD * NR, PIECE, 8, 128), BF16),
        scratch_shapes=[pltpu.VMEM((NR, COLOUR, ZP, 8, NXD * PT), BF16), pltpu.SemaphoreType.DMA((NR,))],
        compiler_params=params(16),
        cost_estimate=cost(2),
        name="pack_half",
    )(images)


def prepare_kernel(labels, owners, counts, codebook, marks, cbt, bands):
    z, x, r = position()
    owner = owners[...]
    own = lax.broadcasted_iota(jnp.int32, (TILES, CELLS), 0) == owner
    own_f = jnp.where(own, 1.0, 0.0)
    earlier = lax.broadcasted_iota(jnp.int32, (CELLS, CELLS), 0) < lax.broadcasted_iota(jnp.int32, (CELLS, CELLS), 1)
    earlier = jnp.where(earlier, 1.0, 0.0).astype(BF16)
    ahead = jnp.dot(own_f.astype(BF16), earlier, preferred_element_type=F32)
    place = jnp.sum(own_f * ahead, axis=0, keepdims=True).astype(jnp.int32)
    cell = lax.broadcasted_iota(jnp.int32, (1, CELLS), 1)
    goes = jnp.where(cell < counts[NXD * z + x], owner * CAP + place, -1)
    for p in range(ZP):
        marks[p * ROWS : (p + 1) * ROWS] = labels[p]
    marks[ZP * ROWS :] = jnp.broadcast_to(goes, (8, CELLS))

    out_row = lax.broadcasted_iota(jnp.int32, (CH, CH), 0)
    in_row = lax.broadcasted_iota(jnp.int32, (CH, CH), 1)
    order = jnp.where(in_row == (out_row % NR) * COLOUR + out_row // NR, 1.0, 0.0).astype(BF16)
    wide = jnp.dot(order, codebook[...], preferred_element_type=F32) * (SOFTMAX_HEAT * LOG2E)
    flat = jnp.concatenate([wide, jnp.zeros((CH, GP - GENES), F32)], axis=1).T
    hi = flat.astype(BF16)
    mid = (flat - hi.astype(F32)).astype(BF16)
    lo = (flat - hi.astype(F32) - mid.astype(F32)).astype(BF16)
    gene = lax.broadcasted_iota(jnp.int32, (GP, 16), 0)
    which = lax.broadcasted_iota(jnp.int32, (GP, 16), 1)
    shut = jnp.where((gene >= GENES) & (which == 0), -3.0e38, 0.0).astype(BF16)
    cbt[...] = jnp.concatenate([hi, mid, lo, shut], axis=1)

    tile = NXD * r + x
    source = lax.broadcasted_iota(jnp.int32, (WIDE, HALF), 0)
    target = lax.broadcasted_iota(jnp.int32, (WIDE, HALF), 1)
    e = source - HALF
    side = e % 4
    beyond = jnp.where(side < 2, side - 2, HALF - 2 + side)
    at = jnp.where(source < HALF, source, jnp.where(e < 4 * PAIRS, beyond, 4 * WIDE))
    gap = jnp.abs(at - target)
    once = jnp.where(gap == 1, 1.0, 0.0).astype(BF16)
    for half in range(2):
        outer = (tile == TILES - 1) if half else (tile == 0)
        edge = jnp.where(at == (HALF - 1 if half else 0), jnp.where(outer, 1.0, 0.0), 0.0)
        bands[half, :, :HALF] = once
        bands[half, :, HALF:] = jnp.where(gap == 2, 1.0, jnp.where(gap == 0, 2.0 - edge, 0.0)).astype(BF16)


def prepare(labels, owners, counts, codebook):
    return pl.pallas_call(
        prepare_kernel,
        in_specs=[VMEM, VMEM, SMEM, VMEM],
        out_specs=[VMEM] * 3,
        out_shape=[
            jax.ShapeDtypeStruct((MARKS, CELLS), jnp.int32),
            jax.ShapeDtypeStruct((GP, 3 * CH + 16), BF16),
            jax.ShapeDtypeStruct((2, WIDE, 2 * HALF), BF16),
        ],
        compiler_params=params(16),
        cost_estimate=cost(2),
        name="prepare",
    )(labels, owners, counts, codebook)


def transposed_rows(src, rows, store):
    lane = lax.broadcasted_iota(jnp.int32, (CH, 128), 1)
    colour = lax.broadcasted_iota(jnp.int32, (CH, 128), 0) // NR

    def swapped(i):
        return jnp.swapaxes(jnp.stack([src(r, i) for r in range(NR)]).astype(F32), 0, 1)

    edge = swapped(PAIRS)
    for p in range(ZP):
        parts = [swapped(ZP * c + p) for c in range(COLOUR)]
        mask = (lane // 4) == colour * ZP + p
        for row in rows:
            store(row, p, 0, jnp.concatenate([part[row] for part in parts], axis=0).astype(BF16))
            border = jnp.concatenate([edge[row]] * COLOUR, axis=0)
            store(row, p, 1, jnp.where(mask, border, 0.0).astype(BF16))


def normalise(value):
    mean = jnp.sum(value * value, axis=0, keepdims=True) * (1.0 / CH)
    return (value * lax.rsqrt(mean + 49.0 * NOISE_LEVEL)).astype(BF16)


def vertical(first, second, third):
    return 6.0 * second - (first + third)


def stencil_kernel(half, g, bands, unit, last, xt, y, a_s, b_s):
    def regroup(k, _):
        base = k * 8 * STEP

        def store(row, p, t, block):
            start = pl.multiple_of(base + (row * ZP + p) * CH, 16)
            xt[pl.ds(start, CH), t * 128 : (t + 1) * 128] = block

        transposed_rows(lambda r, i: g[k * NR + r, i], range(8), store)
        at = pl.ds(pl.multiple_of(base, 16), 8 * STEP)
        y[at, :] = jnp.dot(xt[at, :], bands[half], preferred_element_type=F32)
        return 0

    lax.fori_loop(0, ROWS // 8, regroup, 0)
    last[...] = xt[(ROWS - 4) * STEP :]

    def raw(row, p):
        return xt[pl.ds(pl.multiple_of(row * STEP + p * CH, 16), CH), :HALF].astype(F32)

    def cols(row, p, twice):
        return y[pl.ds(pl.multiple_of(row * STEP + p * CH, 16), CH), twice * HALF : (twice + 1) * HALF]

    def first(row, _):
        here = [raw(row, p) for p in range(ZP)]
        for p in range(ZP):
            cx = cols(row, p, 0)
            a = vertical(raw(row - 1, p), here[p], raw(row + 1, p)) - here[1 - p] - cx
            a_s[row, p] = a
            b_s[row, p] = a - cx
        return 0

    lax.fori_loop(1, ROWS - 1, first, 0)

    def second(k, _):
        for odd in range(2):
            row = 2 * k + odd
            mid = [b_s[row, p] for p in range(ZP)]
            for p in range(ZP):
                mb = vertical(b_s[row - 1, p], mid[p], b_s[row + 1, p]) - mid[1 - p]
                at = (odd * ZP + p) * HALF
                unit[k, :, at : at + HALF] = normalise(a_s[row, p] + SHARPEN * (mb + cols(row, p, 1)))
        return 0

    lax.fori_loop(1, ROWS // 2 - 1, second, 0)


def stencil(g, bands, half):
    return pl.pallas_call(
        functools.partial(stencil_kernel, half),
        in_specs=[VMEM] * 2,
        out_specs=[VMEM] * 2,
        out_shape=[
            jax.ShapeDtypeStruct((ROWS // 2, CH, VOX), BF16),
            jax.ShapeDtypeStruct((4 * STEP, WIDE), BF16),
        ],
        scratch_shapes=[
            pltpu.VMEM((ROWS * STEP, WIDE), BF16),
            pltpu.VMEM((ROWS * STEP, 2 * HALF), F32),
            pltpu.VMEM((ROWS, ZP, CH, HALF), F32),
            pltpu.VMEM((ROWS, ZP, CH, HALF), F32),
        ],
        compiler_params=params(24),
        cost_estimate=cost(4),
        name="stencil_half",
    )(g, bands)


def no_maximum_needed(codebook):
    wide = codebook[...].astype(F32)
    longest = jnp.max(jnp.sum(wide * wide, axis=0, keepdims=True))
    return longest * (CH * (1.01 * SOFTMAX_HEAT * LOG2E) ** 2) <= SAFE * SAFE


def posteriors(fine, steps, take, mark, cbt, acc, e0, e1):
    slots = lax.broadcasted_iota(jnp.int32, (CELLS, VOX), 0)

    def logits_of(u):
        stacked = jnp.concatenate([u, u, u, jnp.ones((16, VOX), BF16)], axis=0)
        return jnp.dot(cbt[...], stacked, preferred_element_type=F32)

    def add(post, k):
        onehot = jnp.where(slots == mark(k), 1.0, 0.0).astype(BF16)
        acc[...] += lax.dot_general(post, onehot, NT, preferred_element_type=F32)

    def begin(k, e_s):
        e = jnp.exp2(logits_of(take(k)))
        e_s[...] = e
        return 1.0 / jnp.sum(e, axis=0, keepdims=True)

    def finish(inverse, k, e_s):
        add((e_s[...] * inverse).astype(BF16), k)

    @pl.when(fine)
    def _():
        def pair(k, inv):
            nxt = begin(2 * k + 1, e1)
            finish(inv, 2 * k, e0)
            inv = begin(2 * k + 2, e0)
            finish(nxt, 2 * k + 1, e1)
            return inv

        inv = lax.fori_loop(0, steps // 2 - 1, pair, begin(0, e0))
        nxt = begin(steps - 1, e1)
        finish(inv, steps - 2, e0)
        finish(nxt, steps - 1, e1)

    @pl.when(jnp.logical_not(fine))
    def _():
        def careful(k, _):
            logits = logits_of(take(k))
            e = jnp.exp2(logits - jnp.max(logits, axis=0, keepdims=True))
            add((e * (1.0 / jnp.sum(e, axis=0, keepdims=True))).astype(BF16), k)
            return 0

        lax.fori_loop(0, steps, careful, 0)


def label_row(marks, half, row):
    parts = [marks[pl.ds(p * ROWS + row + odd, 1), :] for odd in range(2) for p in range(ZP)]
    return jnp.concatenate([part[:, half * HALF : (half + 1) * HALF] for part in parts], axis=1)


def inner_kernel(half, unit, marks, cbt, codebook, *refs):
    if half:
        given, acc, e0, e1 = refs
        acc[...] = given[...]
    else:
        acc, tops, e0, e1 = refs
        acc[...] = jnp.zeros_like(acc)
        parts = [
            marks[p * ROWS + row : p * ROWS + row + 1, h * HALF : (h + 1) * HALF]
            for h in range(2)
            for row in range(2)
            for p in range(ZP)
        ]
        tops[...] = jnp.concatenate(parts, axis=0).astype(F32).astype(BF16)
    posteriors(
        no_maximum_needed(codebook),
        ROWS // 2 - 2,
        lambda k: unit[k + 1],
        lambda k: label_row(marks, half, 2 * k + 2),
        cbt, acc, e0, e1,
    )


def inner(unit, marks, cbt, codebook, half, *given):
    sums = jax.ShapeDtypeStruct((GP, CELLS), F32)
    return pl.pallas_call(
        functools.partial(inner_kernel, half),
        in_specs=[VMEM] * (4 + len(given)),
        out_specs=VMEM if half else [VMEM] * 2,
        out_shape=sums if half else [sums, jax.ShapeDtypeStruct((8, HALF), BF16)],
        scratch_shapes=[pltpu.VMEM((GP, VOX), F32)] * 2,
        compiler_params=params(24),
        cost_estimate=cost(7),
        name="posterior_half",
    )(unit, marks, cbt, codebook, *given)


def border_kernel(last0, last1, bands, following, marks, cbt, codebook, given, out, xh, ue, acc, e0, e1):
    joined = jnp.where(position()[0] < NZ - 1, 1.0, 0.0)
    blocks = NR * PIECE
    for half, last in enumerate((last0, last1)):
        xh[: 4 * STEP] = last[...]

        def store(row, p, t, block):
            start = (4 + row) * STEP + p * CH
            xh[start : start + CH, t * 128 : (t + 1) * 128] = block

        transposed_rows(lambda r, i: following[half * blocks + r * PIECE + i], range(4), store)
        y = jnp.dot(xh[STEP : 7 * STEP], bands[half], preferred_element_type=F32)

        def raw(row, p):
            return xh[row * STEP + p * CH : row * STEP + (p + 1) * CH, :HALF].astype(F32)

        def cols(row, p, twice):
            start = (row - 1) * STEP + p * CH
            return y[start : start + CH, twice * HALF : (twice + 1) * HALF]

        def up(get, row, p):
            return get(row - 1, p) * joined if row == 4 else get(row - 1, p)

        def down(get, row, p):
            return get(row + 1, p) * joined if row == 3 else get(row + 1, p)

        a, b = {}, {}
        for row in range(1, 7):
            for p in range(ZP):
                cx = cols(row, p, 0)
                a[row, p] = vertical(up(raw, row, p), raw(row, p), down(raw, row, p)) - raw(row, 1 - p) - cx
                b[row, p] = a[row, p] - cx

        def get_b(row, p):
            return b[row, p]

        for row in range(2, 6):
            for p in range(ZP):
                mb = vertical(up(get_b, row, p), b[row, p], down(get_b, row, p)) - b[row, 1 - p]
                at = ((row % 2) * ZP + p) * HALF
                ue[half * 2 + row // 2 - 1, :, at : at + HALF] = normalise(
                    a[row, p] + SHARPEN * (mb + cols(row, p, 1))
                )

    acc[...] = given[...]
    tops = [following[2 * blocks + h].astype(F32).astype(jnp.int32) for h in range(2)]

    def mark(k):
        own = [label_row(marks, h, ROWS - 2) for h in range(2)]
        next_ = [
            jnp.concatenate([tops[h][i : i + 1] for i in range(4)], axis=1) for h in range(2)
        ]
        return jnp.where(k < 2, jnp.where(k == 0, own[0], next_[0]), jnp.where(k == 2, own[1], next_[1]))

    posteriors(no_maximum_needed(codebook), 4, lambda k: ue[k], mark, cbt, acc, e0, e1)

    goes = marks[ZP * ROWS : ZP * ROWS + 1]
    select = jnp.where(lax.broadcasted_iota(jnp.int32, (TILES * CAP, CELLS), 0) == goes, SCALE, 0.0).astype(BF16)
    sums = jnp.concatenate([acc[...], jnp.zeros((128 * (FULL + 1) - GP, CELLS), F32)], axis=0)
    high = sums.astype(BF16)
    low = (sums - high.astype(F32)).astype(BF16)
    packed = lax.dot_general(select, high, NT, preferred_element_type=F32)
    packed = packed + lax.dot_general(select, low, NT, preferred_element_type=F32)
    lane = lax.broadcasted_iota(jnp.int32, (CAP // 2, 128), 1)
    for o in range(TILES):
        rows = packed[o * CAP : (o + 1) * CAP]
        for t in range(FULL):
            out[o, t * CAP : (t + 1) * CAP] = rows[:, t * 128 : (t + 1) * 128]
        rest = rows[:, FULL * 128 :]
        out[o, FULL * CAP :] = jnp.where(lane < 64, rest[: CAP // 2], pltpu.roll(rest[CAP // 2 :], 64, 1))


def border(last0, last1, bands, following, marks, cbt, codebook, given):
    return pl.pallas_call(
        border_kernel,
        in_specs=[VMEM] * 8,
        out_specs=VMEM,
        out_shape=jax.ShapeDtypeStruct((TILES, OUT_ROWS, 128), F32),
        scratch_shapes=[
            pltpu.VMEM((8 * STEP, WIDE), BF16),
            pltpu.VMEM((4, CH, VOX), BF16),
            pltpu.VMEM((GP, CELLS), F32),
            pltpu.VMEM((GP, VOX), F32),
            pltpu.VMEM((GP, VOX), F32),
        ],
        compiler_params=params(24),
        cost_estimate=cost(4),
        name="border_rows",
    )(last0, last1, bands, following, marks, cbt, codebook, given)


def unpack_kernel(parts, out):
    for x in range(NXD):
        for r in range(NR):
            src, dst = x * NR + r, NXD * r + x
            for t in range(FULL):
                out[0, dst, :, t * 128 : (t + 1) * 128] = parts[src, t * CAP : (t + 1) * CAP] * (1.0 / SCALE)
            rest = parts[src, FULL * CAP :] * (1.0 / SCALE)
            out[0, dst, : CAP // 2, FULL * 128 :] = rest[:, :REST]
            out[0, dst, CAP // 2 :, FULL * 128 :] = pltpu.roll(rest, 64, 1)[:, :REST]


def unpack(parts):
    return pl.pallas_call(
        unpack_kernel,
        in_specs=[VMEM],
        out_specs=VMEM,
        out_shape=jax.ShapeDtypeStruct((1, TILES, CAP, GENES), F32),
        compiler_params=params(16),
        name="unpack_cells",
    )(parts)


def local(images, labels, counts, owners, codebook):
    swap = [
        (z * NXD * NR + x * NR + r, r * NXD * NR + x * NR + z)
        for z in range(NZ)
        for x in range(NXD)
        for r in range(NR)
    ]
    plane = functools.partial(lax.all_to_all, axis_name=("x", "r"), split_axis=0, concat_axis=0, tiled=True)
    g0 = plane(pack(images, 0))
    g1 = plane(pack(images, 1))
    marks, cbt, bands = prepare(labels, owners.reshape(1, CELLS), counts, codebook)
    marks = lax.ppermute(marks, ("z", "x", "r"), swap)
    unit0, last0 = stencil(g0, bands, 0)
    acc, tops = inner(unit0, marks, cbt, codebook, 0)
    g1, acc, tops = lax.optimization_barrier((g1, acc, tops))
    upper = [g[:NR, :, :4].reshape(NR * PIECE, 4, 128) for g in (g0, g1)]
    upper = jnp.concatenate([*upper, tops.reshape(2, 4, HALF)], axis=0)
    following = lax.ppermute(upper, "z", [((i + 1) % NZ, i) for i in range(NZ)])
    unit1, last1 = stencil(g1, bands, 1)
    acc = inner(unit1, marks, cbt, codebook, 1, acc)
    packed = border(last0, last1, bands, following, marks, cbt, codebook, acc)
    packed = packed.astype(jnp.float16).reshape(NZ, NXD, OUT_ROWS, 128)
    parts = lax.all_to_all(packed, "z", split_axis=0, concat_axis=0, tiled=True)
    summed = jnp.sum(parts.astype(F32), axis=0).astype(jnp.float16)[:, None]
    spread = jnp.broadcast_to(summed, (NXD, NR, OUT_ROWS, 128)).reshape(NXD * NR, OUT_ROWS, 128)
    return unpack(plane(spread).astype(F32))


def solution(mesh):
    grid = Mesh(mesh.devices.reshape(NZ, NXD, NR), ("z", "x", "r"))
    in_specs = (P("r", None, ("z", "x"), None), P(None, "r", ("z", "x")), P(), P(("z", "x"), None), P())
    out_specs = P(("z", "x"), None, None, None)
    return jax.shard_map(local, mesh=grid, in_specs=in_specs, out_specs=out_specs, check_vma=False)
```

time: 483 us -> 117 us (0.24); the launches traced: 476 us -> 116 us
  local copies, waits for them, and re-layouts: 167 us -> 1.58 us
  blocking collectives: 118 us -> 41.3 us
  waiting for transfers between devices: 73.5 us -> 8.65 us
  Pallas kernels: 0 us -> 39.5 us
  other arithmetic: 39.7 us -> 0.41 us
  matrix products: 37.3 us -> 0 us
  between operations: 13.7 us -> 0.23 us
  loops' own time: 5.67 us -> 0 us
    unnamed x24 -> x12, local copies, waits for them, and re-layouts: 95.3 us -> 1.44 us
    all_to_all x3 -> x2, blocking collectives: 118 us -> 41.3 us  [the longest x1 21.2 us: local(): parts = lax.all_to_all(packed, 'z', split_axis=0, concat_axis=0, tiled=True)]
    psum x1 -> x0, waiting for transfers between devices: 66.1 us -> none  [local(): summed = lax.psum(partial_value, 'round')]
    pallas_call x0 -> x9, Pallas kernels: none -> 39.5 us  [the longest x2 22.8 us: inner(): pl.pallas_call(functools.partial(inner_kernel, half), in_specs=[VMEM] * (...]
    dot_general x17 -> x0, matrix products: 37.3 us -> none  [the longest x8 29 us: step(): jnp.dot(onehot, posterior, preferred_element_type=jnp.float32)]
    all_to_all x3 -> x0, local copies, waits for them, and re-layouts: 34.3 us -> none  [the longest x1 34 us: local(): lax.all_to_all(images, 'tile', split_axis=3, concat_axis=2, tiled=True)]
    while x16 -> x0, local copies, waits for them, and re-layouts: 16.2 us -> none
    reduce_sum x11 -> x1, other arithmetic: 15.7 us -> 0.08 us  [local(): summed = jnp.sum(parts.astype(F32), axis=0).astype(jnp.float16)[:, None]]
  transfers between devices with their start and end apart: 9 -> 4, of which waited for: 5 -> 2; matrix products, arithmetic and copies ran while one was open for 2% -> 0% of each run, Pallas kernels for 0% -> 25%
where the time goes in v3:
time: 117 us; the launch traced here: 116 us
  blocking collectives  41.3 us (35%)
  Pallas kernels  39.5 us (34%)
  starting transfers between devices  24.5 us (21%)
  waiting for transfers between devices  8.65 us (7%)
  local copies, waits for them, and re-layouts  1.58 us (1%)
    pallas_call x2, Pallas kernels, inner(): pl.pallas_call(functools.partial(inner_kernel, half), in_specs=[VMEM] * (...  22.8 us
    all_to_all x1, blocking collectives, local(): parts = lax.all_to_all(packed, 'z', split_axis=0, concat_axis=0, tiled=True)  21.2 us
    all_to_all x1, blocking collectives, local(): return unpack(plane(spread).astype(F32))  20.1 us
    all_to_all x1, starting transfers between devices, local(): g0 = plane(pack(images, 0))  8.73 us
    all_to_all x1, waiting for transfers between devices, local(): g0 = plane(pack(images, 0))  8.17 us
    all_to_all x1, starting transfers between devices, local(): g1 = plane(pack(images, 1))  6.41 us
    pallas_call x2, Pallas kernels, stencil(): pl.pallas_call(functools.partial(stencil_kernel, half), in_specs=[VMEM] *...  5.97 us
    ppermute x1, starting transfers between devices, local(): following = lax.ppermute(upper, 'z', [((i + 1) % NZ, i) for i in range(NZ)])  5.73 us
  transfers between devices with their start and end apart: 4, of which 2 were waited for; matrix products, arithmetic and copies ran while one was open for 0% of the time, Pallas kernels for 25%

profile of v3, /device:TPU:1, one launch (start us, length us, event | category | flops | bytes accessed | tf_op | source)
XLA Modules:
  0.0 116.1 jit_solution(17503760949462779728)
XLA Ops:
  0.0 1.4 %copy-done = bf16[6,2,8,8192]{3,2,1,0:T(8,128)(2,1)S(1)} copy-done((bf16[6,2,8,8192]{3,2,1,0:T(8,128)(2,1)S(1)}, bf16[6,2,8,8192]{3,2,1,0:T(8,128)(2,1)}, u32[]{:S(2)}) %copy-start) | copy-done | bytes 1572888
  1.4 2.0 %pack_half.2 = bf16[32,13,8,128]{3,2,1,0:T(8,128)(2,1)} custom-call(bf16[6,2,8,8192]{3,2,1,0:T(8,128)(2,1)S(1)} %copy-done), custom_call_target="tpu_custom_call" | custom-call | flops 2000000000 | bytes 6000000 | tf_op jit(solution)/shard_map/pack_half/pallas_call | solution.py:97
  3.4 0.0 copy-start.2
  3.4 0.0 copy-start.3
  3.5 0.0 copy-start.4
  3.5 0.0 copy-start.5
  3.5 8.7 %all-to-all-start = ((bf16[32,13,8,128]{3,2,1,0:T(8,128)(2,1)}), bf16[32,13,8,128]{3,2,1,0:T(8,128)(2,1)S(1)}, u32[]{:S(2)}, u32[]{:S(2)}) async-start(bf16[32,13,8,128]{3,2,1,0:T(8,128)(2,1)} %pack_half.2), calls=%async_computation | async-start | bytes 1703936 | tf_op jit(solution)/shard_map/all_to_all | solution.py:475
  12.2 0.0 copy-done.2
  12.2 0.0 copy-done.3
  12.3 0.0 copy-start.1
  12.3 0.9 prepare.1
  13.2 3.7 %collective-permute-start = (s32[72,256]{1,0:T(8,128)S(1)}, s32[72,256]{1,0:T(8,128)S(1)}, u32[]{:S(2)}, u32[]{:S(2)}) collective-permute-start(s32[72,256]{1,0:T(8,128)S(1)} %get-tuple-element.20), channel_id=1, source_target_pairs={{0,0},{1,32},{2,64},{3,96},{4,128},{5,160},{6,192},{7,224},{8,8},{... | collective-permute-start | bytes 221192 | tf_op jit(solution)/shard_map/ppermute | solution.py:478
  16.9 2.0 %pack_half.3 = bf16[32,13,8,128]{3,2,1,0:T(8,128)(2,1)} custom-call(bf16[6,2,8,8192]{3,2,1,0:T(8,128)(2,1)S(1)} %copy-done.1), custom_call_target="tpu_custom_call" | custom-call | flops 2000000000 | bytes 6000000 | tf_op jit(solution)/shard_map/pack_half/pallas_call | solution.py:97
  18.9 8.2 %all-to-all-done.g = bf16[32,13,8,128]{3,2,1,0:T(8,128)(2,1)S(1)} async-done(((bf16[32,13,8,128]{3,2,1,0:T(8,128)(2,1)}), bf16[32,13,8,128]{3,2,1,0:T(8,128)(2,1)S(1)}, u32[]{:S(2)}, u32[]{:S(2)}) %all-to-all-start) | async-done | bytes 852000 | tf_op jit(solution)/shard_map/all_to_all | solution.py:475
  27.1 6.4 %all-to-all-start.1 = ((bf16[32,13,8,128]{3,2,1,0:T(8,128)(2,1)}), bf16[32,13,8,128]{3,2,1,0:T(8,128)(2,1)S(1)}, u32[]{:S(2)}, u32[]{:S(2)}) async-start(bf16[32,13,8,128]{3,2,1,0:T(8,128)(2,1)} %pack_half.3), calls=%async_computation.1 | async-start | bytes 1703936 | tf_op jit(solution)/shard_map/all_to_all | solution.py:476
  33.5 3.0 %stencil_half.2 = (bf16[16,48,512]{2,1,0:T(8,128)(2,1)S(1)}, bf16[384,256]{1,0:T(8,128)(2,1)S(1)}) custom-call(bf16[32,13,8,128]{3,2,1,0:T(8,128)(2,1)S(1)} %all-to-all-done.g, bf16[2,256,256]{2,1,0:T(8,128)(2,1)S(1)} %get-tuple-element.17.bands), custom_call_target="tpu_custom_call" | custom-call | flops 4000000000 | bytes 12000000 | tf_op jit(solution)/shard_map/stencil_half/pallas_call | solution.py:242
  36.5 0.0 collective-permute-done.marks
  36.5 11.4 %posterior_half.2 = (f32[552,256]{1,0:T(8,128)S(1)}, bf16[8,128]{1,0:T(8,128)(2,1)S(1)}) custom-call(bf16[16,48,512]{2,1,0:T(8,128)(2,1)S(1)} %get-tuple-element.19.unit, s32[72,256]{1,0:T(8,128)S(1)} %collective-permute-done.marks, bf16[552,160]{1,0:T(8,128)(2,1)S(1)} %get-tuple-element.21.cbt, bf16[48,550]{1,0:T(8,128)(2,1)S(1)} %copy-done.3), custom_call_target="tpu_custom_call" | custom-call | flops 7000000000 | bytes 21000000 | tf_op jit(solution)/shard_map/posterior_half/pallas_call | solution.py:342
  47.9 0.5 all-to-all-done.1.g
  48.4 3.0 %stencil_half.3 = (bf16[16,48,512]{2,1,0:T(8,128)(2,1)S(1)}, bf16[384,256]{1,0:T(8,128)(2,1)S(1)}) custom-call(bf16[32,13,8,128]{3,2,1,0:T(8,128)(2,1)S(1)} %all-to-all-done.1.g, bf16[2,256,256]{2,1,0:T(8,128)(2,1)S(1)} %get-tuple-element.17.bands), custom_call_target="tpu_custom_call" | custom-call | flops 4000000000 | bytes 12000000 | tf_op jit(solution)/shard_map/stencil_half/pallas_call | solution.py:242
  51.4 0.2 pad_maximum_fusion
  51.6 5.7 %collective-permute-start.1 = (bf16[210,4,128]{2,1,0:T(4,128)(2,1)S(1)}, bf16[210,4,128]{2,1,0:T(4,128)(2,1)S(1)}, u32[]{:S(2)}, u32[]{:S(2)}) collective-permute-start(bf16[210,4,128]{2,1,0:T(4,128)(2,1)S(1)} %pad_maximum_fusion), channel_id=1, source_target_pairs={{32,0},{64,32},{96,64},{128,96},{160,128},{192,160},{224,192},{0,2... | collective-permute-start | bytes 645128 | tf_op jit(solution)/shard_map/ppermute | solution.py:484
  57.3 11.4 %posterior_half.3.given = f32[552,256]{1,0:T(8,128)S(1)} custom-call(bf16[16,48,512]{2,1,0:T(8,128)(2,1)S(1)} %get-tuple-element.27.unit, s32[72,256]{1,0:T(8,128)S(1)} %collective-permute-done.marks, bf16[552,160]{1,0:T(8,128)(2,1)S(1)} %get-tuple-element.21.cbt, bf16[48,550]{1,0:T(8,128)(2,1)S(1)} %copy-done.3, f32[552,256]{1,0:T(8,128)S(1)} %get-tuple-element.28.refs_0_), custom_call_target="tpu_custom_call" | custom-call | flops 7000000000 | bytes 21000000 | tf_op jit(solution)/shard_map/posterior_half/pallas_call | solution.py:342
  68.7 0.0 collective-permute-done.1.following
  68.8 4.6 %border_rows.1 = f32[32,72,128]{2,1,0:T(8,128)S(1)} custom-call(bf16[384,256]{1,0:T(8,128)(2,1)S(1)} %get-tuple-element.18.last0, bf16[384,256]{1,0:T(8,128)(2,1)S(1)} %get-tuple-element.25.last1, bf16[2,256,256]{2,1,0:T(8,128)(2,1)S(1)} %get-tuple-element.17.bands, bf16[210,4,128]{2,1,0:T(4,128)(2,1)S(1)} %collective-permute-done.1.following, ...), custom_call_target="tpu_custom_call" | custom-call | flops 4000000000 | bytes 12000000 | tf_op jit(solution)/shard_map/border_rows/pallas_call | solution.py:427
  73.3 0.1 convert_element_type.16
  73.4 21.2 %all_to_all.20 = f16[8,4,72,128]{3,2,1,0:T(8,128)(2,1)S(1)} all-to-all(f16[8,4,72,128]{3,2,1,0:T(8,128)(2,1)S(1)} %bitcast.8), channel_id=1, replica_groups=mesh['z'=8,'x'=4,'r'=8] {'z'}, dimensions={0} | all-to-all | bytes 1179648 | tf_op jit(solution)/shard_map/all_to_all | solution.py:489
  94.6 0.1 convert_reduce_fusion
  94.7 0.1 broadcast_in_dim.2
  94.8 20.1 %all_to_all.21 = f16[32,72,128]{2,1,0:T(8,128)(2,1)S(1)} all-to-all(f16[32,72,128]{2,1,0:T(8,128)(2,1)S(1)} %bitcast.9), channel_id=1, replica_groups=mesh['z'=8,'x'=4,'r'=8] {'x','r'}, dimensions={0} | all-to-all | bytes 1179648 | tf_op jit(solution)/shard_map/all_to_all | solution.py:492
  114.9 0.1 convert_element_type.19.parts
  115.0 1.2 %unpack_cells.1 = f32[1,32,16,550]{3,2,1,0:T(8,128)} custom-call(f32[32,72,128]{2,1,0:T(8,128)S(1)} %convert_element_type.19.parts), custom_call_target="tpu_custom_call" | custom-call | tf_op jit(solution)/shard_map/unpack_cells/pallas_call | solution.py:457
  (7 shorter events, 0.1 us)
Async XLA Ops:
  0.0 1.4 %copy-start = (bf16[6,2,8,8192]{3,2,1,0:T(8,128)(2,1)S(1)}, bf16[6,2,8,8192]{3,2,1,0:T(8,128)(2,1)}, u32[]{:S(2)}) copy-start(bf16[6,2,8,8192]{3,2,1,0:T(8,128)(2,1)} %img.3) | copy-start | bytes 4718596
  3.4 8.8 %copy-start.2 = (s32[2,32,256]{2,1,0:T(8,128)S(1)}, s32[2,32,256]{2,1,0:T(8,128)}, u32[]{:S(2)}) copy-start(s32[2,32,256]{2,1,0:T(8,128)} %labels.1) | copy-start | bytes 196612
  3.4 8.8 %copy-start.3 = (bf16[48,550]{1,0:T(8,128)(2,1)S(1)}, bf16[48,550]{1,0:T(8,128)(2,1)}, u32[]{:S(2)}) copy-start(bf16[48,550]{1,0:T(8,128)(2,1)} %codebook.7) | copy-start | bytes 158404
  3.5 8.8 %copy-start.4 = (s32[256,1]{0,1:T(1,128)S(1)}, s32[256,1]{0,1:T(1,128)}, u32[]{:S(2)}) copy-start(s32[256,1]{0,1:T(1,128)} %param.8) | copy-start | bytes 3076
  3.5 8.8 %copy-start.5 = (s32[32]{0:T(128)S(1)}, s32[32]{0:T(128)}, u32[]{:S(2)}) copy-start(s32[32]{0:T(128)} %counts.1) | copy-start | bytes 388
  3.5 23.6 %all-to-all-start = ((bf16[32,13,8,128]{3,2,1,0:T(8,128)(2,1)}), bf16[32,13,8,128]{3,2,1,0:T(8,128)(2,1)S(1)}, u32[]{:S(2)}, u32[]{:S(2)}) async-start(bf16[32,13,8,128]{3,2,1,0:T(8,128)(2,1)} %pack_half.2), calls=%async_computation | async-start | bytes 1703936 | tf_op jit(solution)/shard_map/all_to_all | solution.py:475
  12.3 4.6 %copy-start.1 = (bf16[6,2,8,8192]{3,2,1,0:T(8,128)(2,1)S(1)}, bf16[6,2,8,8192]{3,2,1,0:T(8,128)(2,1)}, u32[]{:S(2)}) copy-start(bf16[6,2,8,8192]{3,2,1,0:T(8,128)(2,1)} %img.3) | copy-start | bytes 4718596
  13.2 23.3 %collective-permute-start = (s32[72,256]{1,0:T(8,128)S(1)}, s32[72,256]{1,0:T(8,128)S(1)}, u32[]{:S(2)}, u32[]{:S(2)}) collective-permute-start(s32[72,256]{1,0:T(8,128)S(1)} %get-tuple-element.20), channel_id=1, source_target_pairs={{0,0},{1,32},{2,64},{3,96},{4,128},{5,160},{6,192},{7,224},{8,8},{... | collective-permute-start | bytes 221192 | tf_op jit(solution)/shard_map/ppermute | solution.py:478
  27.1 21.3 %all-to-all-start.1 = ((bf16[32,13,8,128]{3,2,1,0:T(8,128)(2,1)}), bf16[32,13,8,128]{3,2,1,0:T(8,128)(2,1)S(1)}, u32[]{:S(2)}, u32[]{:S(2)}) async-start(bf16[32,13,8,128]{3,2,1,0:T(8,128)(2,1)} %pack_half.3), calls=%async_computation.1 | async-start | bytes 1703936 | tf_op jit(solution)/shard_map/all_to_all | solution.py:476
  51.6 17.2 %collective-permute-start.1 = (bf16[210,4,128]{2,1,0:T(4,128)(2,1)S(1)}, bf16[210,4,128]{2,1,0:T(4,128)(2,1)S(1)}, u32[]{:S(2)}, u32[]{:S(2)}) collective-permute-start(bf16[210,4,128]{2,1,0:T(4,128)(2,1)S(1)} %pad_maximum_fusion), channel_id=1, source_target_pairs={{32,0},{64,32},{96,64},{128,96},{160,128},{192,160},{224,192},{0,2... | collective-permute-start | bytes 645128 | tf_op jit(solution)/shard_map/ppermute | solution.py:484

commit v4 on v3

--- a/solution.py
+++ b/solution.py
@@ -48,62 +48,61 @@
     return pl.CostEstimate(flops=int(us * 1e9), bytes_accessed=int(us * 3e6), transcendentals=0)
 
 
-def pack_kernel(half, img, out, buf, sems):
+def pack_kernel(img, out, buf, sems):
     lane = lax.broadcasted_iota(jnp.int32, (8, 128), 1)
     windows = [(lane // 4) == i for i in range(PAIRS)]
+    width = NXD * PT
 
     def fetch(r):
-        start = pl.multiple_of(r * (NXD * PT), NXD * PT)
-        return pltpu.make_async_copy(img.at[:, :, :, pl.ds(start, NXD * PT)], buf.at[r], sems.at[r])
+        start = pl.multiple_of(r * width, width)
+        return pltpu.make_async_copy(img.at[:, :, :, pl.ds(start, width)], buf.at[r], sems.at[r])
 
     for r in range(NR):
         fetch(r).start()
-    if half:
-        fetch(0).wait()
+    fetch(0).wait()
 
     def column(r, _):
-        if half:
-
-            @pl.when(r < NR - 1)
-            def _():
-                fetch(jnp.minimum(r + 1, NR - 1)).wait()
-        else:
-            fetch(r).wait()
-        near = jnp.minimum(r + 1, NR - 1) if half else jnp.maximum(r - 1, 0)
-        inside = ((r < NR - 1) if half else (r > 0)).astype(F32)
+        after, before = jnp.minimum(r + 1, NR - 1), jnp.maximum(r - 1, 0)
+
+        @pl.when(r < NR - 1)
+        def _():
+            fetch(after).wait()
+
+        has_after, has_before = (r < NR - 1).astype(F32), (r > 0).astype(F32)
         for x in range(NXD):
-            at = PT * x + HALF * half
-            border = jnp.zeros((8, 128), F32)
-            for i in range(PAIRS):
-                c, p = i // ZP, i % ZP
-                out[x * NR + r, i] = buf[r, c, p, :, at : at + HALF]
-                if at + HALF < NXD * PT:
-                    right = buf[r, c, p, :, at + HALF : at + 2 * HALF].astype(F32)
-                else:
-                    right = buf[near, c, p, :, :128].astype(F32) * inside
-                if at > 0:
-                    left = buf[r, c, p, :, at - 128 : at].astype(F32)
-                else:
-                    left = buf[near, c, p, :, NXD * PT - 128 :].astype(F32) * inside
-                both = pltpu.roll(jnp.where(lane < 64, right, left), 4 * i + 2, 1)
-                border = jnp.where(windows[i], both, border)
-            out[x * NR + r, PAIRS] = border.astype(BF16)
+            for half in range(2):
+                at = PT * x + HALF * half
+                border = jnp.zeros((8, 128), F32)
+                for i in range(PAIRS):
+                    c, p = i // ZP, i % ZP
+                    out[x * NR + r, half * PIECE + i] = buf[r, c, p, :, at : at + HALF]
+                    if at + HALF < width:
+                        right = buf[r, c, p, :, at + HALF : at + 2 * HALF].astype(F32)
+                    else:
+                        right = buf[after, c, p, :, :128].astype(F32) * has_after
+                    if at > 0:
+                        left = buf[r, c, p, :, at - 128 : at].astype(F32)
+                    else:
+                        left = buf[before, c, p, :, width - 128 :].astype(F32) * has_before
+                    both = pltpu.roll(jnp.where(lane < 64, right, left), 4 * i + 2, 1)
+                    border = jnp.where(windows[i], both, border)
+                out[x * NR + r, half * PIECE + PAIRS] = border.astype(BF16)
         return 0
 
     lax.fori_loop(0, NR, column, 0)
 
 
-def pack(images, half):
+def pack(images):
     return pl.pallas_call(
-        functools.partial(pack_kernel, half),
+        pack_kernel,
         in_specs=[pl.BlockSpec(memory_space=pltpu.HBM)],
         out_specs=VMEM,
-        out_shape=jax.ShapeDtypeStruct((NXD * NR, PIECE, 8, 128), BF16),
+        out_shape=jax.ShapeDtypeStruct((NXD * NR, 2 * PIECE, 8, 128), BF16),
         scratch_shapes=[pltpu.VMEM((NR, COLOUR, ZP, 8, NXD * PT), BF16), pltpu.SemaphoreType.DMA((NR,))],
         compiler_params=params(16),
         cost_estimate=cost(2),
-        name="pack_half",
-    )(images)
+        name="pack_pieces",
+    )(pltpu.with_memory_space_constraint(images, pltpu.HBM))
 
 
 def prepare_kernel(labels, owners, counts, codebook, marks, cbt, bands):
@@ -192,21 +191,20 @@
     return 6.0 * second - (first + third)
 
 
-def stencil_kernel(half, g, bands, unit, last, xt, y, a_s, b_s):
-    def regroup(k, _):
+def stencil_steps(half, g, bands, unit, last, xt, y, a_s, b_s):
+    def regroup(k):
         base = k * 8 * STEP
 
         def store(row, p, t, block):
             start = pl.multiple_of(base + (row * ZP + p) * CH, 16)
             xt[pl.ds(start, CH), t * 128 : (t + 1) * 128] = block
 
-        transposed_rows(lambda r, i: g[k * NR + r, i], range(8), store)
+        transposed_rows(lambda r, i: g[k * NR + r, half * PIECE + i], range(8), store)
         at = pl.ds(pl.multiple_of(base, 16), 8 * STEP)
         y[at, :] = jnp.dot(xt[at, :], bands[half], preferred_element_type=F32)
-        return 0
-
-    lax.fori_loop(0, ROWS // 8, regroup, 0)
-    last[...] = xt[(ROWS - 4) * STEP :]
+
+    def keep():
+        last[half] = xt[(ROWS - 4) * STEP :]
 
     def raw(row, p):
         return xt[pl.ds(pl.multiple_of(row * STEP + p * CH, 16), CH), :HALF].astype(F32)
@@ -214,18 +212,15 @@
     def cols(row, p, twice):
         return y[pl.ds(pl.multiple_of(row * STEP + p * CH, 16), CH), twice * HALF : (twice + 1) * HALF]
 
-    def first(row, _):
+    def first(row):
         here = [raw(row, p) for p in range(ZP)]
         for p in range(ZP):
             cx = cols(row, p, 0)
             a = vertical(raw(row - 1, p), here[p], raw(row + 1, p)) - here[1 - p] - cx
             a_s[row, p] = a
             b_s[row, p] = a - cx
-        return 0
-
-    lax.fori_loop(1, ROWS - 1, first, 0)
-
-    def second(k, _):
+
+    def second(k):
         for odd in range(2):
             row = 2 * k + odd
             mid = [b_s[row, p] for p in range(ZP)]
@@ -233,135 +228,148 @@
                 mb = vertical(b_s[row - 1, p], mid[p], b_s[row + 1, p]) - mid[1 - p]
                 at = (odd * ZP + p) * HALF
                 unit[k, :, at : at + HALF] = normalise(a_s[row, p] + SHARPEN * (mb + cols(row, p, 1)))
+
+    return regroup, keep, first, second
+
+
+def loop(low, high, step):
+    def body(k, _):
+        step(k)
         return 0
 
-    lax.fori_loop(1, ROWS // 2 - 1, second, 0)
-
-
-def stencil(g, bands, half):
+    lax.fori_loop(low, high, body, 0)
+
+
+def no_maximum_needed(codebook):
+    wide = codebook[...].astype(F32)
+    longest = jnp.max(jnp.sum(wide * wide, axis=0, keepdims=True))
+    return longest * (CH * (1.01 * SOFTMAX_HEAT * LOG2E) ** 2) <= SAFE * SAFE
+
+
+def posterior_steps(cbt, acc):
+    slots = lax.broadcasted_iota(jnp.int32, (CELLS, VOX), 0).astype(F32).astype(BF16)
+
+    def logits_of(u):
+        stacked = jnp.concatenate([u, u, u, jnp.ones((16, VOX), BF16)], axis=0)
+        return jnp.dot(cbt[...], stacked, preferred_element_type=F32)
+
+    def add(post, label):
+        onehot = jnp.where(slots == label.astype(F32).astype(BF16), jnp.ones((), BF16), jnp.zeros((), BF16))
+        acc[...] += lax.dot_general(post, onehot, NT, preferred_element_type=F32)
+
+    def begin(u, e_s):
+        e = jnp.exp2(logits_of(u))
+        e_s[...] = e
+        return 1.0 / jnp.sum(e, axis=0, keepdims=True)
+
+    def finish(inverse, label, e_s):
+        add((e_s[...] * inverse).astype(BF16), label)
+
+    def careful(u, label):
+        logits = logits_of(u)
+        e = jnp.exp2(logits - jnp.max(logits, axis=0, keepdims=True))
+        add((e * (1.0 / jnp.sum(e, axis=0, keepdims=True))).astype(BF16), label)
+
+    return begin, finish, careful
+
+
+def label_row(marks, half, row):
+    parts = [marks[pl.ds(p * ROWS + row + odd, 1), :] for odd in range(2) for p in range(ZP)]
+    return jnp.concatenate([part[:, half * HALF : (half + 1) * HALF] for part in parts], axis=1)
+
+
+def decode_kernel(g, bands, marks, cbt, codebook, acc, last, xt, y, a_s, b_s, unit0, unit1, e0, e1):
+    units = (unit0, unit1)
+    acc[...] = jnp.zeros_like(acc)
+    begin, finish, careful = posterior_steps(cbt, acc)
+
+    def label(half, k):
+        return label_row(marks, half, 2 * k)
+
+    regroup, keep, first, second = stencil_steps(0, g, bands, unit0, last, xt, y, a_s, b_s)
+    loop(0, ROWS // 8, regroup)
+    keep()
+    loop(1, ROWS - 1, first)
+    loop(1, ROWS // 2 - 1, second)
+    regroup, keep, first, second = stencil_steps(1, g, bands, unit1, last, xt, y, a_s, b_s)
+    fine = no_maximum_needed(codebook)
+
+    @pl.when(fine)
+    def _():
+        def pair(half, k, inv, following):
+            unit = units[half]
+            nxt = begin(unit[k + 1], e1)
+            finish(inv, label(half, k), e0)
+            inv = begin(following, e0)
+            finish(nxt, label(half, k + 1), e1)
+            return inv
+
+        def with_regroup(i, inv):
+            regroup(i)
+            return pair(0, 2 * i + 1, inv, unit0[2 * i + 3])
+
+        def with_rows(i, inv):
+            for j in range(10):
+                first(10 * i + j + 1)
+            for j in range(5):
+                second(5 * i + j)
+            return pair(0, 2 * i + 9, inv, unit0[2 * i + 11] if not isinstance(i, int) else unit1[1])
+
+        inv = lax.fori_loop(0, ROWS // 8, with_regroup, begin(unit0[1], e0))
+        keep()
+        inv = lax.fori_loop(0, 2, with_rows, inv)
+        inv = with_rows(2, inv)
+        inv = lax.fori_loop(0, 6, lambda i, inv: pair(1, 2 * i + 1, inv, unit1[2 * i + 3]), inv)
+        nxt = begin(unit1[14], e1)
+        finish(inv, label(1, 13), e0)
+        finish(nxt, label(1, 14), e1)
+
+    @pl.when(jnp.logical_not(fine))
+    def _():
+        loop(0, ROWS // 8, regroup)
+        keep()
+        loop(1, ROWS - 1, first)
+        loop(1, ROWS // 2 - 1, second)
+        for half in range(2):
+            loop(1, ROWS // 2 - 1, lambda k: careful(units[half][k], label(half, k)))
+
+
+def decode(g, bands, marks, cbt, codebook):
     return pl.pallas_call(
-        functools.partial(stencil_kernel, half),
-        in_specs=[VMEM] * 2,
+        decode_kernel,
+        in_specs=[VMEM] * 5,
         out_specs=[VMEM] * 2,
         out_shape=[
-            jax.ShapeDtypeStruct((ROWS // 2, CH, VOX), BF16),
-            jax.ShapeDtypeStruct((4 * STEP, WIDE), BF16),
+            jax.ShapeDtypeStruct((GP, CELLS), F32),
+            jax.ShapeDtypeStruct((2, 4 * STEP, WIDE), BF16),
         ],
         scratch_shapes=[
             pltpu.VMEM((ROWS * STEP, WIDE), BF16),
             pltpu.VMEM((ROWS * STEP, 2 * HALF), F32),
             pltpu.VMEM((ROWS, ZP, CH, HALF), F32),
             pltpu.VMEM((ROWS, ZP, CH, HALF), F32),
+            pltpu.VMEM((ROWS // 2, CH, VOX), BF16),
+            pltpu.VMEM((ROWS // 2, CH, VOX), BF16),
+            pltpu.VMEM((GP, VOX), F32),
+            pltpu.VMEM((GP, VOX), F32),
         ],
-        compiler_params=params(24),
-        cost_estimate=cost(4),
-        name="stencil_half",
-    )(g, bands)
-
-
-def no_maximum_needed(codebook):
-    wide = codebook[...].astype(F32)
-    longest = jnp.max(jnp.sum(wide * wide, axis=0, keepdims=True))
-    return longest * (CH * (1.01 * SOFTMAX_HEAT * LOG2E) ** 2) <= SAFE * SAFE
-
-
-def posteriors(fine, steps, take, mark, cbt, acc, e0, e1):
-    slots = lax.broadcasted_iota(jnp.int32, (CELLS, VOX), 0)
-
-    def logits_of(u):
-        stacked = jnp.concatenate([u, u, u, jnp.ones((16, VOX), BF16)], axis=0)
-        return jnp.dot(cbt[...], stacked, preferred_element_type=F32)
-
-    def add(post, k):
-        onehot = jnp.where(slots == mark(k), 1.0, 0.0).astype(BF16)
-        acc[...] += lax.dot_general(post, onehot, NT, preferred_element_type=F32)
-
-    def begin(k, e_s):
-        e = jnp.exp2(logits_of(take(k)))
-        e_s[...] = e
-        return 1.0 / jnp.sum(e, axis=0, keepdims=True)
-
-    def finish(inverse, k, e_s):
-        add((e_s[...] * inverse).astype(BF16), k)
-
-    @pl.when(fine)
-    def _():
-        def pair(k, inv):
-            nxt = begin(2 * k + 1, e1)
-            finish(inv, 2 * k, e0)
-            inv = begin(2 * k + 2, e0)
-            finish(nxt, 2 * k + 1, e1)
-            return inv
-
-        inv = lax.fori_loop(0, steps // 2 - 1, pair, begin(0, e0))
-        nxt = begin(steps - 1, e1)
-        finish(inv, steps - 2, e0)
-        finish(nxt, steps - 1, e1)
-
-    @pl.when(jnp.logical_not(fine))
-    def _():
-        def careful(k, _):
-            logits = logits_of(take(k))
-            e = jnp.exp2(logits - jnp.max(logits, axis=0, keepdims=True))
-            add((e * (1.0 / jnp.sum(e, axis=0, keepdims=True))).astype(BF16), k)
-            return 0
-
-        lax.fori_loop(0, steps, careful, 0)
-
-
-def label_row(marks, half, row):
-    parts = [marks[pl.ds(p * ROWS + row + odd, 1), :] for odd in range(2) for p in range(ZP)]
-    return jnp.concatenate([part[:, half * HALF : (half + 1) * HALF] for part in parts], axis=1)
-
-
-def inner_kernel(half, unit, marks, cbt, codebook, *refs):
-    if half:
-        given, acc, e0, e1 = refs
-        acc[...] = given[...]
-    else:
-        acc, tops, e0, e1 = refs
-        acc[...] = jnp.zeros_like(acc)
-        parts = [
-            marks[p * ROWS + row : p * ROWS + row + 1, h * HALF : (h + 1) * HALF]
-            for h in range(2)
-            for row in range(2)
-            for p in range(ZP)
-        ]
-        tops[...] = jnp.concatenate(parts, axis=0).astype(F32).astype(BF16)
-    posteriors(
-        no_maximum_needed(codebook),
-        ROWS // 2 - 2,
-        lambda k: unit[k + 1],
-        lambda k: label_row(marks, half, 2 * k + 2),
-        cbt, acc, e0, e1,
-    )
-
-
-def inner(unit, marks, cbt, codebook, half, *given):
-    sums = jax.ShapeDtypeStruct((GP, CELLS), F32)
-    return pl.pallas_call(
-        functools.partial(inner_kernel, half),
-        in_specs=[VMEM] * (4 + len(given)),
-        out_specs=VMEM if half else [VMEM] * 2,
-        out_shape=sums if half else [sums, jax.ShapeDtypeStruct((8, HALF), BF16)],
-        scratch_shapes=[pltpu.VMEM((GP, VOX), F32)] * 2,
-        compiler_params=params(24),
-        cost_estimate=cost(7),
-        name="posterior_half",
-    )(unit, marks, cbt, codebook, *given)
-
-
-def border_kernel(last0, last1, bands, following, marks, cbt, codebook, given, out, xh, ue, acc, e0, e1):
+        compiler_params=params(36),
+        cost_estimate=cost(15),
+        name="decode_band",
+    )(g, bands, marks, cbt, codebook)
+
+
+def border_kernel(last, bands, following, marks, cbt, codebook, given, out, xh, ue, acc, e0, e1):
     joined = jnp.where(position()[0] < NZ - 1, 1.0, 0.0)
-    blocks = NR * PIECE
-    for half, last in enumerate((last0, last1)):
-        xh[: 4 * STEP] = last[...]
+    blocks = 2 * PIECE
+    for half in range(2):
+        xh[: 4 * STEP] = last[half]
 
         def store(row, p, t, block):
             start = (4 + row) * STEP + p * CH
             xh[start : start + CH, t * 128 : (t + 1) * 128] = block
 
-        transposed_rows(lambda r, i: following[half * blocks + r * PIECE + i], range(4), store)
+        transposed_rows(lambda r, i: following[r * blocks + half * PIECE + i], range(4), store)
         y = jnp.dot(xh[STEP : 7 * STEP], bands[half], preferred_element_type=F32)
 
         def raw(row, p):
@@ -396,7 +404,7 @@
                 )
 
     acc[...] = given[...]
-    tops = [following[2 * blocks + h].astype(F32).astype(jnp.int32) for h in range(2)]
+    tops = [following[NR * blocks + h].astype(F32).astype(jnp.int32) for h in range(2)]
 
     def mark(k):
         own = [label_row(marks, h, ROWS - 2) for h in range(2)]
@@ -405,7 +413,23 @@
         ]
         return jnp.where(k < 2, jnp.where(k == 0, own[0], next_[0]), jnp.where(k == 2, own[1], next_[1]))
 
-    posteriors(no_maximum_needed(codebook), 4, lambda k: ue[k], mark, cbt, acc, e0, e1)
+    begin, finish, careful = posterior_steps(cbt, acc)
+    fine = no_maximum_needed(codebook)
+
+    @pl.when(fine)
+    def _():
+        inv = begin(ue[0], e0)
+        nxt = begin(ue[1], e1)
+        finish(inv, mark(0), e0)
+        inv = begin(ue[2], e0)
+        finish(nxt, mark(1), e1)
+        nxt = begin(ue[3], e1)
+        finish(inv, mark(2), e0)
+        finish(nxt, mark(3), e1)
+
+    @pl.when(jnp.logical_not(fine))
+    def _():
+        loop(0, 4, lambda k: careful(ue[k], mark(k)))
 
     goes = marks[ZP * ROWS : ZP * ROWS + 1]
     select = jnp.where(lax.broadcasted_iota(jnp.int32, (TILES * CAP, CELLS), 0) == goes, SCALE, 0.0).astype(BF16)
@@ -423,10 +447,10 @@
         out[o, FULL * CAP :] = jnp.where(lane < 64, rest[: CAP // 2], pltpu.roll(rest[CAP // 2 :], 64, 1))
 
 
-def border(last0, last1, bands, following, marks, cbt, codebook, given):
+def border(last, bands, following, marks, cbt, codebook, given):
     return pl.pallas_call(
         border_kernel,
-        in_specs=[VMEM] * 8,
+        in_specs=[VMEM] * 7,
         out_specs=VMEM,
         out_shape=jax.ShapeDtypeStruct((TILES, OUT_ROWS, 128), F32),
         scratch_shapes=[
@@ -439,7 +463,7 @@
         compiler_params=params(24),
         cost_estimate=cost(4),
         name="border_rows",
-    )(last0, last1, bands, following, marks, cbt, codebook, given)
+    )(last, bands, following, marks, cbt, codebook, given)
 
 
 def unpack_kernel(parts, out):
@@ -472,19 +496,14 @@
         for r in range(NR)
     ]
     plane = functools.partial(lax.all_to_all, axis_name=("x", "r"), split_axis=0, concat_axis=0, tiled=True)
-    g0 = plane(pack(images, 0))
-    g1 = plane(pack(images, 1))
+    g = plane(pack(images))
     marks, cbt, bands = prepare(labels, owners.reshape(1, CELLS), counts, codebook)
     marks = lax.ppermute(marks, ("z", "x", "r"), swap)
-    unit0, last0 = stencil(g0, bands, 0)
-    acc, tops = inner(unit0, marks, cbt, codebook, 0)
-    g1, acc, tops = lax.optimization_barrier((g1, acc, tops))
-    upper = [g[:NR, :, :4].reshape(NR * PIECE, 4, 128) for g in (g0, g1)]
-    upper = jnp.concatenate([*upper, tops.reshape(2, 4, HALF)], axis=0)
+    tops = marks[: ZP * ROWS].reshape(ZP, ROWS, 2, HALF)[:, :2].transpose(2, 1, 0, 3).reshape(2, 4, HALF)
+    upper = jnp.concatenate([g[:NR, :, :4].reshape(NR * 2 * PIECE, 4, 128), tops.astype(BF16)], axis=0)
     following = lax.ppermute(upper, "z", [((i + 1) % NZ, i) for i in range(NZ)])
-    unit1, last1 = stencil(g1, bands, 1)
-    acc = inner(unit1, marks, cbt, codebook, 1, acc)
-    packed = border(last0, last1, bands, following, marks, cbt, codebook, acc)
+    acc, last = decode(g, bands, marks, cbt, codebook)
+    packed = border(last, bands, following, marks, cbt, codebook, acc)
     packed = packed.astype(jnp.float16).reshape(NZ, NXD, OUT_ROWS, 128)
     parts = lax.all_to_all(packed, "z", split_axis=0, concat_axis=0, tiled=True)
     summed = jnp.sum(parts.astype(F32), axis=0).astype(jnp.float16)[:, None]

time: 117 us -> 118 us (level)
  waiting for transfers between devices: 8.65 us -> 19.4 us
  starting transfers between devices: 24.5 us -> 18.1 us
  local copies, waits for them, and re-layouts: 1.58 us -> 0.2 us
    all_to_all x2 -> x1, waiting for transfers between devices: 8.64 us -> 17.1 us  [local(): g = plane(pack(images))]
    all_to_all x2 -> x1, starting transfers between devices: 15.1 us -> 8.73 us  [local(): g = plane(pack(images))]
    ppermute x1, waiting for transfers between devices: 0.01 us -> 2.32 us  [local(): marks = lax.ppermute(marks, ('z', 'x', 'r'), swap)]
    unnamed x12 -> x8, local copies, waits for them, and re-layouts: 1.44 us -> 0.03 us
    pallas_call x7 -> x3, Pallas kernels: 37.4 us -> 36.4 us  [the longest x1 28.4 us: decode(): pl.pallas_call(decode_kernel, in_specs=[VMEM] * 5, out_specs=[VMEM] * 2,...]
  transfers between devices with their start and end apart: 4 -> 3, of which waited for: 2 -> 2; matrix products, arithmetic and copies ran while one was open for 0% -> 0% of each run, Pallas kernels for 25% -> 25%
where the time goes in v4:
time: 118 us; the launch traced here: 117 us
  blocking collectives  40.7 us (34%)
  Pallas kernels  38.5 us (33%)
  waiting for transfers between devices  19.4 us (16%)
  starting transfers between devices  18.1 us (15%)
    pallas_call x1, Pallas kernels, decode(): pl.pallas_call(decode_kernel, in_specs=[VMEM] * 5, out_specs=[VMEM] * 2,...  28.4 us
    all_to_all x1, blocking collectives, local(): parts = lax.all_to_all(packed, 'z', split_axis=0, concat_axis=0, tiled=True)  21 us
    all_to_all x1, blocking collectives, local(): return unpack(plane(spread).astype(F32))  19.7 us
    all_to_all x1, waiting for transfers between devices, local(): g = plane(pack(images))  17.1 us
    all_to_all x1, starting transfers between devices, local(): g = plane(pack(images))  8.73 us
    ppermute x1, starting transfers between devices, local(): following = lax.ppermute(upper, 'z', [((i + 1) % NZ, i) for i in range(NZ)])  5.68 us
    pallas_call x1, Pallas kernels, border(): pl.pallas_call(border_kernel, in_specs=[VMEM] * 7, out_specs=VMEM, out_sh...  4.56 us
    ppermute x1, starting transfers between devices, local(): marks = lax.ppermute(marks, ('z', 'x', 'r'), swap)  3.67 us
  transfers between devices with their start and end apart: 3, of which 2 were waited for; matrix products, arithmetic and copies ran while one was open for 0% of the time, Pallas kernels for 25%

profile of v4, /device:TPU:1, one launch (start us, length us, event | category | flops | bytes accessed | tf_op | source)
XLA Modules:
  0.0 117.4 jit_solution(16171410298938713222)
XLA Ops:
  0.0 3.4 %pack_pieces.1 = bf16[32,26,8,128]{3,2,1,0:T(8,128)(2,1)} custom-call(bf16[6,2,8,8192]{3,2,1,0:T(8,128)(2,1)} %img.1), custom_call_target="tpu_custom_call" | custom-call | flops 2000000000 | bytes 6000000 | tf_op jit(solution)/shard_map/pack_pieces/pallas_call | solution.py:96
  3.4 0.0 copy-start
  3.5 0.0 copy-start.1
  3.5 0.0 copy-start.2
  3.5 0.0 copy-start.3
  3.5 8.7 %all-to-all-start = ((bf16[32,26,8,128]{3,2,1,0:T(8,128)(2,1)}), bf16[32,26,8,128]{3,2,1,0:T(8,128)(2,1)S(1)}, u32[]{:S(2)}, u32[]{:S(2)}) async-start(bf16[32,26,8,128]{3,2,1,0:T(8,128)(2,1)} %pack_pieces.1), calls=%async_computation | async-start | bytes 3407872 | tf_op jit(solution)/shard_map/all_to_all | solution.py:499
  12.2 0.0 copy-done
  12.2 0.0 copy-done.1
  12.3 0.0 copy-done.2
  12.3 0.0 copy-done.3
  12.3 0.9 prepare.1
  13.2 3.7 %collective-permute-start = (s32[72,256]{1,0:T(8,128)S(1)}, s32[72,256]{1,0:T(8,128)S(1)}, u32[]{:S(2)}, u32[]{:S(2)}) collective-permute-start(s32[72,256]{1,0:T(8,128)S(1)} %get-tuple-element.11), channel_id=1, source_target_pairs={{0,0},{1,32},{2,64},{3,96},{4,128},{5,160},{6,192},{7,224},{8,8},{... | collective-permute-start | bytes 221192 | tf_op jit(solution)/shard_map/ppermute | solution.py:501
  16.9 2.3 %collective-permute-done.marks = s32[72,256]{1,0:T(8,128)S(1)} collective-permute-done((s32[72,256]{1,0:T(8,128)S(1)}, s32[72,256]{1,0:T(8,128)S(1)}, u32[]{:S(2)}, u32[]{:S(2)}) %collective-permute-start) | collective-permute-done | bytes 73760 | tf_op jit(solution)/shard_map/ppermute | solution.py:501
  19.2 17.1 %all-to-all-done.g = bf16[32,26,8,128]{3,2,1,0:T(8,128)(2,1)S(1)} async-done(((bf16[32,26,8,128]{3,2,1,0:T(8,128)(2,1)}), bf16[32,26,8,128]{3,2,1,0:T(8,128)(2,1)S(1)}, u32[]{:S(2)}, u32[]{:S(2)}) %all-to-all-start) | async-done | bytes 1703968 | tf_op jit(solution)/shard_map/all_to_all | solution.py:499
  36.3 0.1 slice.14
  36.4 0.1 pad_maximum_fusion
  36.5 5.7 %collective-permute-start.1 = (bf16[210,4,128]{2,1,0:T(4,128)(2,1)S(1)}, bf16[210,4,128]{2,1,0:T(4,128)(2,1)S(1)}, u32[]{:S(2)}, u32[]{:S(2)}) collective-permute-start(bf16[210,4,128]{2,1,0:T(4,128)(2,1)S(1)} %pad_maximum_fusion), channel_id=1, source_target_pairs={{32,0},{64,32},{96,64},{128,96},{160,128},{192,160},{224,192},{0,2... | collective-permute-start | bytes 645128 | tf_op jit(solution)/shard_map/ppermute | solution.py:504
  42.2 28.4 %decode_band.1 = (f32[552,256]{1,0:T(8,128)S(1)}, bf16[2,384,256]{2,1,0:T(8,128)(2,1)S(1)}) custom-call(bf16[32,26,8,128]{3,2,1,0:T(8,128)(2,1)S(1)} %all-to-all-done.g, bf16[2,256,256]{2,1,0:T(8,128)(2,1)S(1)} %get-tuple-element.10.bands, s32[72,256]{1,0:T(8,128)S(1)} %collective-permute-done.marks, bf16[552,160]{1,0:T(8,128)(2,1)S(1)} %get-tuple-element.12.cbt, ...), custom_call_target="tpu_custom_call" | custom-call | flops 15000000512 | bytes 45000000 | tf_op jit(solution)/shard_map/decode_band/pallas_call | solution.py:338
  70.6 0.0 collective-permute-done.1.following
  70.6 4.6 %border_rows.1 = f32[32,72,128]{2,1,0:T(8,128)S(1)} custom-call(bf16[2,384,256]{2,1,0:T(8,128)(2,1)S(1)} %get-tuple-element.13.last, bf16[2,256,256]{2,1,0:T(8,128)(2,1)S(1)} %get-tuple-element.10.bands, bf16[210,4,128]{2,1,0:T(4,128)(2,1)S(1)} %collective-permute-done.1.following, s32[72,256]{1,0:T(8,128)S(1)} %collective-permute-done.marks, ...), custom_call_target="tpu_custom_call" | custom-call | flops 4000000000 | bytes 12000000 | tf_op jit(solution)/shard_map/border_rows/pallas_call | solution.py:451
  75.2 0.1 convert_element_type.25
  75.3 21.0 %all_to_all.15 = f16[8,4,72,128]{3,2,1,0:T(8,128)(2,1)S(1)} all-to-all(f16[8,4,72,128]{3,2,1,0:T(8,128)(2,1)S(1)} %bitcast.8), channel_id=1, replica_groups=mesh['z'=8,'x'=4,'r'=8] {'z'}, dimensions={0} | all-to-all | bytes 1179648 | tf_op jit(solution)/shard_map/all_to_all | solution.py:508
  96.2 0.1 convert_reduce_fusion
  96.3 0.1 broadcast_in_dim.2
  96.4 19.7 %all_to_all.16 = f16[32,72,128]{2,1,0:T(8,128)(2,1)S(1)} all-to-all(f16[32,72,128]{2,1,0:T(8,128)(2,1)S(1)} %bitcast.9), channel_id=1, replica_groups=mesh['z'=8,'x'=4,'r'=8] {'x','r'}, dimensions={0} | all-to-all | bytes 1179648 | tf_op jit(solution)/shard_map/all_to_all | solution.py:511
  116.2 0.1 convert_element_type.28.parts
  116.2 1.2 unpack_cells.1
  (5 shorter events, 0.1 us)
Async XLA Ops:
  3.4 8.8 %copy-start = (s32[2,32,256]{2,1,0:T(8,128)S(1)}, s32[2,32,256]{2,1,0:T(8,128)}, u32[]{:S(2)}) copy-start(s32[2,32,256]{2,1,0:T(8,128)} %labels.1) | copy-start | bytes 196612
  3.5 8.8 %copy-start.1 = (bf16[48,550]{1,0:T(8,128)(2,1)S(1)}, bf16[48,550]{1,0:T(8,128)(2,1)}, u32[]{:S(2)}) copy-start(bf16[48,550]{1,0:T(8,128)(2,1)} %codebook.5) | copy-start | bytes 158404
  3.5 8.8 %copy-start.2 = (s32[256,1]{0,1:T(1,128)S(1)}, s32[256,1]{0,1:T(1,128)}, u32[]{:S(2)}) copy-start(s32[256,1]{0,1:T(1,128)} %param.8) | copy-start | bytes 3076
  3.5 8.8 %copy-start.3 = (s32[32]{0:T(128)S(1)}, s32[32]{0:T(128)}, u32[]{:S(2)}) copy-start(s32[32]{0:T(128)} %counts.1) | copy-start | bytes 388
  3.5 32.8 %all-to-all-start = ((bf16[32,26,8,128]{3,2,1,0:T(8,128)(2,1)}), bf16[32,26,8,128]{3,2,1,0:T(8,128)(2,1)S(1)}, u32[]{:S(2)}, u32[]{:S(2)}) async-start(bf16[32,26,8,128]{3,2,1,0:T(8,128)(2,1)} %pack_pieces.1), calls=%async_computation | async-start | bytes 3407872 | tf_op jit(solution)/shard_map/all_to_all | solution.py:499
  13.2 6.0 %collective-permute-start = (s32[72,256]{1,0:T(8,128)S(1)}, s32[72,256]{1,0:T(8,128)S(1)}, u32[]{:S(2)}, u32[]{:S(2)}) collective-permute-start(s32[72,256]{1,0:T(8,128)S(1)} %get-tuple-element.11), channel_id=1, source_target_pairs={{0,0},{1,32},{2,64},{3,96},{4,128},{5,160},{6,192},{7,224},{8,8},{... | collective-permute-start | bytes 221192 | tf_op jit(solution)/shard_map/ppermute | solution.py:501
  36.5 34.1 %collective-permute-start.1 = (bf16[210,4,128]{2,1,0:T(4,128)(2,1)S(1)}, bf16[210,4,128]{2,1,0:T(4,128)(2,1)S(1)}, u32[]{:S(2)}, u32[]{:S(2)}) collective-permute-start(bf16[210,4,128]{2,1,0:T(4,128)(2,1)S(1)} %pad_maximum_fusion), channel_id=1, source_target_pairs={{32,0},{64,32},{96,64},{128,96},{160,128},{192,160},{224,192},{0,2... | collective-permute-start | bytes 645128 | tf_op jit(solution)/shard_map/ppermute | solution.py:504

commit v5 on v4

--- a/solution.py
+++ b/solution.py
@@ -18,7 +18,7 @@
 COLOUR = CH // NR
 PAIRS = COLOUR * ZP
 HALF = PT // 2
-PIECE = PAIRS + 1
+PIECE = 2 * PAIRS + 1
 ROWS = 32
 STEP = ZP * CH
 WIDE = HALF + 128
@@ -37,7 +37,7 @@
 
 
 def position():
-    return lax.axis_index("z"), lax.axis_index("x"), lax.axis_index("r")
+    return lax.axis_index("z"), lax.axis_index("x"), 2 * lax.axis_index("y") + lax.axis_index("c")
 
 
 def params(mib):
@@ -50,7 +50,7 @@
 
 def pack_kernel(img, out, buf, sems):
     lane = lax.broadcasted_iota(jnp.int32, (8, 128), 1)
-    windows = [(lane // 4) == i for i in range(PAIRS)]
+    windows = [(lane // 4) == 16 * half + i for half in range(2) for i in range(PAIRS)]
     width = NXD * PT
 
     def fetch(r):
@@ -70,12 +70,12 @@
 
         has_after, has_before = (r < NR - 1).astype(F32), (r > 0).astype(F32)
         for x in range(NXD):
+            border = jnp.zeros((8, 128), F32)
             for half in range(2):
                 at = PT * x + HALF * half
-                border = jnp.zeros((8, 128), F32)
                 for i in range(PAIRS):
                     c, p = i // ZP, i % ZP
-                    out[x * NR + r, half * PIECE + i] = buf[r, c, p, :, at : at + HALF]
+                    out[x * NR + r, half * PAIRS + i] = buf[r, c, p, :, at : at + HALF]
                     if at + HALF < width:
                         right = buf[r, c, p, :, at + HALF : at + 2 * HALF].astype(F32)
                     else:
@@ -84,9 +84,9 @@
                         left = buf[r, c, p, :, at - 128 : at].astype(F32)
                     else:
                         left = buf[before, c, p, :, width - 128 :].astype(F32) * has_before
-                    both = pltpu.roll(jnp.where(lane < 64, right, left), 4 * i + 2, 1)
-                    border = jnp.where(windows[i], both, border)
-                out[x * NR + r, half * PIECE + PAIRS] = border.astype(BF16)
+                    both = pltpu.roll(jnp.where(lane < 64, right, left), 64 * half + 4 * i + 2, 1)
+                    border = jnp.where(windows[half * PAIRS + i], both, border)
+            out[x * NR + r, 2 * PAIRS] = border.astype(BF16)
         return 0
 
     lax.fori_loop(0, NR, column, 0)
@@ -97,7 +97,7 @@
         pack_kernel,
         in_specs=[pl.BlockSpec(memory_space=pltpu.HBM)],
         out_specs=VMEM,
-        out_shape=jax.ShapeDtypeStruct((NXD * NR, 2 * PIECE, 8, 128), BF16),
+        out_shape=jax.ShapeDtypeStruct((NXD * NR, PIECE, 8, 128), BF16),
         scratch_shapes=[pltpu.VMEM((NR, COLOUR, ZP, 8, NXD * PT), BF16), pltpu.SemaphoreType.DMA((NR,))],
         compiler_params=params(16),
         cost_estimate=cost(2),
@@ -139,7 +139,7 @@
     e = source - HALF
     side = e % 4
     beyond = jnp.where(side < 2, side - 2, HALF - 2 + side)
-    at = jnp.where(source < HALF, source, jnp.where(e < 4 * PAIRS, beyond, 4 * WIDE))
+    at = jnp.where(source < HALF, source, jnp.where(e % 64 < 4 * PAIRS, beyond, 4 * WIDE))
     gap = jnp.abs(at - target)
     once = jnp.where(gap == 1, 1.0, 0.0).astype(BF16)
     for half in range(2):
@@ -165,17 +165,17 @@
     )(labels, owners, counts, codebook)
 
 
-def transposed_rows(src, rows, store):
+def transposed_rows(half, src, rows, store):
     lane = lax.broadcasted_iota(jnp.int32, (CH, 128), 1)
     colour = lax.broadcasted_iota(jnp.int32, (CH, 128), 0) // NR
 
     def swapped(i):
         return jnp.swapaxes(jnp.stack([src(r, i) for r in range(NR)]).astype(F32), 0, 1)
 
-    edge = swapped(PAIRS)
+    edge = swapped(2 * PAIRS)
     for p in range(ZP):
-        parts = [swapped(ZP * c + p) for c in range(COLOUR)]
-        mask = (lane // 4) == colour * ZP + p
+        parts = [swapped(half * PAIRS + ZP * c + p) for c in range(COLOUR)]
+        mask = (lane // 4) == 16 * half + colour * ZP + p
         for row in rows:
             store(row, p, 0, jnp.concatenate([part[row] for part in parts], axis=0).astype(BF16))
             border = jnp.concatenate([edge[row]] * COLOUR, axis=0)
@@ -191,26 +191,29 @@
     return 6.0 * second - (first + third)
 
 
+def rows_at(start, size):
+    return pl.ds(start if isinstance(start, int) else pl.multiple_of(start, 16), size)
+
+
 def stencil_steps(half, g, bands, unit, last, xt, y, a_s, b_s):
     def regroup(k):
         base = k * 8 * STEP
 
         def store(row, p, t, block):
-            start = pl.multiple_of(base + (row * ZP + p) * CH, 16)
-            xt[pl.ds(start, CH), t * 128 : (t + 1) * 128] = block
-
-        transposed_rows(lambda r, i: g[k * NR + r, half * PIECE + i], range(8), store)
-        at = pl.ds(pl.multiple_of(base, 16), 8 * STEP)
+            xt[rows_at(base + (row * ZP + p) * CH, CH), t * 128 : (t + 1) * 128] = block
+
+        transposed_rows(half, lambda r, i: g[k * NR + r, i], range(8), store)
+        at = rows_at(base, 8 * STEP)
         y[at, :] = jnp.dot(xt[at, :], bands[half], preferred_element_type=F32)
 
     def keep():
         last[half] = xt[(ROWS - 4) * STEP :]
 
     def raw(row, p):
-        return xt[pl.ds(pl.multiple_of(row * STEP + p * CH, 16), CH), :HALF].astype(F32)
+        return xt[rows_at(row * STEP + p * CH, CH), :HALF].astype(F32)
 
     def cols(row, p, twice):
-        return y[pl.ds(pl.multiple_of(row * STEP + p * CH, 16), CH), twice * HALF : (twice + 1) * HALF]
+        return y[rows_at(row * STEP + p * CH, CH), twice * HALF : (twice + 1) * HALF]
 
     def first(row):
         here = [raw(row, p) for p in range(ZP)]
@@ -279,58 +282,52 @@
 
 
 def decode_kernel(g, bands, marks, cbt, codebook, acc, last, xt, y, a_s, b_s, unit0, unit1, e0, e1):
-    units = (unit0, unit1)
+    units, buffers = (unit0, unit1), (e0, e1)
     acc[...] = jnp.zeros_like(acc)
     begin, finish, careful = posterior_steps(cbt, acc)
+    halves = [stencil_steps(half, g, bands, units[half], last, xt, y, a_s, b_s) for half in range(2)]
+    fine = no_maximum_needed(codebook)
 
     def label(half, k):
         return label_row(marks, half, 2 * k)
 
-    regroup, keep, first, second = stencil_steps(0, g, bands, unit0, last, xt, y, a_s, b_s)
-    loop(0, ROWS // 8, regroup)
-    keep()
-    loop(1, ROWS - 1, first)
-    loop(1, ROWS // 2 - 1, second)
-    regroup, keep, first, second = stencil_steps(1, g, bands, unit1, last, xt, y, a_s, b_s)
-    fine = no_maximum_needed(codebook)
+    def block(half, k):
+        regroup, keep, first, second = halves[half]
+        regroup(k)
+        if k == ROWS // 8 - 1:
+            keep()
+        for row in range(max(8 * k - 1, 1), 8 * k + 7):
+            first(row)
+        pairs = list(range(max(4 * k - 1, 1), 4 * k + 3))
+        for pair in pairs:
+            second(pair)
+        return [(half, pair) for pair in pairs]
 
     @pl.when(fine)
     def _():
-        def pair(half, k, inv, following):
-            unit = units[half]
-            nxt = begin(unit[k + 1], e1)
-            finish(inv, label(half, k), e0)
-            inv = begin(following, e0)
-            finish(nxt, label(half, k + 1), e1)
-            return inv
-
-        def with_regroup(i, inv):
-            regroup(i)
-            return pair(0, 2 * i + 1, inv, unit0[2 * i + 3])
-
-        def with_rows(i, inv):
-            for j in range(10):
-                first(10 * i + j + 1)
-            for j in range(5):
-                second(5 * i + j)
-            return pair(0, 2 * i + 9, inv, unit0[2 * i + 11] if not isinstance(i, int) else unit1[1])
-
-        inv = lax.fori_loop(0, ROWS // 8, with_regroup, begin(unit0[1], e0))
-        keep()
-        inv = lax.fori_loop(0, 2, with_rows, inv)
-        inv = with_rows(2, inv)
-        inv = lax.fori_loop(0, 6, lambda i, inv: pair(1, 2 * i + 1, inv, unit1[2 * i + 3]), inv)
-        nxt = begin(unit1[14], e1)
-        finish(inv, label(1, 13), e0)
-        finish(nxt, label(1, 14), e1)
+        blocks = [(half, k) for half in range(2) for k in range(ROWS // 8)]
+        ready = block(*blocks[0])
+        started = None
+        for number in range(len(blocks)):
+            coming = block(*blocks[number + 1]) if number + 1 < len(blocks) else []
+            for n, (half, pair) in enumerate(ready):
+                if started is None:
+                    started = (0, begin(units[half][pair], buffers[0]))
+                slot, inverse = started
+                following = (ready[n + 1 :] + coming)[:1]
+                started = None
+                for half2, pair2 in following:
+                    started = (1 - slot, begin(units[half2][pair2], buffers[1 - slot]))
+                finish(inverse, label(half, pair), buffers[slot])
+            ready = coming
 
     @pl.when(jnp.logical_not(fine))
     def _():
-        loop(0, ROWS // 8, regroup)
-        keep()
-        loop(1, ROWS - 1, first)
-        loop(1, ROWS // 2 - 1, second)
-        for half in range(2):
+        for half, (regroup, keep, first, second) in enumerate(halves):
+            loop(0, ROWS // 8, regroup)
+            keep()
+            loop(1, ROWS - 1, first)
+            loop(1, ROWS // 2 - 1, second)
             loop(1, ROWS // 2 - 1, lambda k: careful(units[half][k], label(half, k)))
 
 
@@ -361,50 +358,51 @@
 
 def border_kernel(last, bands, following, marks, cbt, codebook, given, out, xh, ue, acc, e0, e1):
     joined = jnp.where(position()[0] < NZ - 1, 1.0, 0.0)
-    blocks = 2 * PIECE
-    for half in range(2):
-        xh[: 4 * STEP] = last[half]
-
-        def store(row, p, t, block):
-            start = (4 + row) * STEP + p * CH
-            xh[start : start + CH, t * 128 : (t + 1) * 128] = block
-
-        transposed_rows(lambda r, i: following[r * blocks + half * PIECE + i], range(4), store)
-        y = jnp.dot(xh[STEP : 7 * STEP], bands[half], preferred_element_type=F32)
-
-        def raw(row, p):
-            return xh[row * STEP + p * CH : row * STEP + (p + 1) * CH, :HALF].astype(F32)
-
-        def cols(row, p, twice):
-            start = (row - 1) * STEP + p * CH
-            return y[start : start + CH, twice * HALF : (twice + 1) * HALF]
-
-        def up(get, row, p):
-            return get(row - 1, p) * joined if row == 4 else get(row - 1, p)
-
-        def down(get, row, p):
-            return get(row + 1, p) * joined if row == 3 else get(row + 1, p)
-
-        a, b = {}, {}
-        for row in range(1, 7):
-            for p in range(ZP):
-                cx = cols(row, p, 0)
-                a[row, p] = vertical(up(raw, row, p), raw(row, p), down(raw, row, p)) - raw(row, 1 - p) - cx
-                b[row, p] = a[row, p] - cx
-
-        def get_b(row, p):
-            return b[row, p]
-
-        for row in range(2, 6):
-            for p in range(ZP):
-                mb = vertical(up(get_b, row, p), b[row, p], down(get_b, row, p)) - b[row, 1 - p]
-                at = ((row % 2) * ZP + p) * HALF
-                ue[half * 2 + row // 2 - 1, :, at : at + HALF] = normalise(
-                    a[row, p] + SHARPEN * (mb + cols(row, p, 1))
-                )
+
+    def prepare_units():
+        for half in range(2):
+            xh[: 4 * STEP] = last[half]
+
+            def store(row, p, t, block):
+                start = (4 + row) * STEP + p * CH
+                xh[start : start + CH, t * 128 : (t + 1) * 128] = block
+
+            transposed_rows(half, lambda r, i: following[r * PIECE + i], range(4), store)
+            y = jnp.dot(xh[STEP : 7 * STEP], bands[half], preferred_element_type=F32)
+
+            def raw(row, p):
+                return xh[row * STEP + p * CH : row * STEP + (p + 1) * CH, :HALF].astype(F32)
+
+            def cols(row, p, twice):
+                start = (row - 1) * STEP + p * CH
+                return y[start : start + CH, twice * HALF : (twice + 1) * HALF]
+
+            def up(get, row, p):
+                return get(row - 1, p) * joined if row == 4 else get(row - 1, p)
+
+            def down(get, row, p):
+                return get(row + 1, p) * joined if row == 3 else get(row + 1, p)
+
+            a, b = {}, {}
+            for row in range(1, 7):
+                for p in range(ZP):
+                    cx = cols(row, p, 0)
+                    a[row, p] = vertical(up(raw, row, p), raw(row, p), down(raw, row, p)) - raw(row, 1 - p) - cx
+                    b[row, p] = a[row, p] - cx
+
+            def get_b(row, p):
+                return b[row, p]
+
+            for row in range(2, 6):
+                for p in range(ZP):
+                    mb = vertical(up(get_b, row, p), b[row, p], down(get_b, row, p)) - b[row, 1 - p]
+                    at = ((row % 2) * ZP + p) * HALF
+                    ue[half * 2 + row // 2 - 1, :, at : at + HALF] = normalise(
+                        a[row, p] + SHARPEN * (mb + cols(row, p, 1))
+                    )
 
     acc[...] = given[...]
-    tops = [following[NR * blocks + h].astype(F32).astype(jnp.int32) for h in range(2)]
+    tops = [following[NR * PIECE + h].astype(F32).astype(jnp.int32) for h in range(2)]
 
     def mark(k):
         own = [label_row(marks, h, ROWS - 2) for h in range(2)]
@@ -418,6 +416,7 @@
 
     @pl.when(fine)
     def _():
+        prepare_units()
         inv = begin(ue[0], e0)
         nxt = begin(ue[1], e1)
         finish(inv, mark(0), e0)
@@ -429,6 +428,7 @@
 
     @pl.when(jnp.logical_not(fine))
     def _():
+        prepare_units()
         loop(0, 4, lambda k: careful(ue[k], mark(k)))
 
     goes = marks[ZP * ROWS : ZP * ROWS + 1]
@@ -467,14 +467,15 @@
 
 
 def unpack_kernel(parts, out):
-    for x in range(NXD):
-        for r in range(NR):
-            src, dst = x * NR + r, NXD * r + x
-            for t in range(FULL):
-                out[0, dst, :, t * 128 : (t + 1) * 128] = parts[src, t * CAP : (t + 1) * CAP] * (1.0 / SCALE)
-            rest = parts[src, FULL * CAP :] * (1.0 / SCALE)
-            out[0, dst, : CAP // 2, FULL * 128 :] = rest[:, :REST]
-            out[0, dst, CAP // 2 :, FULL * 128 :] = pltpu.roll(rest, 64, 1)[:, :REST]
+    for core in range(2):
+        for x in range(NXD):
+            for y in range(NR // 2):
+                src, dst = (core * NXD + x) * (NR // 2) + y, NXD * (2 * y + core) + x
+                for t in range(FULL):
+                    out[0, dst, :, t * 128 : (t + 1) * 128] = parts[src, t * CAP : (t + 1) * CAP] * (1.0 / SCALE)
+                rest = parts[src, FULL * CAP :] * (1.0 / SCALE)
+                out[0, dst, : CAP // 2, FULL * 128 :] = rest[:, :REST]
+                out[0, dst, CAP // 2 :, FULL * 128 :] = pltpu.roll(rest, 64, 1)[:, :REST]
 
 
 def unpack(parts):
@@ -495,24 +496,26 @@
         for x in range(NXD)
         for r in range(NR)
     ]
-    plane = functools.partial(lax.all_to_all, axis_name=("x", "r"), split_axis=0, concat_axis=0, tiled=True)
-    g = plane(pack(images))
+    exchange = functools.partial(lax.all_to_all, split_axis=0, concat_axis=0, tiled=True)
+    g = exchange(pack(images), ("x", "y", "c"))
     marks, cbt, bands = prepare(labels, owners.reshape(1, CELLS), counts, codebook)
-    marks = lax.ppermute(marks, ("z", "x", "r"), swap)
+    marks = lax.ppermute(marks, ("z", "x", "y", "c"), swap)
     tops = marks[: ZP * ROWS].reshape(ZP, ROWS, 2, HALF)[:, :2].transpose(2, 1, 0, 3).reshape(2, 4, HALF)
-    upper = jnp.concatenate([g[:NR, :, :4].reshape(NR * 2 * PIECE, 4, 128), tops.astype(BF16)], axis=0)
+    upper = jnp.concatenate([g[:NR, :, :4].reshape(NR * PIECE, 4, 128), tops.astype(BF16)], axis=0)
     following = lax.ppermute(upper, "z", [((i + 1) % NZ, i) for i in range(NZ)])
     acc, last = decode(g, bands, marks, cbt, codebook)
     packed = border(last, bands, following, marks, cbt, codebook, acc)
     packed = packed.astype(jnp.float16).reshape(NZ, NXD, OUT_ROWS, 128)
-    parts = lax.all_to_all(packed, "z", split_axis=0, concat_axis=0, tiled=True)
+    parts = exchange(packed, "z")
     summed = jnp.sum(parts.astype(F32), axis=0).astype(jnp.float16)[:, None]
-    spread = jnp.broadcast_to(summed, (NXD, NR, OUT_ROWS, 128)).reshape(NXD * NR, OUT_ROWS, 128)
-    return unpack(plane(spread).astype(F32))
+    spread = jnp.broadcast_to(summed, (NXD, NR // 2, OUT_ROWS, 128)).reshape(NXD * NR // 2, OUT_ROWS, 128)
+    received = lax.all_gather(exchange(spread, ("x", "y")), "c", tiled=True)
+    return unpack(received.astype(F32))
 
 
 def solution(mesh):
-    grid = Mesh(mesh.devices.reshape(NZ, NXD, NR), ("z", "x", "r"))
-    in_specs = (P("r", None, ("z", "x"), None), P(None, "r", ("z", "x")), P(), P(("z", "x"), None), P())
+    grid = Mesh(mesh.devices.reshape(NZ, NXD, NR // 2, 2), ("z", "x", "y", "c"))
+    rounds = ("y", "c")
+    in_specs = (P(rounds, None, ("z", "x"), None), P(None, rounds, ("z", "x")), P(), P(("z", "x"), None), P())
     out_specs = P(("z", "x"), None, None, None)
     return jax.shard_map(local, mesh=grid, in_specs=in_specs, out_specs=out_specs, check_vma=False)

time: 118 us -> 116 us (0.983)
  blocking collectives: 40.7 us -> 39.1 us
    all_to_all x2, blocking collectives: 40.7 us -> 35.2 us  [the longest x1 21 us: local(): parts = exchange(packed, 'z')]
    all_gather x0 -> x1, blocking collectives: none -> 3.9 us  [local(): received = lax.all_gather(exchange(spread, ('x', 'y')), 'c', tiled=True)]
  transfers between devices with their start and end apart: 3 -> 3, of which waited for: 2 -> 2; matrix products, arithmetic and copies ran while one was open for 0% -> 0% of each run, Pallas kernels for 25% -> 26%
where the time goes in v5:
time: 116 us
  blocking collectives  39.1 us (34%)
  Pallas kernels  38.9 us (34%)
  waiting for transfers between devices  18.7 us (16%)
  starting transfers between devices  18.1 us (16%)
    pallas_call x1, Pallas kernels, decode(): pl.pallas_call(decode_kernel, in_specs=[VMEM] * 5, out_specs=[VMEM] * 2,...  28.7 us
    all_to_all x1, blocking collectives, local(): parts = exchange(packed, 'z')  21 us
    all_to_all x1, waiting for transfers between devices, local(): g = exchange(pack(images), ('x', 'y', 'c'))  16.4 us
    all_to_all x1, blocking collectives, local(): received = lax.all_gather(exchange(spread, ('x', 'y')), 'c', tiled=True)  14.2 us
    all_to_all x1, starting transfers between devices, local(): g = exchange(pack(images), ('x', 'y', 'c'))  8.73 us
    ppermute x1, starting transfers between devices, local(): following = lax.ppermute(upper, 'z', [((i + 1) % NZ, i) for i in range(NZ)])  5.75 us
    pallas_call x1, Pallas kernels, border(): pl.pallas_call(border_kernel, in_specs=[VMEM] * 7, out_specs=VMEM, out_sh...  4.67 us
    all_gather x1, blocking collectives, local(): received = lax.all_gather(exchange(spread, ('x', 'y')), 'c', tiled=True)  3.9 us
  transfers between devices with their start and end apart: 3, of which 2 were waited for; matrix products, arithmetic and copies ran while one was open for 0% of the time, Pallas kernels for 26%

profile of v5, /device:TPU:1, one launch (start us, length us, event | category | flops | bytes accessed | tf_op | source)
XLA Modules:
  0.0 115.6 jit_solution(49388230841572224)
XLA Ops:
  0.0 3.4 %pack_pieces.1 = bf16[32,25,8,128]{3,2,1,0:T(8,128)(2,1)} custom-call(bf16[6,2,8,8192]{3,2,1,0:T(8,128)(2,1)} %img.1), custom_call_target="tpu_custom_call" | custom-call | flops 2000000000 | bytes 6000000 | tf_op jit(solution)/shard_map/pack_pieces/pallas_call | solution.py:96
  3.4 0.0 copy-start
  3.4 0.0 copy-start.1
  3.4 0.0 copy-start.2
  3.4 0.0 copy-start.3
  3.5 8.7 %all-to-all-start = ((bf16[32,25,8,128]{3,2,1,0:T(8,128)(2,1)}), bf16[32,25,8,128]{3,2,1,0:T(8,128)(2,1)S(1)}, u32[]{:S(2)}, u32[]{:S(2)}) async-start(bf16[32,25,8,128]{3,2,1,0:T(8,128)(2,1)} %pack_pieces.1), calls=%async_computation | async-start | bytes 3276800 | tf_op jit(solution)/shard_map/all_to_all | solution.py:500
  12.2 0.0 copy-done
  12.2 0.0 copy-done.1
  12.2 0.0 copy-done.2
  12.2 0.0 copy-done.3
  12.2 0.9 prepare.1
  13.2 3.7 %collective-permute-start = (s32[72,256]{1,0:T(8,128)S(1)}, s32[72,256]{1,0:T(8,128)S(1)}, u32[]{:S(2)}, u32[]{:S(2)}) collective-permute-start(s32[72,256]{1,0:T(8,128)S(1)} %get-tuple-element.11), channel_id=1, source_target_pairs={{0,0},{1,32},{2,64},{3,96},{4,128},{5,160},{6,192},{7,224},{8,8},{... | collective-permute-start | bytes 221192 | tf_op jit(solution)/shard_map/ppermute | solution.py:502
  16.8 2.3 %collective-permute-done.marks = s32[72,256]{1,0:T(8,128)S(1)} collective-permute-done((s32[72,256]{1,0:T(8,128)S(1)}, s32[72,256]{1,0:T(8,128)S(1)}, u32[]{:S(2)}, u32[]{:S(2)}) %collective-permute-start) | collective-permute-done | bytes 73760 | tf_op jit(solution)/shard_map/ppermute | solution.py:502
  19.2 16.4 %all-to-all-done.g = bf16[32,25,8,128]{3,2,1,0:T(8,128)(2,1)S(1)} async-done(((bf16[32,25,8,128]{3,2,1,0:T(8,128)(2,1)}), bf16[32,25,8,128]{3,2,1,0:T(8,128)(2,1)S(1)}, u32[]{:S(2)}, u32[]{:S(2)}) %all-to-all-start) | async-done | bytes 1638432 | tf_op jit(solution)/shard_map/all_to_all | solution.py:500
  35.6 0.1 slice.14
  35.6 0.1 pad_maximum_fusion
  35.8 5.7 %collective-permute-start.1 = (bf16[202,4,128]{2,1,0:T(4,128)(2,1)S(1)}, bf16[202,4,128]{2,1,0:T(4,128)(2,1)S(1)}, u32[]{:S(2)}, u32[]{:S(2)}) collective-permute-start(bf16[202,4,128]{2,1,0:T(4,128)(2,1)S(1)} %pad_maximum_fusion), channel_id=1, source_target_pairs={{32,0},{64,32},{96,64},{128,96},{160,128},{192,160},{224,192},{0,2... | collective-permute-start | bytes 620552 | tf_op jit(solution)/shard_map/ppermute | solution.py:505
  41.5 28.7 %decode_band.1 = (f32[552,256]{1,0:T(8,128)S(1)}, bf16[2,384,256]{2,1,0:T(8,128)(2,1)S(1)}) custom-call(bf16[32,25,8,128]{3,2,1,0:T(8,128)(2,1)S(1)} %all-to-all-done.g, bf16[2,256,256]{2,1,0:T(8,128)(2,1)S(1)} %get-tuple-element.10.bands, s32[72,256]{1,0:T(8,128)S(1)} %collective-permute-done.marks, bf16[552,160]{1,0:T(8,128)(2,1)S(1)} %get-tuple-element.12.cbt, ...), custom_call_target="tpu_custom_call" | custom-call | flops 15000000512 | bytes 45000000 | tf_op jit(solution)/shard_map/decode_band/pallas_call | solution.py:335
  70.3 0.0 collective-permute-done.1.following
  70.3 4.7 %border_rows.1 = f32[32,72,128]{2,1,0:T(8,128)S(1)} custom-call(bf16[2,384,256]{2,1,0:T(8,128)(2,1)S(1)} %get-tuple-element.13.last, bf16[2,256,256]{2,1,0:T(8,128)(2,1)S(1)} %get-tuple-element.10.bands, bf16[202,4,128]{2,1,0:T(4,128)(2,1)S(1)} %collective-permute-done.1.following, s32[72,256]{1,0:T(8,128)S(1)} %collective-permute-done.marks, ...), custom_call_target="tpu_custom_call" | custom-call | flops 4000000000 | bytes 12000000 | tf_op jit(solution)/shard_map/border_rows/pallas_call | solution.py:451
  74.9 0.1 convert_element_type.25
  75.0 21.0 %all_to_all.15 = f16[8,4,72,128]{3,2,1,0:T(8,128)(2,1)S(1)} all-to-all(f16[8,4,72,128]{3,2,1,0:T(8,128)(2,1)S(1)} %bitcast.8), channel_id=1, replica_groups=mesh['z'=8,'x'=4,'y'=4,'c'=2] {'z'}, dimensions={0} | all-to-all | bytes 1179648 | tf_op jit(solution)/shard_map/all_to_all | solution.py:509
  96.1 0.1 convert_reduce_fusion
  96.2 14.2 %all_to_all.16 = f16[16,72,128]{2,1,0:T(8,128)(2,1)S(1)} all-to-all(f16[16,72,128]{2,1,0:T(8,128)(2,1)S(1)} %bitcast.9), channel_id=1, replica_groups=mesh['z'=8,'x'=4,'y'=4,'c'=2] {'x','y'}, dimensions={0} | all-to-all | bytes 589824 | tf_op jit(solution)/shard_map/all_to_all | solution.py:512
  110.4 3.9 %all_gather.3 = f16[32,72,128]{2,1,0:T(8,128)(2,1)S(1)} all-gather(f16[16,72,128]{2,1,0:T(8,128)(2,1)S(1)} %all_to_all.16), channel_id=1, replica_groups=mesh['z'=8,'x'=4,'y'=4,'c'=2] {'c'}, dimensions={0}, use_global_device_ids=true | all-gather | bytes 884736 | tf_op jit(solution)/shard_map/all_gather | solution.py:512
  114.3 0.1 convert_element_type.28.parts
  114.4 1.2 %unpack_cells.1 = f32[1,32,16,550]{3,2,1,0:T(8,128)} custom-call(f32[32,72,128]{2,1,0:T(8,128)S(1)} %convert_element_type.28.parts), custom_call_target="tpu_custom_call" | custom-call | tf_op jit(solution)/shard_map/unpack_cells/pallas_call | solution.py:482
  (6 shorter events, 0.1 us)
Async XLA Ops:
  3.4 8.8 %copy-start = (s32[2,32,256]{2,1,0:T(8,128)S(1)}, s32[2,32,256]{2,1,0:T(8,128)}, u32[]{:S(2)}) copy-start(s32[2,32,256]{2,1,0:T(8,128)} %labels.1) | copy-start | bytes 196612
  3.4 8.8 %copy-start.1 = (bf16[48,550]{1,0:T(8,128)(2,1)S(1)}, bf16[48,550]{1,0:T(8,128)(2,1)}, u32[]{:S(2)}) copy-start(bf16[48,550]{1,0:T(8,128)(2,1)} %codebook.5) | copy-start | bytes 158404
  3.4 8.8 %copy-start.2 = (s32[256,1]{0,1:T(1,128)S(1)}, s32[256,1]{0,1:T(1,128)}, u32[]{:S(2)}) copy-start(s32[256,1]{0,1:T(1,128)} %param.8) | copy-start | bytes 3076
  3.4 8.8 %copy-start.3 = (s32[32]{0:T(128)S(1)}, s32[32]{0:T(128)}, u32[]{:S(2)}) copy-start(s32[32]{0:T(128)} %counts.1) | copy-start | bytes 388
  3.5 32.1 %all-to-all-start = ((bf16[32,25,8,128]{3,2,1,0:T(8,128)(2,1)}), bf16[32,25,8,128]{3,2,1,0:T(8,128)(2,1)S(1)}, u32[]{:S(2)}, u32[]{:S(2)}) async-start(bf16[32,25,8,128]{3,2,1,0:T(8,128)(2,1)} %pack_pieces.1), calls=%async_computation | async-start | bytes 3276800 | tf_op jit(solution)/shard_map/all_to_all | solution.py:500
  13.2 6.0 %collective-permute-start = (s32[72,256]{1,0:T(8,128)S(1)}, s32[72,256]{1,0:T(8,128)S(1)}, u32[]{:S(2)}, u32[]{:S(2)}) collective-permute-start(s32[72,256]{1,0:T(8,128)S(1)} %get-tuple-element.11), channel_id=1, source_target_pairs={{0,0},{1,32},{2,64},{3,96},{4,128},{5,160},{6,192},{7,224},{8,8},{... | collective-permute-start | bytes 221192 | tf_op jit(solution)/shard_map/ppermute | solution.py:502
  35.8 34.5 %collective-permute-start.1 = (bf16[202,4,128]{2,1,0:T(4,128)(2,1)S(1)}, bf16[202,4,128]{2,1,0:T(4,128)(2,1)S(1)}, u32[]{:S(2)}, u32[]{:S(2)}) collective-permute-start(bf16[202,4,128]{2,1,0:T(4,128)(2,1)S(1)} %pad_maximum_fusion), channel_id=1, source_target_pairs={{32,0},{64,32},{96,64},{128,96},{160,128},{192,160},{224,192},{0,2... | collective-permute-start | bytes 620552 | tf_op jit(solution)/shard_map/ppermute | solution.py:505

commit v6 on v5

--- a/solution.py
+++ b/solution.py
@@ -467,10 +467,13 @@
 
 
 def unpack_kernel(parts, out):
+    half_rounds = NR // 2
+    y = lax.axis_index("y")
     for core in range(2):
-        for x in range(NXD):
-            for y in range(NR // 2):
-                src, dst = (core * NXD + x) * (NR // 2) + y, NXD * (2 * y + core) + x
+        for back in range(half_rounds):
+            r = 2 * ((y + half_rounds - back) % half_rounds) + core
+            for x in range(NXD):
+                src, dst = (core * half_rounds + back) * NXD + x, NXD * r + x
                 for t in range(FULL):
                     out[0, dst, :, t * 128 : (t + 1) * 128] = parts[src, t * CAP : (t + 1) * CAP] * (1.0 / SCALE)
                 rest = parts[src, FULL * CAP :] * (1.0 / SCALE)
@@ -505,11 +508,11 @@
     following = lax.ppermute(upper, "z", [((i + 1) % NZ, i) for i in range(NZ)])
     acc, last = decode(g, bands, marks, cbt, codebook)
     packed = border(last, bands, following, marks, cbt, codebook, acc)
-    packed = packed.astype(jnp.float16).reshape(NZ, NXD, OUT_ROWS, 128)
-    parts = exchange(packed, "z")
-    summed = jnp.sum(parts.astype(F32), axis=0).astype(jnp.float16)[:, None]
-    spread = jnp.broadcast_to(summed, (NXD, NR // 2, OUT_ROWS, 128)).reshape(NXD * NR // 2, OUT_ROWS, 128)
-    received = lax.all_gather(exchange(spread, ("x", "y")), "c", tiled=True)
+    parts = exchange(packed.astype(jnp.float16), ("z", "x")).reshape(NZ, NXD, OUT_ROWS, 128)
+    summed = jnp.sum(parts.astype(F32), axis=0).astype(jnp.float16)
+    ring = NR // 2
+    hops = [lax.ppermute(summed, "y", [(i, (i + k) % ring) for i in range(ring)]) for k in range(1, ring)]
+    received = lax.all_gather(jnp.concatenate([summed, *hops], axis=0), "c", tiled=True)
     return unpack(received.astype(F32))
 
 

time: 116 us -> 113 us (0.974)
  blocking collectives: 39.1 us -> 30.1 us
  waiting for transfers between devices: 18.7 us -> 22.8 us
  starting transfers between devices: 18.1 us -> 19.7 us
    all_to_all x2 -> x1, blocking collectives: 35.2 us -> 24.5 us  [local(): exchange(packed.astype(jnp.float16), ('z', 'x'))]
    ppermute x0 -> x3, waiting for transfers between devices: none -> 4.13 us  [local(): lax.ppermute(summed, 'y', [(i, (i + k) % ring) for i in range(ring)])]
    all_gather x1, blocking collectives: 3.9 us -> 5.68 us  [local(): lax.all_gather(jnp.concatenate([summed, *hops], axis=0), 'c', tiled=True)]
    ppermute x0 -> x3, starting transfers between devices: none -> 1.54 us  [local(): lax.ppermute(summed, 'y', [(i, (i + k) % ring) for i in range(ring)])]
  transfers between devices with their start and end apart: 3 -> 6, of which waited for: 2 -> 5; matrix products, arithmetic and copies ran while one was open for 0% -> 0% of each run, Pallas kernels for 26% -> 26%
where the time goes in v6:
time: 113 us; the launch traced here: 112 us
  Pallas kernels  38.9 us (34%)
  blocking collectives  30.1 us (27%)
  waiting for transfers between devices  22.8 us (20%)
  starting transfers between devices  19.7 us (17%)
    pallas_call x1, Pallas kernels, decode(): pl.pallas_call(decode_kernel, in_specs=[VMEM] * 5, out_specs=[VMEM] * 2,...  28.7 us
    all_to_all x1, blocking collectives, local(): exchange(packed.astype(jnp.float16), ('z', 'x'))  24.5 us
    all_to_all x1, waiting for transfers between devices, local(): g = exchange(pack(images), ('x', 'y', 'c'))  16.4 us
    all_to_all x1, starting transfers between devices, local(): g = exchange(pack(images), ('x', 'y', 'c'))  8.73 us
    ppermute x1, starting transfers between devices, local(): following = lax.ppermute(upper, 'z', [((i + 1) % NZ, i) for i in range(NZ)])  5.75 us
    all_gather x1, blocking collectives, local(): lax.all_gather(jnp.concatenate([summed, *hops], axis=0), 'c', tiled=True)  5.68 us
    pallas_call x1, Pallas kernels, border(): pl.pallas_call(border_kernel, in_specs=[VMEM] * 7, out_specs=VMEM, out_sh...  4.67 us
    ppermute x3, waiting for transfers between devices, local(): lax.ppermute(summed, 'y', [(i, (i + k) % ring) for i in range(ring)])  4.13 us
  transfers between devices with their start and end apart: 6, of which 5 were waited for; matrix products, arithmetic and copies ran while one was open for 0% of the time, Pallas kernels for 26%

profile of v6, /device:TPU:1, one launch (start us, length us, event | category | flops | bytes accessed | tf_op | source)
XLA Modules:
  0.0 112.3 jit_solution(6381150607326370652)
XLA Ops:
  0.0 3.4 %pack_pieces.1 = bf16[32,25,8,128]{3,2,1,0:T(8,128)(2,1)} custom-call(bf16[6,2,8,8192]{3,2,1,0:T(8,128)(2,1)} %img.1), custom_call_target="tpu_custom_call" | custom-call | flops 2000000000 | bytes 6000000 | tf_op jit(solution)/shard_map/pack_pieces/pallas_call | solution.py:96
  3.4 0.0 copy-start
  3.4 0.0 copy-start.1
  3.5 0.0 copy-start.2
  3.5 0.0 copy-start.3
  3.5 8.7 %all-to-all-start = ((bf16[32,25,8,128]{3,2,1,0:T(8,128)(2,1)}), bf16[32,25,8,128]{3,2,1,0:T(8,128)(2,1)S(1)}, u32[]{:S(2)}, u32[]{:S(2)}) async-start(bf16[32,25,8,128]{3,2,1,0:T(8,128)(2,1)} %pack_pieces.1), calls=%async_computation | async-start | bytes 3276800 | tf_op jit(solution)/shard_map/all_to_all | solution.py:503
  12.2 0.0 copy-done
  12.2 0.0 copy-done.1
  12.2 0.0 copy-done.2
  12.3 0.9 prepare.1
  13.2 3.7 %collective-permute-start = (s32[72,256]{1,0:T(8,128)S(1)}, s32[72,256]{1,0:T(8,128)S(1)}, u32[]{:S(2)}, u32[]{:S(2)}) collective-permute-start(s32[72,256]{1,0:T(8,128)S(1)} %get-tuple-element.11), channel_id=1, source_target_pairs={{0,0},{1,32},{2,64},{3,96},{4,128},{5,160},{6,192},{7,224},{8,8},{... | collective-permute-start | bytes 221192 | tf_op jit(solution)/shard_map/ppermute | solution.py:505
  16.9 2.3 %collective-permute-done.marks = s32[72,256]{1,0:T(8,128)S(1)} collective-permute-done((s32[72,256]{1,0:T(8,128)S(1)}, s32[72,256]{1,0:T(8,128)S(1)}, u32[]{:S(2)}, u32[]{:S(2)}) %collective-permute-start) | collective-permute-done | bytes 73760 | tf_op jit(solution)/shard_map/ppermute | solution.py:505
  19.2 16.4 %all-to-all-done.g = bf16[32,25,8,128]{3,2,1,0:T(8,128)(2,1)S(1)} async-done(((bf16[32,25,8,128]{3,2,1,0:T(8,128)(2,1)}), bf16[32,25,8,128]{3,2,1,0:T(8,128)(2,1)S(1)}, u32[]{:S(2)}, u32[]{:S(2)}) %all-to-all-start) | async-done | bytes 1638432 | tf_op jit(solution)/shard_map/all_to_all | solution.py:503
  35.6 0.1 slice.14
  35.7 0.1 pad_maximum_fusion.1
  35.8 5.7 %collective-permute-start.1 = (bf16[202,4,128]{2,1,0:T(4,128)(2,1)S(1)}, bf16[202,4,128]{2,1,0:T(4,128)(2,1)S(1)}, u32[]{:S(2)}, u32[]{:S(2)}) collective-permute-start(bf16[202,4,128]{2,1,0:T(4,128)(2,1)S(1)} %pad_maximum_fusion.1), channel_id=1, source_target_pairs={{32,0},{64,32},{96,64},{128,96},{160,128},{192,160},{224,192},{0,2... | collective-permute-start | bytes 620552 | tf_op jit(solution)/shard_map/ppermute | solution.py:508
  41.5 28.7 %decode_band.1 = (f32[552,256]{1,0:T(8,128)S(1)}, bf16[2,384,256]{2,1,0:T(8,128)(2,1)S(1)}) custom-call(bf16[32,25,8,128]{3,2,1,0:T(8,128)(2,1)S(1)} %all-to-all-done.g, bf16[2,256,256]{2,1,0:T(8,128)(2,1)S(1)} %get-tuple-element.10.bands, s32[72,256]{1,0:T(8,128)S(1)} %collective-permute-done.marks, bf16[552,160]{1,0:T(8,128)(2,1)S(1)} %get-tuple-element.12.cbt, ...), custom_call_target="tpu_custom_call" | custom-call | flops 15000000512 | bytes 45000000 | tf_op jit(solution)/shard_map/decode_band/pallas_call | solution.py:335
  70.3 0.0 collective-permute-done.1.following
  70.3 4.7 %border_rows.1 = f32[32,72,128]{2,1,0:T(8,128)S(1)} custom-call(bf16[2,384,256]{2,1,0:T(8,128)(2,1)S(1)} %get-tuple-element.13.last, bf16[2,256,256]{2,1,0:T(8,128)(2,1)S(1)} %get-tuple-element.10.bands, bf16[202,4,128]{2,1,0:T(4,128)(2,1)S(1)} %collective-permute-done.1.following, s32[72,256]{1,0:T(8,128)S(1)} %collective-permute-done.marks, ...), custom_call_target="tpu_custom_call" | custom-call | flops 4000000000 | bytes 12000000 | tf_op jit(solution)/shard_map/border_rows/pallas_call | solution.py:451
  74.9 0.1 convert_element_type.24
  75.0 24.5 %all_to_all.10 = f16[32,72,128]{2,1,0:T(8,128)(2,1)S(1)} all-to-all(f16[32,72,128]{2,1,0:T(8,128)(2,1)S(1)} %convert_element_type.24), channel_id=1, replica_groups=mesh['z'=8,'x'=4,'y'=4,'c'=2] {'z','x'}, dimensions={0} | all-to-all | bytes 1179648 | tf_op jit(solution)/shard_map/all_to_all | solution.py:511
  99.5 0.1 convert_reduce_fusion
  99.6 0.1 collective-permute-start.4
  99.7 1.0 collective-permute-start.3
  100.7 0.4 collective-permute-start.2
  101.1 1.7 %collective-permute-done.4 = f16[4,72,128]{2,1,0:T(8,128)(2,1)S(1)} collective-permute-done((f16[4,72,128]{2,1,0:T(8,128)(2,1)S(1)}, f16[4,72,128]{2,1,0:T(8,128)(2,1)S(1)}, u32[]{:S(2)}, u32[]{:S(2)}) %collective-permute-start.4) | collective-permute-done | bytes 73760 | tf_op jit(solution)/shard_map/ppermute | solution.py:514
  102.9 1.6 %collective-permute-done.3 = f16[4,72,128]{2,1,0:T(8,128)(2,1)S(1)} collective-permute-done((f16[4,72,128]{2,1,0:T(8,128)(2,1)S(1)}, f16[4,72,128]{2,1,0:T(8,128)(2,1)S(1)}, u32[]{:S(2)}, u32[]{:S(2)}) %collective-permute-start.3) | collective-permute-done | bytes 73760 | tf_op jit(solution)/shard_map/ppermute | solution.py:514
  104.5 0.8 collective-permute-done.2
  105.3 0.1 pad_maximum_fusion
  105.4 5.7 %all_gather.3 = f16[32,72,128]{2,1,0:T(8,128)(2,1)S(1)} all-gather(f16[16,72,128]{2,1,0:T(8,128)(2,1)S(1)} %pad_maximum_fusion), channel_id=1, replica_groups=mesh['z'=8,'x'=4,'y'=4,'c'=2] {'c'}, dimensions={0}, use_global_device_ids=true | all-gather | bytes 884736 | tf_op jit(solution)/shard_map/all_gather | solution.py:515
  111.1 0.1 convert_element_type.28.parts
  111.1 1.2 %unpack_cells.1 = f32[1,32,16,550]{3,2,1,0:T(8,128)} custom-call(f32[32,72,128]{2,1,0:T(8,128)S(1)} %convert_element_type.28.parts), custom_call_target="tpu_custom_call" | custom-call | tf_op jit(solution)/shard_map/unpack_cells/pallas_call | solution.py:485
  (6 shorter events, 0.1 us)
Async XLA Ops:
  3.4 8.8 %copy-start = (s32[2,32,256]{2,1,0:T(8,128)S(1)}, s32[2,32,256]{2,1,0:T(8,128)}, u32[]{:S(2)}) copy-start(s32[2,32,256]{2,1,0:T(8,128)} %labels.1) | copy-start | bytes 196612
  3.4 8.8 %copy-start.1 = (bf16[48,550]{1,0:T(8,128)(2,1)S(1)}, bf16[48,550]{1,0:T(8,128)(2,1)}, u32[]{:S(2)}) copy-start(bf16[48,550]{1,0:T(8,128)(2,1)} %codebook.5) | copy-start | bytes 158404
  3.5 8.8 %copy-start.2 = (s32[256,1]{0,1:T(1,128)S(1)}, s32[256,1]{0,1:T(1,128)}, u32[]{:S(2)}) copy-start(s32[256,1]{0,1:T(1,128)} %param.8) | copy-start | bytes 3076
  3.5 8.8 %copy-start.3 = (s32[32]{0:T(128)S(1)}, s32[32]{0:T(128)}, u32[]{:S(2)}) copy-start(s32[32]{0:T(128)} %counts.1) | copy-start | bytes 388
  3.5 32.1 %all-to-all-start = ((bf16[32,25,8,128]{3,2,1,0:T(8,128)(2,1)}), bf16[32,25,8,128]{3,2,1,0:T(8,128)(2,1)S(1)}, u32[]{:S(2)}, u32[]{:S(2)}) async-start(bf16[32,25,8,128]{3,2,1,0:T(8,128)(2,1)} %pack_pieces.1), calls=%async_computation | async-start | bytes 3276800 | tf_op jit(solution)/shard_map/all_to_all | solution.py:503
  13.2 6.0 %collective-permute-start = (s32[72,256]{1,0:T(8,128)S(1)}, s32[72,256]{1,0:T(8,128)S(1)}, u32[]{:S(2)}, u32[]{:S(2)}) collective-permute-start(s32[72,256]{1,0:T(8,128)S(1)} %get-tuple-element.11), channel_id=1, source_target_pairs={{0,0},{1,32},{2,64},{3,96},{4,128},{5,160},{6,192},{7,224},{8,8},{... | collective-permute-start | bytes 221192 | tf_op jit(solution)/shard_map/ppermute | solution.py:505
  35.8 34.5 %collective-permute-start.1 = (bf16[202,4,128]{2,1,0:T(4,128)(2,1)S(1)}, bf16[202,4,128]{2,1,0:T(4,128)(2,1)S(1)}, u32[]{:S(2)}, u32[]{:S(2)}) collective-permute-start(bf16[202,4,128]{2,1,0:T(4,128)(2,1)S(1)} %pad_maximum_fusion.1), channel_id=1, source_target_pairs={{32,0},{64,32},{96,64},{128,96},{160,128},{192,160},{224,192},{0,2... | collective-permute-start | bytes 620552 | tf_op jit(solution)/shard_map/ppermute | solution.py:508
  99.6 3.3 %collective-permute-start.4 = (f16[4,72,128]{2,1,0:T(8,128)(2,1)S(1)}, f16[4,72,128]{2,1,0:T(8,128)(2,1)S(1)}, u32[]{:S(2)}, u32[]{:S(2)}) collective-permute-start(f16[4,72,128]{2,1,0:T(8,128)(2,1)S(1)} %convert_element_type.27), channel_id=1, source_target_pairs={{0,6},{2,0},{4,2},{6,4},{1,7},{3,1},{5,3},{7,5},{8,14},{10,8},{12,... | collective-permute-start | bytes 221192 | tf_op jit(solution)/shard_map/ppermute | solution.py:514
  99.7 4.8 %collective-permute-start.3 = (f16[4,72,128]{2,1,0:T(8,128)(2,1)S(1)}, f16[4,72,128]{2,1,0:T(8,128)(2,1)S(1)}, u32[]{:S(2)}, u32[]{:S(2)}) collective-permute-start(f16[4,72,128]{2,1,0:T(8,128)(2,1)S(1)} %convert_element_type.27), channel_id=1, source_target_pairs={{0,4},{2,6},{4,0},{6,2},{1,5},{3,7},{5,1},{7,3},{8,12},{10,14},{12... | collective-permute-start | bytes 221192 | tf_op jit(solution)/shard_map/ppermute | solution.py:514
  100.7 4.5 %collective-permute-start.2 = (f16[4,72,128]{2,1,0:T(8,128)(2,1)S(1)}, f16[4,72,128]{2,1,0:T(8,128)(2,1)S(1)}, u32[]{:S(2)}, u32[]{:S(2)}) collective-permute-start(f16[4,72,128]{2,1,0:T(8,128)(2,1)S(1)} %convert_element_type.27), channel_id=1, source_target_pairs={{0,2},{2,4},{4,6},{6,0},{1,3},{3,5},{5,7},{7,1},{8,10},{10,12},{12... | collective-permute-start | bytes 221192 | tf_op jit(solution)/shard_map/ppermute | solution.py:514

commit v7 on v6

--- a/solution.py
+++ b/solution.py
@@ -468,12 +468,12 @@
 
 def unpack_kernel(parts, out):
     half_rounds = NR // 2
-    y = lax.axis_index("y")
-    for core in range(2):
+    y, c = lax.axis_index("y"), lax.axis_index("c")
+    for other in range(2):
         for back in range(half_rounds):
-            r = 2 * ((y + half_rounds - back) % half_rounds) + core
+            r = 2 * ((y + half_rounds - back) % half_rounds) + (c + other) % 2
             for x in range(NXD):
-                src, dst = (core * half_rounds + back) * NXD + x, NXD * r + x
+                src, dst = (other * half_rounds + back) * NXD + x, NXD * r + x
                 for t in range(FULL):
                     out[0, dst, :, t * 128 : (t + 1) * 128] = parts[src, t * CAP : (t + 1) * CAP] * (1.0 / SCALE)
                 rest = parts[src, FULL * CAP :] * (1.0 / SCALE)
@@ -512,7 +512,9 @@
     summed = jnp.sum(parts.astype(F32), axis=0).astype(jnp.float16)
     ring = NR // 2
     hops = [lax.ppermute(summed, "y", [(i, (i + k) % ring) for i in range(ring)]) for k in range(1, ring)]
-    received = lax.all_gather(jnp.concatenate([summed, *hops], axis=0), "c", tiled=True)
+    own = [summed, *hops]
+    others = [lax.ppermute(piece, "c", [(0, 1), (1, 0)]) for piece in own]
+    received = jnp.concatenate(own + others, axis=0)
     return unpack(received.astype(F32))
 
 

time: 113 us -> 111 us (0.982)
  starting transfers between devices: 19.7 us -> 27.4 us
  blocking collectives: 30.1 us -> 24.5 us
  waiting for transfers between devices: 22.8 us -> 19.5 us
    ppermute x0 -> x4, starting transfers between devices: none -> 6.47 us  [local(): others = [lax.ppermute(piece, 'c', [(0, 1), (1, 0)]) for piece in own]]
    all_gather x1 -> x0, blocking collectives: 5.68 us -> none  [local(): lax.all_gather(jnp.concatenate([summed, *hops], axis=0), 'c', tiled=True)]
    ppermute x3, waiting for transfers between devices: 4.13 us -> 0.01 us  [local(): lax.ppermute(summed, 'y', [(i, (i + k) % ring) for i in range(ring)])]
    ppermute x3, starting transfers between devices: 1.54 us -> 2.75 us  [local(): lax.ppermute(summed, 'y', [(i, (i + k) % ring) for i in range(ring)])]
  transfers between devices with their start and end apart: 6 -> 10, of which waited for: 5 -> 4; matrix products, arithmetic and copies ran while one was open for 0% -> 0% of each run, Pallas kernels for 26% -> 27%
where the time goes in v7:
time: 111 us
  Pallas kernels  38.9 us (35%)
  starting transfers between devices  27.4 us (25%)
  blocking collectives  24.5 us (22%)
  waiting for transfers between devices  19.5 us (18%)
    pallas_call x1, Pallas kernels, decode(): pl.pallas_call(decode_kernel, in_specs=[VMEM] * 5, out_specs=[VMEM] * 2,...  28.7 us
    all_to_all x1, blocking collectives, local(): exchange(packed.astype(jnp.float16), ('z', 'x'))  24.5 us
    all_to_all x1, waiting for transfers between devices, local(): g = exchange(pack(images), ('x', 'y', 'c'))  16.4 us
    all_to_all x1, starting transfers between devices, local(): g = exchange(pack(images), ('x', 'y', 'c'))  8.73 us
    ppermute x4, starting transfers between devices, local(): others = [lax.ppermute(piece, 'c', [(0, 1), (1, 0)]) for piece in own]  6.47 us
    ppermute x1, starting transfers between devices, local(): following = lax.ppermute(upper, 'z', [((i + 1) % NZ, i) for i in range(NZ)])  5.75 us
    pallas_call x1, Pallas kernels, border(): pl.pallas_call(border_kernel, in_specs=[VMEM] * 7, out_specs=VMEM, out_sh...  4.67 us
    ppermute x1, starting transfers between devices, local(): marks = lax.ppermute(marks, ('z', 'x', 'y', 'c'), swap)  3.67 us
  transfers between devices with their start and end apart: 10, of which 4 were waited for; matrix products, arithmetic and copies ran while one was open for 0% of the time, Pallas kernels for 27%

profile of v7, /device:TPU:1, one launch (start us, length us, event | category | flops | bytes accessed | tf_op | source)
XLA Modules:
  0.0 111.2 jit_solution(14094506880714130518)
XLA Ops:
  0.0 3.4 %pack_pieces.1 = bf16[32,25,8,128]{3,2,1,0:T(8,128)(2,1)} custom-call(bf16[6,2,8,8192]{3,2,1,0:T(8,128)(2,1)} %img.1), custom_call_target="tpu_custom_call" | custom-call | flops 2000000000 | bytes 6000000 | tf_op jit(solution)/shard_map/pack_pieces/pallas_call | solution.py:96
  3.4 0.0 copy-start
  3.4 0.0 copy-start.1
  3.5 0.0 copy-start.2
  3.5 0.0 copy-start.3
  3.5 8.7 %all-to-all-start = ((bf16[32,25,8,128]{3,2,1,0:T(8,128)(2,1)}), bf16[32,25,8,128]{3,2,1,0:T(8,128)(2,1)S(1)}, u32[]{:S(2)}, u32[]{:S(2)}) async-start(bf16[32,25,8,128]{3,2,1,0:T(8,128)(2,1)} %pack_pieces.1), calls=%async_computation | async-start | bytes 3276800 | tf_op jit(solution)/shard_map/all_to_all | solution.py:503
  12.3 0.9 prepare.1
  13.2 3.7 %collective-permute-start = (s32[72,256]{1,0:T(8,128)S(1)}, s32[72,256]{1,0:T(8,128)S(1)}, u32[]{:S(2)}, u32[]{:S(2)}) collective-permute-start(s32[72,256]{1,0:T(8,128)S(1)} %get-tuple-element.11), channel_id=1, source_target_pairs={{0,0},{1,32},{2,64},{3,96},{4,128},{5,160},{6,192},{7,224},{8,8},{... | collective-permute-start | bytes 221192 | tf_op jit(solution)/shard_map/ppermute | solution.py:505
  16.9 2.3 %collective-permute-done.marks = s32[72,256]{1,0:T(8,128)S(1)} collective-permute-done((s32[72,256]{1,0:T(8,128)S(1)}, s32[72,256]{1,0:T(8,128)S(1)}, u32[]{:S(2)}, u32[]{:S(2)}) %collective-permute-start) | collective-permute-done | bytes 73760 | tf_op jit(solution)/shard_map/ppermute | solution.py:505
  19.2 16.4 %all-to-all-done.g = bf16[32,25,8,128]{3,2,1,0:T(8,128)(2,1)S(1)} async-done(((bf16[32,25,8,128]{3,2,1,0:T(8,128)(2,1)}), bf16[32,25,8,128]{3,2,1,0:T(8,128)(2,1)S(1)}, u32[]{:S(2)}, u32[]{:S(2)}) %all-to-all-start) | async-done | bytes 1638432 | tf_op jit(solution)/shard_map/all_to_all | solution.py:503
  35.6 0.1 slice.14
  35.7 0.1 pad_maximum_fusion
  35.8 5.7 %collective-permute-start.1 = (bf16[202,4,128]{2,1,0:T(4,128)(2,1)S(1)}, bf16[202,4,128]{2,1,0:T(4,128)(2,1)S(1)}, u32[]{:S(2)}, u32[]{:S(2)}) collective-permute-start(bf16[202,4,128]{2,1,0:T(4,128)(2,1)S(1)} %pad_maximum_fusion), channel_id=1, source_target_pairs={{32,0},{64,32},{96,64},{128,96},{160,128},{192,160},{224,192},{0,2... | collective-permute-start | bytes 620552 | tf_op jit(solution)/shard_map/ppermute | solution.py:508
  41.6 28.7 %decode_band.1 = (f32[552,256]{1,0:T(8,128)S(1)}, bf16[2,384,256]{2,1,0:T(8,128)(2,1)S(1)}) custom-call(bf16[32,25,8,128]{3,2,1,0:T(8,128)(2,1)S(1)} %all-to-all-done.g, bf16[2,256,256]{2,1,0:T(8,128)(2,1)S(1)} %get-tuple-element.10.bands, s32[72,256]{1,0:T(8,128)S(1)} %collective-permute-done.marks, bf16[552,160]{1,0:T(8,128)(2,1)S(1)} %get-tuple-element.12.cbt, ...), custom_call_target="tpu_custom_call" | custom-call | flops 15000000512 | bytes 45000000 | tf_op jit(solution)/shard_map/decode_band/pallas_call | solution.py:335
  70.3 0.0 collective-permute-done.1.following
  70.3 4.7 %border_rows.1 = f32[32,72,128]{2,1,0:T(8,128)S(1)} custom-call(bf16[2,384,256]{2,1,0:T(8,128)(2,1)S(1)} %get-tuple-element.13.last, bf16[2,256,256]{2,1,0:T(8,128)(2,1)S(1)} %get-tuple-element.10.bands, bf16[202,4,128]{2,1,0:T(4,128)(2,1)S(1)} %collective-permute-done.1.following, s32[72,256]{1,0:T(8,128)S(1)} %collective-permute-done.marks, ...), custom_call_target="tpu_custom_call" | custom-call | flops 4000000000 | bytes 12000000 | tf_op jit(solution)/shard_map/border_rows/pallas_call | solution.py:451
  75.0 0.1 convert_element_type.24
  75.0 24.5 %all_to_all.10 = f16[32,72,128]{2,1,0:T(8,128)(2,1)S(1)} all-to-all(f16[32,72,128]{2,1,0:T(8,128)(2,1)S(1)} %convert_element_type.24), channel_id=1, replica_groups=mesh['z'=8,'x'=4,'y'=4,'c'=2] {'z','x'}, dimensions={0} | all-to-all | bytes 1179648 | tf_op jit(solution)/shard_map/all_to_all | solution.py:511
  99.5 0.1 convert_reduce_fusion
  99.7 0.1 collective-permute-start.2
  99.7 0.3 collective-permute-start.3
  100.0 2.4 %collective-permute-start.4 = (f16[4,72,128]{2,1,0:T(8,128)(2,1)S(1)}, f16[4,72,128]{2,1,0:T(8,128)(2,1)S(1)}, u32[]{:S(2)}, u32[]{:S(2)}) collective-permute-start(f16[4,72,128]{2,1,0:T(8,128)(2,1)S(1)} %get-tuple-element.16), channel_id=1, source_target_pairs={{0,6},{2,0},{4,2},{6,4},{1,7},{3,1},{5,3},{7,5},{8,14},{10,8},{12,... | collective-permute-start | bytes 221192 | tf_op jit(solution)/shard_map/ppermute | solution.py:514
  102.4 2.6 %collective-permute-start.5 = (f16[4,72,128]{2,1,0:T(8,128)(2,1)S(1)}, f16[4,72,128]{2,1,0:T(8,128)(2,1)S(1)}, u32[]{:S(2)}, u32[]{:S(2)}) collective-permute-start(f16[4,72,128]{2,1,0:T(8,128)(2,1)S(1)} %get-tuple-element.16), channel_id=1, source_target_pairs={{0,1},{1,0},{2,3},{3,2},{4,5},{5,4},{6,7},{7,6},{8,9},{9,8},{10,11... | collective-permute-start | bytes 221192 | tf_op jit(solution)/shard_map/ppermute | solution.py:516
  105.0 0.0 collective-permute-done.2
  105.0 3.1 %collective-permute-start.6 = (f16[4,72,128]{2,1,0:T(8,128)(2,1)S(1)}, f16[4,72,128]{2,1,0:T(8,128)(2,1)S(1)}, u32[]{:S(2)}, u32[]{:S(2)}) collective-permute-start(f16[4,72,128]{2,1,0:T(8,128)(2,1)S(1)} %collective-permute-done.2), channel_id=1, source_target_pairs={{0,1},{1,0},{2,3},{3,2},{4,5},{5,4},{6,7},{7,6},{8,9},{9,8},{10,11... | collective-permute-start | bytes 221192 | tf_op jit(solution)/shard_map/ppermute | solution.py:516
  108.2 0.1 collective-permute-start.7
  108.3 0.7 collective-permute-start.8
  109.0 0.0 collective-permute-done.5
  109.1 0.4 collective-permute-done.7
  109.5 0.3 collective-permute-done.8
  109.9 0.1 convert_element_type.28.parts
  110.0 1.2 %unpack_cells.1 = f32[1,32,16,550]{3,2,1,0:T(8,128)} custom-call(f32[32,72,128]{2,1,0:T(8,128)S(1)} %convert_element_type.28.parts), custom_call_target="tpu_custom_call" | custom-call | tf_op jit(solution)/shard_map/unpack_cells/pallas_call | solution.py:485
  (19 shorter events, 0.3 us)
Async XLA Ops:
  3.4 8.8 %copy-start = (s32[2,32,256]{2,1,0:T(8,128)S(1)}, s32[2,32,256]{2,1,0:T(8,128)}, u32[]{:S(2)}) copy-start(s32[2,32,256]{2,1,0:T(8,128)} %labels.1) | copy-start | bytes 196612
  3.4 8.8 %copy-start.1 = (bf16[48,550]{1,0:T(8,128)(2,1)S(1)}, bf16[48,550]{1,0:T(8,128)(2,1)}, u32[]{:S(2)}) copy-start(bf16[48,550]{1,0:T(8,128)(2,1)} %codebook.5) | copy-start | bytes 158404
  3.5 8.8 %copy-start.2 = (s32[256,1]{0,1:T(1,128)S(1)}, s32[256,1]{0,1:T(1,128)}, u32[]{:S(2)}) copy-start(s32[256,1]{0,1:T(1,128)} %param.8) | copy-start | bytes 3076
  3.5 8.8 %copy-start.3 = (s32[32]{0:T(128)S(1)}, s32[32]{0:T(128)}, u32[]{:S(2)}) copy-start(s32[32]{0:T(128)} %counts.1) | copy-start | bytes 388
  3.5 32.1 %all-to-all-start = ((bf16[32,25,8,128]{3,2,1,0:T(8,128)(2,1)}), bf16[32,25,8,128]{3,2,1,0:T(8,128)(2,1)S(1)}, u32[]{:S(2)}, u32[]{:S(2)}) async-start(bf16[32,25,8,128]{3,2,1,0:T(8,128)(2,1)} %pack_pieces.1), calls=%async_computation | async-start | bytes 3276800 | tf_op jit(solution)/shard_map/all_to_all | solution.py:503
  13.2 6.0 %collective-permute-start = (s32[72,256]{1,0:T(8,128)S(1)}, s32[72,256]{1,0:T(8,128)S(1)}, u32[]{:S(2)}, u32[]{:S(2)}) collective-permute-start(s32[72,256]{1,0:T(8,128)S(1)} %get-tuple-element.11), channel_id=1, source_target_pairs={{0,0},{1,32},{2,64},{3,96},{4,128},{5,160},{6,192},{7,224},{8,8},{... | collective-permute-start | bytes 221192 | tf_op jit(solution)/shard_map/ppermute | solution.py:505
  35.8 34.5 %collective-permute-start.1 = (bf16[202,4,128]{2,1,0:T(4,128)(2,1)S(1)}, bf16[202,4,128]{2,1,0:T(4,128)(2,1)S(1)}, u32[]{:S(2)}, u32[]{:S(2)}) collective-permute-start(bf16[202,4,128]{2,1,0:T(4,128)(2,1)S(1)} %pad_maximum_fusion), channel_id=1, source_target_pairs={{32,0},{64,32},{96,64},{128,96},{160,128},{192,160},{224,192},{0,2... | collective-permute-start | bytes 620552 | tf_op jit(solution)/shard_map/ppermute | solution.py:508
  99.7 5.4 %collective-permute-start.2 = (f16[4,72,128]{2,1,0:T(8,128)(2,1)S(1)}, f16[4,72,128]{2,1,0:T(8,128)(2,1)S(1)}, u32[]{:S(2)}, u32[]{:S(2)}) collective-permute-start(f16[4,72,128]{2,1,0:T(8,128)(2,1)S(1)} %get-tuple-element.16), channel_id=1, source_target_pairs={{0,2},{2,4},{4,6},{6,0},{1,3},{3,5},{5,7},{7,1},{8,10},{10,12},{12... | collective-permute-start | bytes 221192 | tf_op jit(solution)/shard_map/ppermute | solution.py:514
  99.7 8.4 %collective-permute-start.3 = (f16[4,72,128]{2,1,0:T(8,128)(2,1)S(1)}, f16[4,72,128]{2,1,0:T(8,128)(2,1)S(1)}, u32[]{:S(2)}, u32[]{:S(2)}) collective-permute-start(f16[4,72,128]{2,1,0:T(8,128)(2,1)S(1)} %get-tuple-element.16), channel_id=1, source_target_pairs={{0,4},{2,6},{4,0},{6,2},{1,5},{3,7},{5,1},{7,3},{8,12},{10,14},{12... | collective-permute-start | bytes 221192 | tf_op jit(solution)/shard_map/ppermute | solution.py:514
  100.0 8.3 %collective-permute-start.4 = (f16[4,72,128]{2,1,0:T(8,128)(2,1)S(1)}, f16[4,72,128]{2,1,0:T(8,128)(2,1)S(1)}, u32[]{:S(2)}, u32[]{:S(2)}) collective-permute-start(f16[4,72,128]{2,1,0:T(8,128)(2,1)S(1)} %get-tuple-element.16), channel_id=1, source_target_pairs={{0,6},{2,0},{4,2},{6,4},{1,7},{3,1},{5,3},{7,5},{8,14},{10,8},{12,... | collective-permute-start | bytes 221192 | tf_op jit(solution)/shard_map/ppermute | solution.py:514
  102.4 6.6 %collective-permute-start.5 = (f16[4,72,128]{2,1,0:T(8,128)(2,1)S(1)}, f16[4,72,128]{2,1,0:T(8,128)(2,1)S(1)}, u32[]{:S(2)}, u32[]{:S(2)}) collective-permute-start(f16[4,72,128]{2,1,0:T(8,128)(2,1)S(1)} %get-tuple-element.16), channel_id=1, source_target_pairs={{0,1},{1,0},{2,3},{3,2},{4,5},{5,4},{6,7},{7,6},{8,9},{9,8},{10,11... | collective-permute-start | bytes 221192 | tf_op jit(solution)/shard_map/ppermute | solution.py:516
  105.0 4.0 %collective-permute-start.6 = (f16[4,72,128]{2,1,0:T(8,128)(2,1)S(1)}, f16[4,72,128]{2,1,0:T(8,128)(2,1)S(1)}, u32[]{:S(2)}, u32[]{:S(2)}) collective-permute-start(f16[4,72,128]{2,1,0:T(8,128)(2,1)S(1)} %collective-permute-done.2), channel_id=1, source_target_pairs={{0,1},{1,0},{2,3},{3,2},{4,5},{5,4},{6,7},{7,6},{8,9},{9,8},{10,11... | collective-permute-start | bytes 221192 | tf_op jit(solution)/shard_map/ppermute | solution.py:516
  108.2 1.4 %collective-permute-start.7 = (f16[4,72,128]{2,1,0:T(8,128)(2,1)S(1)}, f16[4,72,128]{2,1,0:T(8,128)(2,1)S(1)}, u32[]{:S(2)}, u32[]{:S(2)}) collective-permute-start(f16[4,72,128]{2,1,0:T(8,128)(2,1)S(1)} %collective-permute-done.3), channel_id=1, source_target_pairs={{0,1},{1,0},{2,3},{3,2},{4,5},{5,4},{6,7},{7,6},{8,9},{9,8},{10,11... | collective-permute-start | bytes 221192 | tf_op jit(solution)/shard_map/ppermute | solution.py:516
  108.3 1.6 %collective-permute-start.8 = (f16[4,72,128]{2,1,0:T(8,128)(2,1)S(1)}, f16[4,72,128]{2,1,0:T(8,128)(2,1)S(1)}, u32[]{:S(2)}, u32[]{:S(2)}) collective-permute-start(f16[4,72,128]{2,1,0:T(8,128)(2,1)S(1)} %collective-permute-done.4), channel_id=1, source_target_pairs={{0,1},{1,0},{2,3},{3,2},{4,5},{5,4},{6,7},{7,6},{8,9},{9,8},{10,11... | collective-permute-start | bytes 221192 | tf_op jit(solution)/shard_map/ppermute | solution.py:516

commit v8 on v7

--- a/solution.py
+++ b/solution.py
@@ -511,7 +511,9 @@
     parts = exchange(packed.astype(jnp.float16), ("z", "x")).reshape(NZ, NXD, OUT_ROWS, 128)
     summed = jnp.sum(parts.astype(F32), axis=0).astype(jnp.float16)
     ring = NR // 2
-    hops = [lax.ppermute(summed, "y", [(i, (i + k) % ring) for i in range(ring)]) for k in range(1, ring)]
+    order = sorted(range(1, ring), key=lambda k: -min(k, ring - k))
+    sent = {k: lax.ppermute(summed, "y", [(i, (i + k) % ring) for i in range(ring)]) for k in order}
+    hops = [sent[k] for k in range(1, ring)]
     own = [summed, *hops]
     others = [lax.ppermute(piece, "c", [(0, 1), (1, 0)]) for piece in own]
     received = jnp.concatenate(own + others, axis=0)

time: 111 us -> 111 us (level)
  no operation moved by 1% of the time
where the time goes in v8:
time: 111 us
  Pallas kernels  38.9 us (35%)
  starting transfers between devices  27.4 us (25%)
  blocking collectives  24.5 us (22%)
  waiting for transfers between devices  19.5 us (18%)
    pallas_call x1, Pallas kernels, decode(): pl.pallas_call(decode_kernel, in_specs=[VMEM] * 5, out_specs=[VMEM] * 2,...  28.7 us
    all_to_all x1, blocking collectives, local(): exchange(packed.astype(jnp.float16), ('z', 'x'))  24.5 us
    all_to_all x1, waiting for transfers between devices, local(): g = exchange(pack(images), ('x', 'y', 'c'))  16.4 us
    all_to_all x1, starting transfers between devices, local(): g = exchange(pack(images), ('x', 'y', 'c'))  8.73 us
    ppermute x4, starting transfers between devices, local(): others = [lax.ppermute(piece, 'c', [(0, 1), (1, 0)]) for piece in own]  6.47 us
    ppermute x1, starting transfers between devices, local(): following = lax.ppermute(upper, 'z', [((i + 1) % NZ, i) for i in range(NZ)])  5.75 us
    pallas_call x1, Pallas kernels, border(): pl.pallas_call(border_kernel, in_specs=[VMEM] * 7, out_specs=VMEM, out_sh...  4.67 us
    ppermute x1, starting transfers between devices, local(): marks = lax.ppermute(marks, ('z', 'x', 'y', 'c'), swap)  3.67 us
  transfers between devices with their start and end apart: 10, of which 4 were waited for; matrix products, arithmetic and copies ran while one was open for 0% of the time, Pallas kernels for 27%

profile of v8, /device:TPU:1, one launch (start us, length us, event | category | flops | bytes accessed | tf_op | source)
XLA Modules:
  0.0 111.2 jit_solution(14094506880714130518)
XLA Ops:
  0.0 3.4 %pack_pieces.1 = bf16[32,25,8,128]{3,2,1,0:T(8,128)(2,1)} custom-call(bf16[6,2,8,8192]{3,2,1,0:T(8,128)(2,1)} %img.1), custom_call_target="tpu_custom_call" | custom-call | flops 2000000000 | bytes 6000000 | tf_op jit(solution)/shard_map/pack_pieces/pallas_call | solution.py:96
  3.4 0.0 copy-start
  3.4 0.0 copy-start.1
  3.5 0.0 copy-start.2
  3.5 0.0 copy-start.3
  3.5 8.7 %all-to-all-start = ((bf16[32,25,8,128]{3,2,1,0:T(8,128)(2,1)}), bf16[32,25,8,128]{3,2,1,0:T(8,128)(2,1)S(1)}, u32[]{:S(2)}, u32[]{:S(2)}) async-start(bf16[32,25,8,128]{3,2,1,0:T(8,128)(2,1)} %pack_pieces.1), calls=%async_computation | async-start | bytes 3276800 | tf_op jit(solution)/shard_map/all_to_all | solution.py:503
  12.3 0.9 prepare.1
  13.2 3.7 %collective-permute-start = (s32[72,256]{1,0:T(8,128)S(1)}, s32[72,256]{1,0:T(8,128)S(1)}, u32[]{:S(2)}, u32[]{:S(2)}) collective-permute-start(s32[72,256]{1,0:T(8,128)S(1)} %get-tuple-element.11), channel_id=1, source_target_pairs={{0,0},{1,32},{2,64},{3,96},{4,128},{5,160},{6,192},{7,224},{8,8},{... | collective-permute-start | bytes 221192 | tf_op jit(solution)/shard_map/ppermute | solution.py:505
  16.9 2.3 %collective-permute-done.marks = s32[72,256]{1,0:T(8,128)S(1)} collective-permute-done((s32[72,256]{1,0:T(8,128)S(1)}, s32[72,256]{1,0:T(8,128)S(1)}, u32[]{:S(2)}, u32[]{:S(2)}) %collective-permute-start) | collective-permute-done | bytes 73760 | tf_op jit(solution)/shard_map/ppermute | solution.py:505
  19.2 16.4 %all-to-all-done.g = bf16[32,25,8,128]{3,2,1,0:T(8,128)(2,1)S(1)} async-done(((bf16[32,25,8,128]{3,2,1,0:T(8,128)(2,1)}), bf16[32,25,8,128]{3,2,1,0:T(8,128)(2,1)S(1)}, u32[]{:S(2)}, u32[]{:S(2)}) %all-to-all-start) | async-done | bytes 1638432 | tf_op jit(solution)/shard_map/all_to_all | solution.py:503
  35.6 0.1 slice.14
  35.7 0.1 pad_maximum_fusion
  35.8 5.7 %collective-permute-start.1 = (bf16[202,4,128]{2,1,0:T(4,128)(2,1)S(1)}, bf16[202,4,128]{2,1,0:T(4,128)(2,1)S(1)}, u32[]{:S(2)}, u32[]{:S(2)}) collective-permute-start(bf16[202,4,128]{2,1,0:T(4,128)(2,1)S(1)} %pad_maximum_fusion), channel_id=1, source_target_pairs={{32,0},{64,32},{96,64},{128,96},{160,128},{192,160},{224,192},{0,2... | collective-permute-start | bytes 620552 | tf_op jit(solution)/shard_map/ppermute | solution.py:508
  41.6 28.7 %decode_band.1 = (f32[552,256]{1,0:T(8,128)S(1)}, bf16[2,384,256]{2,1,0:T(8,128)(2,1)S(1)}) custom-call(bf16[32,25,8,128]{3,2,1,0:T(8,128)(2,1)S(1)} %all-to-all-done.g, bf16[2,256,256]{2,1,0:T(8,128)(2,1)S(1)} %get-tuple-element.10.bands, s32[72,256]{1,0:T(8,128)S(1)} %collective-permute-done.marks, bf16[552,160]{1,0:T(8,128)(2,1)S(1)} %get-tuple-element.12.cbt, ...), custom_call_target="tpu_custom_call" | custom-call | flops 15000000512 | bytes 45000000 | tf_op jit(solution)/shard_map/decode_band/pallas_call | solution.py:335
  70.3 0.0 collective-permute-done.1.following
  70.3 4.7 %border_rows.1 = f32[32,72,128]{2,1,0:T(8,128)S(1)} custom-call(bf16[2,384,256]{2,1,0:T(8,128)(2,1)S(1)} %get-tuple-element.13.last, bf16[2,256,256]{2,1,0:T(8,128)(2,1)S(1)} %get-tuple-element.10.bands, bf16[202,4,128]{2,1,0:T(4,128)(2,1)S(1)} %collective-permute-done.1.following, s32[72,256]{1,0:T(8,128)S(1)} %collective-permute-done.marks, ...), custom_call_target="tpu_custom_call" | custom-call | flops 4000000000 | bytes 12000000 | tf_op jit(solution)/shard_map/border_rows/pallas_call | solution.py:451
  75.0 0.1 convert_element_type.24
  75.0 24.5 %all_to_all.10 = f16[32,72,128]{2,1,0:T(8,128)(2,1)S(1)} all-to-all(f16[32,72,128]{2,1,0:T(8,128)(2,1)S(1)} %convert_element_type.24), channel_id=1, replica_groups=mesh['z'=8,'x'=4,'y'=4,'c'=2] {'z','x'}, dimensions={0} | all-to-all | bytes 1179648 | tf_op jit(solution)/shard_map/all_to_all | solution.py:511
  99.5 0.1 convert_reduce_fusion
  99.7 0.1 collective-permute-start.2
  99.7 0.3 collective-permute-start.3
  100.0 2.4 %collective-permute-start.4 = (f16[4,72,128]{2,1,0:T(8,128)(2,1)S(1)}, f16[4,72,128]{2,1,0:T(8,128)(2,1)S(1)}, u32[]{:S(2)}, u32[]{:S(2)}) collective-permute-start(f16[4,72,128]{2,1,0:T(8,128)(2,1)S(1)} %get-tuple-element.16), channel_id=1, source_target_pairs={{0,6},{2,0},{4,2},{6,4},{1,7},{3,1},{5,3},{7,5},{8,14},{10,8},{12,... | collective-permute-start | bytes 221192 | tf_op jit(solution)/shard_map/ppermute | solution.py:515
  102.4 2.6 %collective-permute-start.5 = (f16[4,72,128]{2,1,0:T(8,128)(2,1)S(1)}, f16[4,72,128]{2,1,0:T(8,128)(2,1)S(1)}, u32[]{:S(2)}, u32[]{:S(2)}) collective-permute-start(f16[4,72,128]{2,1,0:T(8,128)(2,1)S(1)} %get-tuple-element.16), channel_id=1, source_target_pairs={{0,1},{1,0},{2,3},{3,2},{4,5},{5,4},{6,7},{7,6},{8,9},{9,8},{10,11... | collective-permute-start | bytes 221192 | tf_op jit(solution)/shard_map/ppermute | solution.py:518
  105.0 0.0 collective-permute-done.2
  105.0 3.1 %collective-permute-start.6 = (f16[4,72,128]{2,1,0:T(8,128)(2,1)S(1)}, f16[4,72,128]{2,1,0:T(8,128)(2,1)S(1)}, u32[]{:S(2)}, u32[]{:S(2)}) collective-permute-start(f16[4,72,128]{2,1,0:T(8,128)(2,1)S(1)} %collective-permute-done.2), channel_id=1, source_target_pairs={{0,1},{1,0},{2,3},{3,2},{4,5},{5,4},{6,7},{7,6},{8,9},{9,8},{10,11... | collective-permute-start | bytes 221192 | tf_op jit(solution)/shard_map/ppermute | solution.py:518
  108.2 0.1 collective-permute-start.7
  108.3 0.7 collective-permute-start.8
  109.0 0.0 collective-permute-done.5
  109.1 0.4 collective-permute-done.7
  109.5 0.3 collective-permute-done.8
  109.9 0.1 convert_element_type.28.parts
  110.0 1.2 %unpack_cells.1 = f32[1,32,16,550]{3,2,1,0:T(8,128)} custom-call(f32[32,72,128]{2,1,0:T(8,128)S(1)} %convert_element_type.28.parts), custom_call_target="tpu_custom_call" | custom-call | tf_op jit(solution)/shard_map/unpack_cells/pallas_call | solution.py:485
  (19 shorter events, 0.3 us)
Async XLA Ops:
  3.4 8.8 %copy-start = (s32[2,32,256]{2,1,0:T(8,128)S(1)}, s32[2,32,256]{2,1,0:T(8,128)}, u32[]{:S(2)}) copy-start(s32[2,32,256]{2,1,0:T(8,128)} %labels.1) | copy-start | bytes 196612
  3.4 8.8 %copy-start.1 = (bf16[48,550]{1,0:T(8,128)(2,1)S(1)}, bf16[48,550]{1,0:T(8,128)(2,1)}, u32[]{:S(2)}) copy-start(bf16[48,550]{1,0:T(8,128)(2,1)} %codebook.5) | copy-start | bytes 158404
  3.5 8.8 %copy-start.2 = (s32[256,1]{0,1:T(1,128)S(1)}, s32[256,1]{0,1:T(1,128)}, u32[]{:S(2)}) copy-start(s32[256,1]{0,1:T(1,128)} %param.8) | copy-start | bytes 3076
  3.5 8.8 %copy-start.3 = (s32[32]{0:T(128)S(1)}, s32[32]{0:T(128)}, u32[]{:S(2)}) copy-start(s32[32]{0:T(128)} %counts.1) | copy-start | bytes 388
  3.5 32.1 %all-to-all-start = ((bf16[32,25,8,128]{3,2,1,0:T(8,128)(2,1)}), bf16[32,25,8,128]{3,2,1,0:T(8,128)(2,1)S(1)}, u32[]{:S(2)}, u32[]{:S(2)}) async-start(bf16[32,25,8,128]{3,2,1,0:T(8,128)(2,1)} %pack_pieces.1), calls=%async_computation | async-start | bytes 3276800 | tf_op jit(solution)/shard_map/all_to_all | solution.py:503
  13.2 6.0 %collective-permute-start = (s32[72,256]{1,0:T(8,128)S(1)}, s32[72,256]{1,0:T(8,128)S(1)}, u32[]{:S(2)}, u32[]{:S(2)}) collective-permute-start(s32[72,256]{1,0:T(8,128)S(1)} %get-tuple-element.11), channel_id=1, source_target_pairs={{0,0},{1,32},{2,64},{3,96},{4,128},{5,160},{6,192},{7,224},{8,8},{... | collective-permute-start | bytes 221192 | tf_op jit(solution)/shard_map/ppermute | solution.py:505
  35.8 34.5 %collective-permute-start.1 = (bf16[202,4,128]{2,1,0:T(4,128)(2,1)S(1)}, bf16[202,4,128]{2,1,0:T(4,128)(2,1)S(1)}, u32[]{:S(2)}, u32[]{:S(2)}) collective-permute-start(bf16[202,4,128]{2,1,0:T(4,128)(2,1)S(1)} %pad_maximum_fusion), channel_id=1, source_target_pairs={{32,0},{64,32},{96,64},{128,96},{160,128},{192,160},{224,192},{0,2... | collective-permute-start | bytes 620552 | tf_op jit(solution)/shard_map/ppermute | solution.py:508
  99.7 5.4 %collective-permute-start.2 = (f16[4,72,128]{2,1,0:T(8,128)(2,1)S(1)}, f16[4,72,128]{2,1,0:T(8,128)(2,1)S(1)}, u32[]{:S(2)}, u32[]{:S(2)}) collective-permute-start(f16[4,72,128]{2,1,0:T(8,128)(2,1)S(1)} %get-tuple-element.16), channel_id=1, source_target_pairs={{0,2},{2,4},{4,6},{6,0},{1,3},{3,5},{5,7},{7,1},{8,10},{10,12},{12... | collective-permute-start | bytes 221192 | tf_op jit(solution)/shard_map/ppermute | solution.py:515
  99.7 8.4 %collective-permute-start.3 = (f16[4,72,128]{2,1,0:T(8,128)(2,1)S(1)}, f16[4,72,128]{2,1,0:T(8,128)(2,1)S(1)}, u32[]{:S(2)}, u32[]{:S(2)}) collective-permute-start(f16[4,72,128]{2,1,0:T(8,128)(2,1)S(1)} %get-tuple-element.16), channel_id=1, source_target_pairs={{0,4},{2,6},{4,0},{6,2},{1,5},{3,7},{5,1},{7,3},{8,12},{10,14},{12... | collective-permute-start | bytes 221192 | tf_op jit(solution)/shard_map/ppermute | solution.py:515
  100.0 8.3 %collective-permute-start.4 = (f16[4,72,128]{2,1,0:T(8,128)(2,1)S(1)}, f16[4,72,128]{2,1,0:T(8,128)(2,1)S(1)}, u32[]{:S(2)}, u32[]{:S(2)}) collective-permute-start(f16[4,72,128]{2,1,0:T(8,128)(2,1)S(1)} %get-tuple-element.16), channel_id=1, source_target_pairs={{0,6},{2,0},{4,2},{6,4},{1,7},{3,1},{5,3},{7,5},{8,14},{10,8},{12,... | collective-permute-start | bytes 221192 | tf_op jit(solution)/shard_map/ppermute | solution.py:515
  102.4 6.6 %collective-permute-start.5 = (f16[4,72,128]{2,1,0:T(8,128)(2,1)S(1)}, f16[4,72,128]{2,1,0:T(8,128)(2,1)S(1)}, u32[]{:S(2)}, u32[]{:S(2)}) collective-permute-start(f16[4,72,128]{2,1,0:T(8,128)(2,1)S(1)} %get-tuple-element.16), channel_id=1, source_target_pairs={{0,1},{1,0},{2,3},{3,2},{4,5},{5,4},{6,7},{7,6},{8,9},{9,8},{10,11... | collective-permute-start | bytes 221192 | tf_op jit(solution)/shard_map/ppermute | solution.py:518
  105.0 4.0 %collective-permute-start.6 = (f16[4,72,128]{2,1,0:T(8,128)(2,1)S(1)}, f16[4,72,128]{2,1,0:T(8,128)(2,1)S(1)}, u32[]{:S(2)}, u32[]{:S(2)}) collective-permute-start(f16[4,72,128]{2,1,0:T(8,128)(2,1)S(1)} %collective-permute-done.2), channel_id=1, source_target_pairs={{0,1},{1,0},{2,3},{3,2},{4,5},{5,4},{6,7},{7,6},{8,9},{9,8},{10,11... | collective-permute-start | bytes 221192 | tf_op jit(solution)/shard_map/ppermute | solution.py:518
  108.2 1.4 %collective-permute-start.7 = (f16[4,72,128]{2,1,0:T(8,128)(2,1)S(1)}, f16[4,72,128]{2,1,0:T(8,128)(2,1)S(1)}, u32[]{:S(2)}, u32[]{:S(2)}) collective-permute-start(f16[4,72,128]{2,1,0:T(8,128)(2,1)S(1)} %collective-permute-done.3), channel_id=1, source_target_pairs={{0,1},{1,0},{2,3},{3,2},{4,5},{5,4},{6,7},{7,6},{8,9},{9,8},{10,11... | collective-permute-start | bytes 221192 | tf_op jit(solution)/shard_map/ppermute | solution.py:518
  108.3 1.6 %collective-permute-start.8 = (f16[4,72,128]{2,1,0:T(8,128)(2,1)S(1)}, f16[4,72,128]{2,1,0:T(8,128)(2,1)S(1)}, u32[]{:S(2)}, u32[]{:S(2)}) collective-permute-start(f16[4,72,128]{2,1,0:T(8,128)(2,1)S(1)} %collective-permute-done.4), channel_id=1, source_target_pairs={{0,1},{1,0},{2,3},{3,2},{4,5},{5,4},{6,7},{7,6},{8,9},{9,8},{10,11... | collective-permute-start | bytes 221192 | tf_op jit(solution)/shard_map/ppermute | solution.py:518
